TPU v7x, 32 devices: a whole 2x2x4 slice. The times are simulated.
32 devices in a mesh: dp: 4 (over y, x), seq: 8 (over z, core).
Axes of the slice: x: 2, y: 2, z: 4, core: 2. Of those that a mesh axis runs over, the one named last changes fastest.
Arguments:
- tokens: bfloat16 [16, 1024, 768], P('dp', 'seq'), may hold values from -6 to 6
- cotangent: bfloat16 [16, 1024, 768], P('dp', 'seq'), may hold values from -6 to 6
- document_starts: int32 [16, 8], P('dp'), may hold values from 0 to 1023, as said below
- vectors: float32 [2, 11, 768], P(None, None, ('dp', 'seq')), may hold values from -17 to 2
- matrices: float32 [2, 4, 768, 768], P(None, None, ('dp', 'seq')), may hold values from -0.21875 to 0.21875
- time_output: float32 [2, 768, 768], P(None, ('dp', 'seq')), may hold values from -0.875 to 0.875
- feed_key: float32 [2, 768, 3072], P(None, ('dp', 'seq')), may hold values from -0.21875 to 0.21875
- feed_value: float32 [2, 3072, 768], P(None, ('dp', 'seq')), may hold values from -0.109375 to 0.109375
- mean_vectors: float32 [2, 11, 768], P(None, None, ('dp', 'seq')), may hold values from -128 to 128
- mean_matrices: float32 [2, 4, 768, 768], P(None, None, ('dp', 'seq')), may hold values from -128 to 128
- mean_output: float32 [2, 768, 768], P(None, ('dp', 'seq')), may hold values from -128 to 128
- mean_key: float32 [2, 768, 3072], P(None, ('dp', 'seq')), may hold values from -128 to 128
- mean_value: float32 [2, 3072, 768], P(None, ('dp', 'seq')), may hold values from -128 to 128
- power_vectors: float32 [2, 11, 768], P(None, None, ('dp', 'seq')), may hold values from 0 to 1638
- power_matrices: float32 [2, 4, 768, 768], P(None, None, ('dp', 'seq')), may hold values from 0 to 327
- power_output: float32 [2, 768, 768], P(None, ('dp', 'seq')), may hold values from 0 to 327
- power_key: float32 [2, 768, 3072], P(None, ('dp', 'seq')), may hold values from 0 to 327
- power_value: float32 [2, 3072, 768], P(None, ('dp', 'seq')), may hold values from 0 to 327
Outputs:
- block_out: bfloat16 [16, 1024, 768], P('dp', 'seq')
- grad_tokens: float32 [16, 1024, 768], P('dp', 'seq')
- grad_vectors: float32 [2, 11, 768], P(None, None, ('dp', 'seq'))
- grad_matrices: float32 [2, 4, 768, 768], P(None, None, ('dp', 'seq'))
- grad_output: float32 [2, 768, 768], P(None, ('dp', 'seq'))
- grad_key: float32 [2, 768, 3072], P(None, ('dp', 'seq'))
- grad_value: float32 [2, 3072, 768], P(None, ('dp', 'seq'))
- step_vectors: float32 [2, 11, 768], P(None, None, ('dp', 'seq'))
- step_matrices: float32 [2, 4, 768, 768], P(None, None, ('dp', 'seq'))
- step_output: float32 [2, 768, 768], P(None, ('dp', 'seq'))
- step_key: float32 [2, 768, 3072], P(None, ('dp', 'seq'))
- step_value: float32 [2, 3072, 768], P(None, ('dp', 'seq'))
- new_mean_vectors: float32 [2, 11, 768], P(None, None, ('dp', 'seq'))
- new_mean_matrices: float32 [2, 4, 768, 768], P(None, None, ('dp', 'seq'))
- new_mean_output: float32 [2, 768, 768], P(None, ('dp', 'seq'))
- new_mean_key: float32 [2, 768, 3072], P(None, ('dp', 'seq'))
- new_mean_value: float32 [2, 3072, 768], P(None, ('dp', 'seq'))
- new_power_vectors: float32 [2, 11, 768], P(None, None, ('dp', 'seq'))
- new_power_matrices: float32 [2, 4, 768, 768], P(None, None, ('dp', 'seq'))
- new_power_output: float32 [2, 768, 768], P(None, ('dp', 'seq'))
- new_power_key: float32 [2, 768, 3072], P(None, ('dp', 'seq'))
- new_power_value: float32 [2, 3072, 768], P(None, ('dp', 'seq'))
Inputs may be any that keep to these rules, and one draw needn't show every extreme that they name: `document_starts`: each row's starts are strictly increasing and the first is 0. In each group of 4 rows on one index of dp, one row drawn from the seed has a document that begins within the first 128 positions and ends within the last 128, and that row's last document is its final position alone.
All inputs are finite; a program needn't handle non-finite values.
Results may differ from a plain program's by a relative error of at most 0.033.
Values may be sent and summed in bfloat16 or wider, within the bound.
No kernel may reach another device: no remote copies, remote signals or barrier semaphores. Data moves between devices by JAX's collectives and lax.ppermute only.
A program may use at most 256 MiB of HBM per device.

v0:
```python
from functools import partial

import jax
import jax.numpy as jnp
from jax import lax
from jax.sharding import PartitionSpec as P

WBLK = 8


norm_epsilon = 1e-05
beta_one = 0.9
beta_two = 0.99
adam_epsilon = 1e-08
step_count = 10
rate_main = 0.0006
rate_time = 0.0012
weight_decay = 0.1


def prefix(array, axis, combine, identity):
    length, index = (lax.axis_size(axis), lax.axis_index(axis))
    everything = jax.tree.map(
        lambda part, kind: lax.all_gather(part.astype(kind), axis),
        array,
        (jnp.bfloat16, jnp.bfloat16, jnp.bfloat16),
    )
    start = jax.tree.map(
        lambda part, zero: jnp.broadcast_to(jnp.asarray(zero, part.dtype), part.shape),
        array,
        identity,
    )

    def step(k, before):
        reached = k < index
        new = combine(
            before, jax.tree.map(lambda part, own: part[k].astype(own.dtype), everything, array)
        )
        return jax.tree.map(lambda a, b: jnp.where(reached, a, b), new, before)

    return lax.fori_loop(0, length, step, start)


def prefix_2(array, axis, combine, identity):
    length, index = (lax.axis_size(axis), lax.axis_index(axis))
    everything = jax.tree.map(
        lambda part, kind: lax.all_gather(part.astype(kind), axis),
        array,
        jax.tree.map(lambda a: jnp.bfloat16 if a.dtype == jnp.float32 else a.dtype, array),
    )
    start = jax.tree.map(
        lambda part, zero: jnp.broadcast_to(jnp.asarray(zero, part.dtype), part.shape),
        array,
        identity,
    )

    def step(k, before):
        at = length - 1 - k
        reached = at > index
        new = combine(
            before, jax.tree.map(lambda part, own: part[at].astype(own.dtype), everything, array)
        )
        return jax.tree.map(lambda a, b: jnp.where(reached, a, b), new, before)

    return lax.fori_loop(0, length, step, start)


def from_behind(block, axis, distance):
    devices = range(lax.axis_size(axis))
    route = [(i - distance, i) for i in devices if i - distance in devices]
    return lax.ppermute(block, axis, route)


def layer_norm(values_in, gain, bias):
    centre = jnp.mean(values_in, axis=-1, keepdims=True)
    centred = values_in - centre
    spread = jnp.mean(centred * centred, axis=-1, keepdims=True)
    return centred * lax.rsqrt(spread + norm_epsilon) * gain + bias


def decay_block(carry_state, block_item, decay_rate):
    running_state_numerator, running_state_denominator, state_document = carry_state
    lookup_projection_lines, value_matrix_rows, document_index = block_item
    block_length = lookup_projection_lines.shape[1]
    offsets = jnp.arange(block_length)
    lag_steps = offsets[:, None] - offsets[None, :] - 1
    earlier = lag_steps >= 0
    lag_decay = jnp.exp(-jnp.maximum(lag_steps, 0).astype(jnp.float32)[:, :, None] * decay_rate)
    same_document = (document_index[:, :, None] == document_index[:, None, :]) & earlier[None]
    coefficient = jnp.where(same_document[..., None], lag_decay[None], 0.0)
    exp_keys = jnp.exp(lookup_projection_lines)
    weighted = exp_keys * value_matrix_rows
    numerator = jnp.sum(coefficient * weighted[:, None], axis=2)
    denominator = jnp.sum(coefficient * exp_keys[:, None], axis=2)
    recurrent_memory = (document_index == state_document[:, None]).astype(jnp.float32)[
        :, :, None
    ] * jnp.exp(-offsets.astype(jnp.float32)[:, None] * decay_rate)[None]
    numerator = numerator + recurrent_memory * running_state_numerator[:, None]
    denominator = denominator + recurrent_memory * running_state_denominator[:, None]
    last_document = document_index[:, -1]
    tail_weight = (document_index == last_document[:, None]).astype(jnp.float32)[
        :, :, None
    ] * jnp.exp(-(block_length - 1 - offsets).astype(jnp.float32)[:, None] * decay_rate)[None]
    keep_factor = (state_document == last_document).astype(jnp.float32)[:, None] * jnp.exp(
        -block_length * decay_rate
    )[None]
    new_numerator = keep_factor * running_state_numerator + jnp.sum(tail_weight * weighted, axis=1)
    new_denominator = keep_factor * running_state_denominator + jnp.sum(
        tail_weight * exp_keys, axis=1
    )
    return ((new_numerator, new_denominator, last_document), (numerator, denominator))


def decay_sums(
    lookup_projection_lines,
    value_matrix_rows,
    document_index,
    decay_rate,
    document_start_flag,
    running_state_numerator,
    running_state_denominator,
):
    row_count, token_count, model_width = lookup_projection_lines.shape
    block_count = token_count // WBLK

    def to_blocks(array):
        return jnp.swapaxes(array.reshape((row_count, block_count, WBLK) + array.shape[2:]), 0, 1)

    def from_blocks(array):
        return jnp.swapaxes(array, 0, 1).reshape(row_count, token_count, model_width)

    block_step = jax.checkpoint(decay_block)
    final_state, (numerator, denominator) = lax.scan(
        lambda carry_state, block_item: block_step(carry_state, block_item, decay_rate),
        (running_state_numerator, running_state_denominator, document_start_flag),
        (
            to_blocks(lookup_projection_lines),
            to_blocks(value_matrix_rows),
            to_blocks(document_index),
        ),
    )
    return (final_state, from_blocks(numerator), from_blocks(denominator))


def decay_core(
    lookup_projection_lines,
    value_matrix_rows,
    forgetting_multiplier,
    document_index,
    document_start_flag,
):
    decay_rate = jnp.exp(forgetting_multiplier)
    zero_state = jnp.zeros(
        (lookup_projection_lines.shape[0], lookup_projection_lines.shape[2]), jnp.float32
    )
    final_state, numerator, denominator = decay_sums(
        lookup_projection_lines,
        value_matrix_rows,
        document_index,
        decay_rate,
        document_start_flag,
        zero_state,
        zero_state,
    )
    token_count = lookup_projection_lines.shape[1]
    carry_factor = (document_index[:, -1] == document_start_flag).astype(jnp.float32)[
        :, None
    ] * jnp.exp(-token_count * decay_rate)[None]
    return (numerator, denominator, final_state[0], final_state[1], carry_factor)


def decay_finish(
    numerator,
    denominator,
    lookup_projection_lines,
    value_matrix_rows,
    forgetting_multiplier,
    present_extra_weight,
    running_state_numerator,
    running_state_denominator,
    local_numerator,
    local_denominator,
    carry_factor,
    document_index,
    document_start_flag,
):
    decay_rate = jnp.exp(forgetting_multiplier)
    token_count = lookup_projection_lines.shape[1]
    fade = (document_index == document_start_flag[:, None]).astype(jnp.float32)[
        :, :, None
    ] * jnp.exp(-jnp.arange(token_count).astype(jnp.float32)[:, None] * decay_rate)[None]
    initial_extra_weight = jnp.exp(present_extra_weight + lookup_projection_lines)
    weighted_mean = (
        numerator
        + fade * running_state_numerator[:, None]
        + initial_extra_weight * value_matrix_rows
    ) / (denominator + fade * running_state_denominator[:, None] + initial_extra_weight)
    return (
        weighted_mean,
        carry_factor * running_state_numerator + local_numerator,
        carry_factor * running_state_denominator + local_denominator,
    )


def decay_whole(
    lookup_projection_lines,
    value_matrix_rows,
    forgetting_multiplier,
    present_extra_weight,
    running_state_numerator,
    running_state_denominator,
    document_index,
    document_start_flag,
):
    numerator, denominator, local_numerator, local_denominator, carry_factor = decay_core(
        lookup_projection_lines,
        value_matrix_rows,
        forgetting_multiplier,
        document_index,
        document_start_flag,
    )
    return decay_finish(
        numerator,
        denominator,
        lookup_projection_lines,
        value_matrix_rows,
        forgetting_multiplier,
        present_extra_weight,
        running_state_numerator,
        running_state_denominator,
        local_numerator,
        local_denominator,
        carry_factor,
        document_index,
        document_start_flag,
    )


def combine_maps(earlier_map, later_map):
    return (
        earlier_map[0] * later_map[0],
        later_map[0] * earlier_map[1] + later_map[1],
        later_map[0] * earlier_map[2] + later_map[2],
    )


def chain_forward(carry_factor, local_numerator, local_denominator):
    unit_factor = jnp.ones_like(carry_factor)
    zero_state = jnp.zeros_like(carry_factor)
    _, running_state_numerator, running_state_denominator = prefix(
        (carry_factor, local_numerator, local_denominator),
        "seq",
        combine_maps,
        (unit_factor, zero_state, zero_state),
    )
    return (running_state_numerator, running_state_denominator)


def chain_backward(carry_factor, direct_numerator, direct_denominator):
    unit_factor = jnp.ones_like(carry_factor)
    zero_state = jnp.zeros_like(carry_factor)
    _, after_numerator, after_denominator = prefix_2(
        (carry_factor, direct_numerator, direct_denominator),
        "seq",
        combine_maps,
        (unit_factor, zero_state, zero_state),
    )
    return (after_numerator, after_denominator)


def product(left, weight):
    return jnp.einsum("rtd,de->rte", left, weight, preferred_element_type=jnp.float32)


def weight_grad(left, gradient):
    return jnp.einsum("rtd,rte->de", left, gradient, preferred_element_type=jnp.float32)


def input_grad(gradient, weight):
    return jnp.einsum("rte,de->rtd", gradient, weight, preferred_element_type=jnp.float32)


def shift_tokens(normalized, document_index, document_start_flag):
    edge_token = from_behind(normalized[:, -1], "seq", 1)
    before = jnp.concatenate([document_start_flag[:, None], document_index[:, :-1]], axis=1)
    joined = (document_index == before).astype(jnp.float32)[:, :, None]
    previous = jnp.concatenate([edge_token[:, None], normalized[:, :-1]], axis=1) * joined
    return (previous, joined)


def shift_back(grad_previous, joined):
    masked = grad_previous * joined
    edge_grad = from_behind(masked[:, 0], "seq", -1)
    return jnp.concatenate([masked[:, 1:], edge_grad[:, None]], axis=1)


def mix_back(mix_grads, channel_quantities, normalized, previous):
    grad_normalized = sum(
        (gradient * amount for gradient, amount in zip(mix_grads, channel_quantities))
    )
    grad_previous = sum(
        (gradient * (1.0 - amount) for gradient, amount in zip(mix_grads, channel_quantities))
    )
    difference = normalized - previous
    grad_amounts = [jnp.sum(gradient * difference, axis=(0, 1)) for gradient in mix_grads]
    return (grad_normalized, grad_previous, grad_amounts)


def layer_forward(layer_input, weights, document_index, document_start_flag):
    vectors, matrices, time_output, feed_key, feed_value = weights
    channel_quantities = vectors.astype(jnp.float32)
    normalized = layer_norm(layer_input, channel_quantities[0], channel_quantities[1])
    previous, joined = shift_tokens(normalized, document_index, document_start_flag)
    mix_key = (
        normalized * channel_quantities[2] + previous * (1.0 - channel_quantities[2])
    ).astype(jnp.bfloat16)
    mix_value = (
        normalized * channel_quantities[3] + previous * (1.0 - channel_quantities[3])
    ).astype(jnp.bfloat16)
    mix_recept = (
        normalized * channel_quantities[4] + previous * (1.0 - channel_quantities[4])
    ).astype(jnp.bfloat16)
    lookup_projection_lines = product(mix_key, matrices[0])
    value_matrix_rows = product(mix_value, matrices[1])
    receptance = product(mix_recept, matrices[2])
    numerator, denominator, local_numerator, local_denominator, carry_factor = decay_core(
        lookup_projection_lines,
        value_matrix_rows,
        channel_quantities[5],
        document_index,
        document_start_flag,
    )
    running_state_numerator, running_state_denominator = chain_forward(
        carry_factor, local_numerator, local_denominator
    )
    weighted_mean, _, _ = decay_finish(
        numerator,
        denominator,
        lookup_projection_lines,
        value_matrix_rows,
        channel_quantities[5],
        channel_quantities[6],
        running_state_numerator,
        running_state_denominator,
        local_numerator,
        local_denominator,
        carry_factor,
        document_index,
        document_start_flag,
    )
    gated_mean = (jax.nn.sigmoid(receptance) * weighted_mean).astype(jnp.bfloat16)
    middle = layer_input + product(gated_mean, time_output)
    normalized_two = layer_norm(middle, channel_quantities[7], channel_quantities[8])
    previous_two, joined_two = shift_tokens(normalized_two, document_index, document_start_flag)
    feed_mix = (
        normalized_two * channel_quantities[9] + previous_two * (1.0 - channel_quantities[9])
    ).astype(jnp.bfloat16)
    gate_mix = (
        normalized_two * channel_quantities[10] + previous_two * (1.0 - channel_quantities[10])
    ).astype(jnp.bfloat16)
    hidden_input = product(feed_mix, feed_key)
    hidden = jnp.square(jax.nn.softplus(hidden_input)).astype(jnp.bfloat16)
    value_branch = product(hidden, feed_value)
    gate_logit = product(gate_mix, matrices[3])
    layer_response = middle + jax.nn.sigmoid(gate_logit) * value_branch
    saved = (
        layer_input,
        normalized,
        previous,
        joined,
        mix_key,
        mix_value,
        mix_recept,
        lookup_projection_lines,
        value_matrix_rows,
        receptance,
        weighted_mean,
        gated_mean,
        running_state_numerator,
        running_state_denominator,
        carry_factor,
        middle,
        normalized_two,
        previous_two,
        joined_two,
        feed_mix,
        gate_mix,
        hidden_input,
        hidden,
        value_branch,
        gate_logit,
    )
    return (layer_response, saved)


def layer_backward(gradient, saved, weights, document_index, document_start_flag):
    (
        layer_input,
        normalized,
        previous,
        joined,
        mix_key,
        mix_value,
        mix_recept,
        lookup_projection_lines,
        value_matrix_rows,
        receptance,
        weighted_mean,
        gated_mean,
        running_state_numerator,
        running_state_denominator,
        carry_factor,
        middle,
        normalized_two,
        previous_two,
        joined_two,
        feed_mix,
        gate_mix,
        hidden_input,
        hidden,
        value_branch,
        gate_logit,
    ) = saved
    vectors, matrices, time_output, feed_key, feed_value = weights
    channel_quantities = vectors.astype(jnp.float32)
    gate_sigmoid = jax.nn.sigmoid(gate_logit)
    grad_branch = (gradient * gate_sigmoid).astype(jnp.bfloat16)
    grad_gate = (gradient * value_branch * gate_sigmoid * (1.0 - gate_sigmoid)).astype(jnp.bfloat16)
    grad_feed_value = weight_grad(hidden, grad_branch)
    grad_hidden = input_grad(grad_branch, feed_value)
    grad_input_pre = (
        grad_hidden * 2.0 * jax.nn.softplus(hidden_input) * jax.nn.sigmoid(hidden_input)
    ).astype(jnp.bfloat16)
    grad_feed_key = weight_grad(feed_mix, grad_input_pre)
    grad_gate_matrix = weight_grad(gate_mix, grad_gate)
    grad_feed_mix = input_grad(grad_input_pre, feed_key)
    grad_gate_mix = input_grad(grad_gate, matrices[3])
    grad_norm_two, grad_previous_two, channel_amounts = mix_back(
        (grad_feed_mix, grad_gate_mix),
        (channel_quantities[9], channel_quantities[10]),
        normalized_two,
        previous_two,
    )
    grad_norm_two = grad_norm_two + shift_back(grad_previous_two, joined_two)
    _, second_pull = jax.vjp(layer_norm, middle, channel_quantities[7], channel_quantities[8])
    grad_middle_norm, grad_gain_two, grad_bias_two = second_pull(grad_norm_two)
    grad_middle = gradient + grad_middle_norm
    grad_block = grad_middle.astype(jnp.bfloat16)
    grad_time_output = weight_grad(gated_mean, grad_block)
    grad_gated = input_grad(grad_block, time_output)
    recept_sigmoid = jax.nn.sigmoid(receptance)
    grad_receptance = (grad_gated * weighted_mean * recept_sigmoid * (1.0 - recept_sigmoid)).astype(
        jnp.bfloat16
    )
    grad_weighted = grad_gated * recept_sigmoid
    local_decay = partial(
        decay_whole, document_index=document_index, document_start_flag=document_start_flag
    )
    _, decay_pull = jax.vjp(
        local_decay,
        lookup_projection_lines,
        value_matrix_rows,
        channel_quantities[5],
        channel_quantities[6],
        running_state_numerator,
        running_state_denominator,
    )
    zero_state = jnp.zeros_like(running_state_numerator)
    immediate_contribution = decay_pull((grad_weighted, zero_state, zero_state))
    after_numerator, after_denominator = chain_backward(
        carry_factor, immediate_contribution[4], immediate_contribution[5]
    )
    recurrent_memory = decay_pull(
        (jnp.zeros_like(grad_weighted), after_numerator, after_denominator)
    )
    grad_keys = (immediate_contribution[0] + recurrent_memory[0]).astype(jnp.bfloat16)
    grad_values = (immediate_contribution[1] + recurrent_memory[1]).astype(jnp.bfloat16)
    grad_decay = immediate_contribution[2] + recurrent_memory[2]
    extra_weight_cotangent = immediate_contribution[3] + recurrent_memory[3]
    grad_key_matrix = weight_grad(mix_key, grad_keys)
    grad_value_matrix = weight_grad(mix_value, grad_values)
    grad_recept_matrix = weight_grad(mix_recept, grad_receptance)
    grad_mix_key = input_grad(grad_keys, matrices[0])
    grad_mix_value = input_grad(grad_values, matrices[1])
    grad_mix_recept = input_grad(grad_receptance, matrices[2])
    grad_normalized, grad_previous, time_amounts = mix_back(
        (grad_mix_key, grad_mix_value, grad_mix_recept),
        (channel_quantities[2], channel_quantities[3], channel_quantities[4]),
        normalized,
        previous,
    )
    grad_normalized = grad_normalized + shift_back(grad_previous, joined)
    _, first_pull = jax.vjp(layer_norm, layer_input, channel_quantities[0], channel_quantities[1])
    grad_input_norm, grad_gain, grad_bias = first_pull(grad_normalized)
    grad_input = grad_middle + grad_input_norm
    grad_vectors = jnp.stack(
        [
            grad_gain,
            grad_bias,
            time_amounts[0],
            time_amounts[1],
            time_amounts[2],
            grad_decay,
            extra_weight_cotangent,
            grad_gain_two,
            grad_bias_two,
            channel_amounts[0],
            channel_amounts[1],
        ]
    )
    grad_matrices = jnp.stack(
        [grad_key_matrix, grad_value_matrix, grad_recept_matrix, grad_gate_matrix]
    )
    return (
        grad_input,
        (grad_vectors, grad_matrices, grad_time_output, grad_feed_key, grad_feed_value),
    )


def vector_rates(row_total):
    present_sequence_slot = jnp.arange(row_total)
    special = (present_sequence_slot == 5) | (present_sequence_slot == 6)
    return jnp.where(special, rate_time, rate_main)[:, None]


def adam_step(parameter, gradient, first_moment, second_moment, learning_rates, decay_weight):
    new_first = beta_one * first_moment + (1.0 - beta_one) * gradient
    new_second = beta_two * second_moment + (1.0 - beta_two) * gradient * gradient
    step_ratio = (
        new_first
        / (1.0 - beta_one**step_count)
        / (jnp.sqrt(new_second / (1.0 - beta_two**step_count)) + adam_epsilon)
    )
    return (learning_rates * (step_ratio + decay_weight * parameter), new_first, new_second)


def body(
    tokens,
    cotangent,
    document_starts,
    vectors,
    matrices,
    time_output,
    feed_key,
    feed_value,
    mean_vectors,
    mean_matrices,
    mean_output,
    mean_key,
    mean_value,
    power_vectors,
    power_matrices,
    power_output,
    power_key,
    power_value,
):
    row_count, token_count, model_width = tokens.shape
    layer_total = vectors.shape[0]
    seq_index = lax.axis_index("seq")
    positions = seq_index * token_count + jnp.arange(token_count, dtype=jnp.int32)
    document_index = jnp.sum(
        (document_starts[:, :, None] <= positions[None, None, :]).astype(jnp.int32), axis=1
    )
    document_start_flag = jnp.sum(
        (document_starts <= seq_index * token_count - 1).astype(jnp.int32), axis=1
    )
    gathered = (
        lax.all_gather(vectors.astype(jnp.bfloat16), ("dp", "seq"), axis=2, tiled=True),
        lax.all_gather(matrices.astype(jnp.bfloat16), ("dp", "seq"), axis=2, tiled=True),
        lax.all_gather(time_output.astype(jnp.bfloat16), ("dp", "seq"), axis=1, tiled=True),
        lax.all_gather(feed_key.astype(jnp.bfloat16), ("dp", "seq"), axis=1, tiled=True),
        lax.all_gather(feed_value.astype(jnp.bfloat16), ("dp", "seq"), axis=1, tiled=True),
    )
    per_layer = [
        tuple((weight[layer_index] for weight in gathered)) for layer_index in range(layer_total)
    ]
    hidden_state = tokens.astype(jnp.float32)
    saved_layers = []
    for layer_index in range(layer_total):
        hidden_state, saved = layer_forward(
            hidden_state, per_layer[layer_index], document_index, document_start_flag
        )
        saved_layers.append(saved)
    block_out = hidden_state.astype(jnp.bfloat16)
    gradient = cotangent.astype(jnp.float32)
    collected = []
    for layer_index in reversed(range(layer_total)):
        gradient, layer_grads = layer_backward(
            gradient,
            saved_layers[layer_index],
            per_layer[layer_index],
            document_index,
            document_start_flag,
        )
        collected.insert(0, layer_grads)
    stacked = tuple(
        (jnp.stack([layer_grads[member] for layer_grads in collected]) for member in range(5))
    )
    shards = (
        lax.psum_scatter(stacked[0], ("dp", "seq"), scatter_dimension=2, tiled=True),
        lax.psum_scatter(stacked[1], ("dp", "seq"), scatter_dimension=2, tiled=True),
        lax.psum_scatter(stacked[2], ("dp", "seq"), scatter_dimension=1, tiled=True),
        lax.psum_scatter(stacked[3], ("dp", "seq"), scatter_dimension=1, tiled=True),
        lax.psum_scatter(stacked[4], ("dp", "seq"), scatter_dimension=1, tiled=True),
    )
    vector_new = adam_step(
        vectors, shards[0], mean_vectors, power_vectors, vector_rates(vectors.shape[1]), 0.0
    )
    matrix_new = adam_step(
        matrices, shards[1], mean_matrices, power_matrices, rate_main, weight_decay
    )
    output_new = adam_step(
        time_output, shards[2], mean_output, power_output, rate_main, weight_decay
    )
    key_new = adam_step(feed_key, shards[3], mean_key, power_key, rate_main, weight_decay)
    value_new = adam_step(feed_value, shards[4], mean_value, power_value, rate_main, weight_decay)
    return (
        block_out,
        gradient,
        shards[0],
        shards[1],
        shards[2],
        shards[3],
        shards[4],
        vector_new[0],
        matrix_new[0],
        output_new[0],
        key_new[0],
        value_new[0],
        vector_new[1],
        matrix_new[1],
        output_new[1],
        key_new[1],
        value_new[1],
        vector_new[2],
        matrix_new[2],
        output_new[2],
        key_new[2],
        value_new[2],
    )


def solution(mesh):
    in_specs = (
        P("dp", "seq", None),
        P("dp", "seq", None),
        P("dp", None),
        P(None, None, ("dp", "seq")),
        P(None, None, ("dp", "seq"), None),
        P(None, ("dp", "seq"), None),
        P(None, ("dp", "seq"), None),
        P(None, ("dp", "seq"), None),
        P(None, None, ("dp", "seq")),
        P(None, None, ("dp", "seq"), None),
        P(None, ("dp", "seq"), None),
        P(None, ("dp", "seq"), None),
        P(None, ("dp", "seq"), None),
        P(None, None, ("dp", "seq")),
        P(None, None, ("dp", "seq"), None),
        P(None, ("dp", "seq"), None),
        P(None, ("dp", "seq"), None),
        P(None, ("dp", "seq"), None),
    )
    out_specs = (
        P("dp", "seq", None),
        P("dp", "seq", None),
        P(None, None, ("dp", "seq")),
        P(None, None, ("dp", "seq"), None),
        P(None, ("dp", "seq"), None),
        P(None, ("dp", "seq"), None),
        P(None, ("dp", "seq"), None),
        P(None, None, ("dp", "seq")),
        P(None, None, ("dp", "seq"), None),
        P(None, ("dp", "seq"), None),
        P(None, ("dp", "seq"), None),
        P(None, ("dp", "seq"), None),
        P(None, None, ("dp", "seq")),
        P(None, None, ("dp", "seq"), None),
        P(None, ("dp", "seq"), None),
        P(None, ("dp", "seq"), None),
        P(None, ("dp", "seq"), None),
        P(None, None, ("dp", "seq")),
        P(None, None, ("dp", "seq"), None),
        P(None, ("dp", "seq"), None),
        P(None, ("dp", "seq"), None),
        P(None, ("dp", "seq"), None),
    )
    return jax.shard_map(body, mesh=mesh, in_specs=in_specs, out_specs=out_specs, check_vma=False)
```

profile of v0, /device:TPU:0, one launch (start us, length us, event | category | flops | bytes accessed | tf_op | source)
XLA Modules:
  0.0 2419.3 jit_solution(18088838012671695971)
XLA Ops:
  11.8 45.4 %all_gather.67 = bf16[2,11,768]{1,0,2:T(2,128)(2,1)S(1)} all-gather(bf16[2,11,24]{1,0,2:T(2,128)(2,1)S(1)} %copy.410), channel_id=1, replica_groups=mesh['dp'=4,'seq'=8] {'dp','seq'}, dimensions={2}, use_global_device_ids=true | all-gather | bytes 34848 | tf_op jit(solution)/shard_map/all_gather | solution.py:568
  58.4 36.0 %exponential_reduce_fusion = (f32[768]{0:T(1024)S(1)}, f32[768]{0:T(1024)S(1)}, f32[768]{0:T(1024)S(1)}, f32[768]{0:T(1024)S(1)}, f32[768]{0:T(1024)}, /*index=5...) fusion(f32[1,11,768]{1,0,2:T(1,128)S(1)} %get-tuple-element.4273), kind=kLoop, calls=%fused_computation.670 | loop fusion | flops 1536 | bytes 73728 | tf_op jit(solution)/shard_map/exp | solution.py:104
  101.9 36.1 %exponential_reduce_fusion.1 = (f32[768]{0:T(1024)}, f32[768]{0:T(1024)S(1)}, f32[768]{0:T(1024)}, f32[768]{0:T(1024)}, f32[768]{0:T(1024)}, /*index=5*/f32[768]...) fusion(f32[1,11,768]{1,0,2:T(1,128)S(1)} %get-tuple-element.4272), kind=kLoop, calls=%fused_computation.671 | loop fusion | flops 1536 | bytes 73728 | tf_op jit(solution)/shard_map/exp | solution.py:104
  141.7 15.4 all_gather.69
  171.1 72.3 %while.262 = (s32[]{:T(128)}, f32[4,768]{1,0:T(4,128)S(1)}, f32[4,768]{1,0:T(4,128)S(1)}, s32[4]{0:T(128)S(1)}, f32[16,4,8,768]{3,2,1,0:T(8,128)}, /*index=5*/f3...) while((s32[]{:T(128)}, f32[4,768]{1,0:T(4,128)S(1)}, ...), condition=%wide.region_9.10_spmd.clone, body=%wide.region_4.9_spmd.clone.sunk | while | flops 1282995 | bytes 1836687 | solution.py:133
  248.0 100.6 %while.273 = (s32[]{:T(128)}, f32[4,768]{1,0:T(4,128)S(1)}, f32[4,768]{1,0:T(4,128)S(1)}, s32[4]{0:T(128)S(1)}, f32[16,4,8,768]{3,2,1,0:T(8,128)}, /*index=5*/f3...) while((s32[]{:T(128)}, f32[4,768]{1,0:T(4,128)S(1)}, ...), condition=%wide.region_73.74_spmd.clone.clone.clone, body=%wide.region_68.73_spmd.clone.clone.clone.sunk | while | flops 1232715 | bytes 1685599 | solution.py:133
  348.7 14.0 all-gather.4
  362.6 14.0 all-gather.5
  382.5 10.2 fusion.247
  410.5 9.9 fusion.138
  427.6 15.1 all_gather.77
  455.6 143.4 %while.264 = (s32[]{:T(128)}, f32[4,768]{1,0:T(4,128)}, f32[4,768]{1,0:T(4,128)}, s32[4]{0:T(128)S(1)}, f32[16,4,8,768]{3,2,1,0:T(8,128)}, /*index=5*/f32[16,4,8...) while((s32[]{:T(128)}, f32[4,768]{1,0:T(4,128)}, ...), condition=%wide.region_21.22_spmd.clone, body=%wide.region_16.21_spmd.clone.sunk | while | flops 1282995 | bytes 1836779 | solution.py:133
  599.7 14.0 all-gather.6
  614.4 14.0 all-gather.7
  628.4 10.8 while.265
  643.8 242.1 %while.272 = (s32[]{:T(128)}, f32[4,768]{1,0:T(4,128)}, f32[4,768]{1,0:T(4,128)}, s32[4]{0:T(128)}, f32[16,4,8,768]{3,2,1,0:T(8,128)}, /*index=5*/f32[16,4,8,768...) while((s32[]{:T(128)}, f32[4,768]{1,0:T(4,128)}, ...), condition=%wide.region_33.34_spmd.clone.clone.clone, body=%wide.region_28.33_spmd.clone.clone.clone.sunk | while | flops 1232715 | bytes 1688151 | solution.py:133
  885.9 9.9 fusion.251
  916.9 9.7 multiply_convert_fusion.1
  955.9 101.1 %while.266 = (s32[]{:T(128)}, f32[768]{0:T(1024)S(1)}, f32[4,768]{1,0:T(4,128)S(1)}, f32[4,768]{1,0:T(4,128)S(1)}, f32[16,4,8,768]{3,2,1,0:T(8,128)}, /*index=5*...) while((s32[]{:T(128)}, f32[768]{0:T(1024)S(1)}, ...), condition=%wide.region_46.47_spmd.clone, body=%wide.region_34.46_spmd.clone.sunk | while | flops 2806708 | bytes 3892252 | solution.py:133
  1057.0 14.9 all_gather.82
  1071.9 14.0 all_gather.83
  1099.0 101.1 %while.268 = (s32[]{:T(128)}, f32[768]{0:T(1024)S(1)}, f32[4,768]{1,0:T(4,128)S(1)}, f32[4,768]{1,0:T(4,128)S(1)}, f32[16,4,8,768]{3,2,1,0:T(8,128)}, /*index=5*...) while((s32[]{:T(128)}, f32[768]{0:T(1024)S(1)}, ...), condition=%wide.region_63.64_spmd.clone, body=%wide.region_51.63_spmd.clone.sunk | while | flops 2800564 | bytes 3843099 | solution.py:133
  1224.9 9.0 multiply_convert_fusion
  1261.9 16.9 all_gather.84
  1278.8 14.1 all_gather.85
  1303.9 101.0 %while.269 = (s32[]{:T(128)}, f32[768]{0:T(1024)S(1)}, f32[4,768]{1,0:T(4,128)S(1)}, f32[4,768]{1,0:T(4,128)S(1)}, f32[16,4,8,768]{3,2,1,0:T(8,128)}, /*index=5*...) while((s32[]{:T(128)}, f32[768]{0:T(1024)S(1)}, ...), condition=%wide.region_86.87_spmd.clone, body=%wide.region_74.86_spmd.clone.sunk | while | flops 2806708 | bytes 3892252 | solution.py:133
  1411.7 101.1 %while.271 = (s32[]{:T(128)}, f32[768]{0:T(1024)S(1)}, f32[4,768]{1,0:T(4,128)S(1)}, f32[4,768]{1,0:T(4,128)S(1)}, f32[16,4,8,768]{3,2,1,0:T(8,128)}, /*index=5*...) while((s32[]{:T(128)}, f32[768]{0:T(1024)S(1)}, ...), condition=%wide.region_103.104_spmd.clone, body=%wide.region_91.103_spmd.clone.sunk | while | flops 2800564 | bytes 3843099 | solution.py:133
  1606.2 53.4 %all-reduce.3.cloned.1.call-done = f32[2,11,768]{2,1,0:T(8,128)} async-done(((f32[2,11,768]{2,1,0:T(8,128)}), f32[2,11,768]{2,1,0:T(8,128)}) %all-reduce.3.cloned.1.call-update) | async-done | bytes 67600
  1662.8 110.5 %reduce-scatter.8.cloned.1.call-done = f32[2,24,768]{2,1,0:T(8,128)} async-done(((f32[2,768,768]{2,1,0:T(8,128)}), f32[2,24,768]{2,1,0:T(8,128)}) %reduce-scatter.8.cloned.1.call-update) | async-done | bytes 147472 | tf_op jit(solution)/shard_map/reduce_scatter | solution.py:602
  1775.1 210.5 %reduce-scatter.12.cloned.1.call-done = f32[2,96,768]{2,1,0:T(8,128)} async-done(((f32[2,3072,768]{2,1,0:T(8,128)}), f32[2,96,768]{2,1,0:T(8,128)}) %reduce-scatter.12.cloned.1.call-update) | async-done | bytes 589840 | tf_op jit(solution)/shard_map/reduce_scatter | solution.py:604
  1988.3 209.3 %reduce-scatter.10.cloned.1.call-done = f32[2,24,3072]{2,1,0:T(8,128)} async-done(((f32[2,768,3072]{2,1,0:T(8,128)}), f32[2,24,3072]{2,1,0:T(8,128)}) %reduce-scatter.10.cloned.1.call-update) | async-done | bytes 589840 | tf_op jit(solution)/shard_map/reduce_scatter | solution.py:603
  2200.2 209.5 %reduce-scatter.6.cloned.1.call-done = f32[2,4,24,768]{3,2,1,0:T(8,128)} async-done(((f32[2,4,768,768]{3,2,1,0:T(8,128)}), f32[2,4,24,768]{3,2,1,0:T(8,128)}) %reduce-scatter.6.cloned.1.call-update) | async-done | bytes 589840 | tf_op jit(solution)/shard_map/reduce_scatter | solution.py:601
  (3490 shorter events, 1305.5 us)
Async XLA Ops:
  7.2 153.4 %all-gather.13.cloned.1.call-start = ((), (), s32[]{:S(2)}) async-start(), calls=%async_computation.4 | async-start | bytes 9732096 | tf_op jit(solution)/shard_map/all_gather | solution.py:569
  9.2 383.5 %all-gather.15.cloned.1.call-start = ((), (), s32[]{:S(2)}) async-start(), calls=%async_computation.5 | async-start | bytes 2433024 | tf_op jit(solution)/shard_map/all_gather | solution.py:570
  10.8 391.6 %all-gather.17.cloned.1.call-start = ((), (), s32[]{:S(2)}) async-start(), calls=%async_computation.6 | async-start | bytes 9732096 | tf_op jit(solution)/shard_map/all_gather | solution.py:571
  11.7 398.8 %all-gather.19.cloned.1.call-start = ((), (), s32[]{:S(2)}) async-start(), calls=%async_computation.7 | async-start | bytes 9732096 | tf_op jit(solution)/shard_map/all_gather | solution.py:572
  94.5 305.8 %copy-start.144 = (f32[768]{0:T(1024)}, f32[768]{0:T(1024)S(1)}, u32[]{:S(2)}) copy-start(f32[768]{0:T(1024)S(1)} %get-tuple-element.3728) | copy-start | bytes 9220
  94.5 305.8 %copy-start.167 = (f32[768]{0:T(1024)}, f32[768]{0:T(1024)S(1)}, u32[]{:S(2)}) copy-start(f32[768]{0:T(1024)S(1)} %get-tuple-element.3725) | copy-start | bytes 9220
  95.6 61.5 %collective-permute-start = (f32[4,768]{1,0:T(4,128)}, f32[4,768]{1,0:T(4,128)}, u32[]{:S(2)}, u32[]{:S(2)}) collective-permute-start(f32[4,768]{1,0:T(4,128)} %bitcast.619), channel_id=1, source_target_pairs={{0,1},{1,2},{2,3},{3,4},{4,5},{5,6},{6,7},{8,9},{9,10},{10,11},{11... | collective-permute-start | bytes 36872 | tf_op jit(solution)/shard_map/ppermute | solution.py:71
  99.2 1560.3 %all-reduce.3.cloned.1.call-start = ((), (), s32[]{:S(2)}) async-start(), calls=%async_computation.12 | async-start | bytes 196608
  101.9 340.8 %copy-start.132 = (f32[4,128]{1,0:T(4,128)}, f32[4,128]{1,0:T(4,128)S(1)}, u32[]{:S(2)}) copy-start(f32[4,128]{1,0:T(4,128)S(1)} %get-tuple-element.4281) | copy-start | bytes 6148
  138.0 304.7 %copy-start.134 = (f32[768]{0:T(1024)}, f32[768]{0:T(1024)S(1)}, u32[]{:S(2)}) copy-start(f32[768]{0:T(1024)S(1)} %get-tuple-element.3748) | copy-start | bytes 9220
  138.0 304.7 %copy-start.153 = (f32[768]{0:T(1024)}, f32[768]{0:T(1024)S(1)}, u32[]{:S(2)}) copy-start(f32[768]{0:T(1024)S(1)} %get-tuple-element.3746) | copy-start | bytes 9220
  138.0 304.7 %copy-start.155 = (f32[768]{0:T(1024)}, f32[768]{0:T(1024)S(1)}, u32[]{:S(2)}) copy-start(f32[768]{0:T(1024)S(1)} %get-tuple-element.3743) | copy-start | bytes 9220
  138.0 304.8 %copy-start.157 = (f32[768]{0:T(1024)}, f32[768]{0:T(1024)S(1)}, u32[]{:S(2)}) copy-start(f32[768]{0:T(1024)S(1)} %get-tuple-element.3744) | copy-start | bytes 9220
  396.6 3.7 collective-permute-start.1
  425.7 17.0 collective-permute-start.2
  897.8 3.0 collective-permute-start.3
  934.4 3.1 collective-permute-start.4
  1214.8 3.1 collective-permute-start.5
  1241.5 4.7 collective-permute-start.6
  1527.9 3.2 collective-permute-start.7
  1538.5 234.9 %reduce-scatter.8.cloned.1.call-start = ((), (), s32[]{:S(2)}) async-start(), calls=%async_computation.9 | async-start | bytes 4866048 | tf_op jit(solution)/shard_map/reduce_scatter | solution.py:602
  1543.4 442.3 %reduce-scatter.12.cloned.1.call-start = ((), (), s32[]{:S(2)}) async-start(), calls=%async_computation.11 | async-start | bytes 19464192 | tf_op jit(solution)/shard_map/reduce_scatter | solution.py:604
  1567.2 630.4 %reduce-scatter.10.cloned.1.call-start = ((), (), s32[]{:S(2)}) async-start(), calls=%async_computation.10 | async-start | bytes 19464192 | tf_op jit(solution)/shard_map/reduce_scatter | solution.py:603
  1582.2 827.6 %reduce-scatter.6.cloned.1.call-start = ((), (), s32[]{:S(2)}) async-start(), calls=%async_computation.8 | async-start | bytes 19464192 | tf_op jit(solution)/shard_map/reduce_scatter | solution.py:601
  1606.1 379.5 %copy-start.88 = (f32[2,96,768]{2,1,0:T(8,128)S(1)}, f32[2,96,768]{2,1,0:T(8,128)}, u32[]{:S(2)}) copy-start(f32[2,96,768]{2,1,0:T(8,128)} %param.49) | copy-start | bytes 1769476
  1606.1 379.5 %copy-start.127 = (f32[2,96,768]{2,1,0:T(8,128)S(1)}, f32[2,96,768]{2,1,0:T(8,128)}, u32[]{:S(2)}) copy-start(f32[2,96,768]{2,1,0:T(8,128)} %param.54) | copy-start | bytes 1769476
  1775.1 422.6 %copy-start.90 = (f32[2,24,3072]{2,1,0:T(8,128)S(1)}, f32[2,24,3072]{2,1,0:T(8,128)}, u32[]{:S(2)}) copy-start(f32[2,24,3072]{2,1,0:T(8,128)} %param.48) | copy-start | bytes 1769476
  1775.1 422.6 %copy-start.128 = (f32[2,24,3072]{2,1,0:T(8,128)S(1)}, f32[2,24,3072]{2,1,0:T(8,128)}, u32[]{:S(2)}) copy-start(f32[2,24,3072]{2,1,0:T(8,128)} %param.53) | copy-start | bytes 1769476
  1775.1 422.6 %copy-start.129 = (f32[2,24,3072]{2,1,0:T(8,128)S(1)}, f32[2,24,3072]{2,1,0:T(8,128)}, u32[]{:S(2)}) copy-start(f32[2,24,3072]{2,1,0:T(8,128)} %param.58) | copy-start | bytes 1769476
  1988.3 421.4 %copy-start.91 = (f32[2,4,24,768]{3,2,1,0:T(8,128)S(1)}, f32[2,4,24,768]{3,2,1,0:T(8,128)}, u32[]{:S(2)}) copy-start(f32[2,4,24,768]{3,2,1,0:T(8,128)} %param.46) | copy-start | bytes 1769476
  1988.3 421.4 %copy-start.130 = (f32[2,4,24,768]{3,2,1,0:T(8,128)S(1)}, f32[2,4,24,768]{3,2,1,0:T(8,128)}, u32[]{:S(2)}) copy-start(f32[2,4,24,768]{3,2,1,0:T(8,128)} %param.51) | copy-start | bytes 1769476
  1988.3 421.4 %copy-start.131 = (f32[2,4,24,768]{3,2,1,0:T(8,128)S(1)}, f32[2,4,24,768]{3,2,1,0:T(8,128)}, u32[]{:S(2)}) copy-start(f32[2,4,24,768]{3,2,1,0:T(8,128)} %param.56) | copy-start | bytes 1769476
  (314 other events, 3277.7 us)
Sparse Core Ops, SparseCore 0:
  11.8 85.2 all-gather.12
  100.9 56.1 all-gather.14
  160.8 81.3 all-gather.16
  245.8 80.9 all-gather.18
  1538.6 120.9 all-reduce.2
  1665.4 107.8 reduce-scatter.7
  1781.4 204.1 reduce-scatter.11
  1993.7 203.8 reduce-scatter.9
  2205.8 203.9 reduce-scatter.5
where the time goes:
time: 2460 us; the launch traced here: 2420 us
  waiting for transfers between devices  796 us (32%)
  other arithmetic  792 us (32%)
  local copies, waits for them, and re-layouts  439 us (18%)
  blocking collectives  192 us (8%)
  matrix products  159 us (6%)
    squeeze x320, local copies, waits for them, and re-layouts, decay_sums(): lax.scan(lambda carry_state, block_item: block_step(carry_state, block_it...  257 us
    reduce_scatter x1, waiting for transfers between devices, body(): lax.psum_scatter(stacked[4], ('dp', 'seq'), scatter_dimension=1, tiled=True)  211 us
    reduce_scatter x1, waiting for transfers between devices, body(): lax.psum_scatter(stacked[1], ('dp', 'seq'), scatter_dimension=2, tiled=True)  210 us
    reduce_scatter x1, waiting for transfers between devices, body(): lax.psum_scatter(stacked[3], ('dp', 'seq'), scatter_dimension=1, tiled=True)  209 us
    dynamic_update_slice x160, other arithmetic, decay_sums(): lax.scan(lambda carry_state, block_item: block_step(carry_state, block_it...  154 us
    reduce_scatter x1, waiting for transfers between devices, body(): lax.psum_scatter(stacked[2], ('dp', 'seq'), scatter_dimension=1, tiled=True)  110 us
    all_gather x6, blocking collectives, prefix(): lax.all_gather(part.astype(kind), axis)  86.4 us
    reduce_sum x64, other arithmetic, decay_block(): jnp.sum(tail_weight * exp_keys, axis=1)  85.2 us
  transfers between devices with their start and end apart: 17, of which 8 were waited for; matrix products, arithmetic and copies ran while one was open for 16% of the time, Pallas kernels for 0%

commit v1 on v0

v1 whole, which is shorter than its diff:
```python
import jax
import jax.numpy as jnp
from jax import lax
from jax.experimental import pallas as pl
from jax.experimental.pallas import tpu as pltpu
from jax.sharding import PartitionSpec as P

norm_epsilon = 1e-05
beta_one = 0.9
beta_two = 0.99
adam_epsilon = 1e-08
step_count = 10
rate_main = 0.0006
rate_time = 0.0012
weight_decay = 0.1

RB = 2
VMEM = 48 * 1024 * 1024
F32, BF16 = jnp.float32, jnp.bfloat16


def wide(mask, width):
    return jnp.concatenate([mask] * (width // 128), axis=1)


def dot_nn(a, b):
    return lax.dot_general(a, b, (((1,), (0,)), ((), ())), preferred_element_type=F32)


def dot_nt(a, b):
    return lax.dot_general(a, b, (((1,), (1,)), ((), ())), preferred_element_type=F32)


def colsum(a):
    return jnp.sum(a, axis=0, keepdims=True)


def places(starts_ref, base_ref, first_row, rows, T):
    at = lax.broadcasted_iota(jnp.int32, (T, 128), 0)
    base = base_ref[0]
    local, dist, tail = [], [], []
    for q in range(rows):
        begin = jnp.zeros((T, 128), jnp.int32)
        last_begin = jnp.int32(0)
        for j in range(starts_ref.shape[1]):
            s = starts_ref[first_row + q, j]
            begin = jnp.where(at + base >= s, jnp.maximum(begin, s), begin)
            last_begin = jnp.where(base + T - 1 >= s, jnp.maximum(last_begin, s), last_begin)
        local.append(at)
        dist.append(at + base - begin)
        tail.append((at + base >= last_begin).astype(F32))
    return tuple(jnp.concatenate(z, axis=0) for z in (local, dist, tail))


def norm_parts(x):
    centred = x - jnp.mean(x, axis=-1, keepdims=True)
    rstd = lax.rsqrt(jnp.mean(centred * centred, axis=-1, keepdims=True) + norm_epsilon)
    return centred * rstd, rstd


def shifted(normalized, edge, local, joined, T):
    M, D = normalized.shape
    rolled = pltpu.roll(normalized, 1, 0)
    edges = jnp.concatenate(
        [jnp.broadcast_to(edge[q : q + 1], (T, D)) for q in range(M // T)], axis=0
    )
    return jnp.where(wide(local, D) == 0, edges, rolled) * wide(joined, D)


def shift_up(masked, local, T):
    M, D = masked.shape
    rolled = pltpu.roll(masked, M - 1, 0)
    return jnp.where(wide(local, D) == T - 1, 0.0, rolled)


def row_firsts(a, T):
    return jnp.concatenate([a[q * T : q * T + 1] for q in range(a.shape[0] // T)], axis=0)


def row_lasts(a, T):
    return jnp.concatenate(
        [a[q * T + T - 1 : q * T + T] for q in range(a.shape[0] // T)], axis=0
    )


def levels(T):
    k = 1
    while k < T:
        yield k
        k *= 2


def scan_down(pair, rate, local, dist, T):
    M, D = pair[0].shape
    for k in levels(T):
        keep = ((dist >= k) & (local >= k)).astype(F32)
        weight = wide(keep, D) * jnp.exp(-float(k) * rate)
        pair = tuple(a + weight * pltpu.roll(a, k, 0) for a in pair)
    return pair


def scan_up(pair, rate, local, dist, T):
    M, D = pair[0].shape
    for k in levels(T):
        keep = ((dist >= k) & (local >= k)).astype(F32)
        weight = wide(keep, D) * jnp.exp(-float(k) * rate)
        pair = tuple(a + pltpu.roll(weight * a, M - k, 0) for a in pair)
    return pair


def per_row(values, T, D):
    return jnp.concatenate(
        [jnp.broadcast_to(values[q : q + 1], (T, D)) for q in range(values.shape[0])], axis=0
    )


def k_time_in(T, starts, base, x, edge, vec, wk, wv, wr,
              mk, mv, mr, ko, vo, ro, no, do, last):
    D = x.shape[1]
    i = pl.program_id(0)
    local, dist, _ = places(starts, base, i * RB, RB, T)
    joined = (dist >= 1).astype(F32)
    gain, bias = vec[0:1], vec[1:2]
    normalized = norm_parts(x[...].astype(F32))[0] * gain + bias
    edge_norm = norm_parts(edge[0])[0] * gain + bias
    previous = shifted(normalized, edge_norm, local, joined, T)
    for j, out in ((2, mk), (3, mv), (4, mr)):
        mu = vec[j : j + 1]
        out[...] = (normalized * mu + previous * (1.0 - mu)).astype(BF16)
    key = dot_nn(mk[...], wk[...])
    value = dot_nn(mv[...], wv[...])
    ko[...] = key
    vo[...] = value
    ro[...] = dot_nn(mr[...], wr[...]).astype(ro.dtype)
    rate = jnp.exp(vec[5:6])
    weight = jnp.exp(key)
    num, den = scan_down((weight * value, weight), rate, local, dist, T)
    keep = wide(((dist >= 1) & (local >= 1)).astype(F32), D)
    no[...] = keep * pltpu.roll(num, 1, 0)
    do[...] = keep * pltpu.roll(den, 1, 0)
    ends = (row_lasts(num, T), row_lasts(den, T))
    for q in range(RB):
        last[q] = jnp.concatenate([ends[0][q : q + 1], ends[1][q : q + 1]], axis=0)


def decay_state(vec, key, value, num, den, state, local, dist, T):
    D = key.shape[1]
    rate = jnp.exp(vec[5:6])
    fade = wide((dist >= local + 1).astype(F32), D) * jnp.exp(
        -wide(local.astype(F32), D) * rate
    )
    full_n = num + fade * per_row(state[:, 0], T, D)
    full_d = den + fade * per_row(state[:, 1], T, D)
    extra = jnp.exp(vec[6:7] + key)
    inverse = 1.0 / (full_d + extra)
    mean = (full_n + extra * value) * inverse
    return full_n, full_d, extra, inverse, mean


def k_time_out(T, starts, base, x, key, value, recept, num, den, state, vec, wo,
               gated, middle):
    i = pl.program_id(0)
    local, dist, _ = places(starts, base, i * RB, RB, T)
    mean = decay_state(
        vec, key[...], value[...], num[...], den[...], state[...], local, dist, T
    )[4]
    gated[...] = (jax.nn.sigmoid(recept[...].astype(F32)) * mean).astype(BF16)
    middle[...] = x[...].astype(F32) + dot_nn(gated[...], wo[...])


def k_feed(T, starts, base, middle, edge, vec, wg, wk, wv,
           fm, gm, sp, hid, vb, gl, xo, acc):
    M, D = middle.shape
    j = pl.program_id(0)

    @pl.when(j == 0)
    def _():
        local, dist, _ = places(starts, base, 0, M // T, T)
        gain, bias = vec[7:8], vec[8:9]
        normalized = norm_parts(middle[...])[0] * gain + bias
        edge_norm = norm_parts(edge[...])[0] * gain + bias
        previous = shifted(normalized, edge_norm, local, (dist >= 1).astype(F32), T)
        for row, out in ((9, fm), (10, gm)):
            mu = vec[row : row + 1]
            out[...] = (normalized * mu + previous * (1.0 - mu)).astype(BF16)
        acc[...] = jnp.zeros_like(acc)

    pre = dot_nn(fm[...], wk[...])
    soft = jnp.maximum(pre, 0.0) + jnp.log1p(jnp.exp(-jnp.abs(pre)))
    sp[...] = soft.astype(BF16)
    hidden = (soft * soft).astype(BF16)
    hid[...] = hidden
    acc[...] += dot_nn(hidden, wv[...])

    @pl.when(j == pl.num_programs(0) - 1)
    def _():
        gate = dot_nn(gm[...], wg[...])
        gl[...] = gate.astype(BF16)
        vb[...] = acc[...].astype(BF16)
        xo[...] = middle[...] + jax.nn.sigmoid(gate) * acc[...]


def k_feed_back(T, starts, base, grad, gl, vb, sp, middle, edge, vec, wg, wk, wv,
                gb, gg, gin, gn, first, sums, acc):
    M, D = middle.shape
    j = pl.program_id(0)

    @pl.when(j == 0)
    def _():
        g = grad[...].astype(F32)
        s = jax.nn.sigmoid(gl[...].astype(F32))
        gb[...] = (g * s).astype(BF16)
        gg[...] = (g * vb[...].astype(F32) * s * (1.0 - s)).astype(BF16)
        acc[...] = jnp.zeros_like(acc)

    soft = sp[...].astype(F32)
    gh = dot_nt(gb[...], wv[...])
    pre = (gh * (2.0 * soft * (1.0 - jnp.exp(-soft)))).astype(BF16)
    gin[...] = pre
    acc[...] += dot_nt(pre, wk[...])

    @pl.when(j == pl.num_programs(0) - 1)
    def _():
        local, dist, _ = places(starts, base, 0, M // T, T)
        joined = (dist >= 1).astype(F32)
        gain, bias = vec[7:8], vec[8:9]
        normalized = norm_parts(middle[...])[0] * gain + bias
        edge_norm = norm_parts(edge[...])[0] * gain + bias
        difference = normalized - shifted(normalized, edge_norm, local, joined, T)
        ga = acc[...]
        gc = dot_nt(gg[...], wg[...])
        sums[0:1] = colsum(ga * difference)
        sums[1:2] = colsum(gc * difference)
        sums[2:8] = jnp.zeros((6, D), F32)
        mu_a, mu_c = vec[9:10], vec[10:11]
        masked = (ga * (1.0 - mu_a) + gc * (1.0 - mu_c)) * wide(joined, D)
        gn[...] = ga * mu_a + gc * mu_c + shift_up(masked, local, T)
        first[...] = row_firsts(masked, T)


def norm_back(x, gain, gn):
    hat, rstd = norm_parts(x)
    scaled = gn * gain
    gx = rstd * (
        scaled
        - jnp.mean(scaled, axis=-1, keepdims=True)
        - hat * jnp.mean(scaled * hat, axis=-1, keepdims=True)
    )
    return gx, colsum(gn * hat), colsum(gn)


def with_edge(gn, edge, local, T):
    D = gn.shape[1]
    return gn + jnp.where(wide(local, D) == T - 1, per_row(edge, T, D), 0.0)


def k_mid_back(T, starts, base, gn, edge, middle, grad, vec, wo,
               key, value, recept, num, den, state,
               gm, gblk, gr, gkp, gvp, gno, gdo, direct, sums):
    D = middle.shape[1]
    i = pl.program_id(0)
    local, dist, _ = places(starts, base, i * RB, RB, T)
    total = with_edge(gn[...], edge[0], local, T)
    gx, ggain, gbias = norm_back(middle[...], vec[7:8], total)
    gmid = grad[...].astype(F32) + gx
    gm[...] = gmid
    gblk[...] = gmid.astype(BF16)
    ggated = dot_nt(gblk[...], wo[...])
    v = value[...]
    _, _, extra, inverse, mean = decay_state(
        vec, key[...], v, num[...], den[...], state[...], local, dist, T
    )
    s = jax.nn.sigmoid(recept[...].astype(F32))
    gr[...] = (ggated * mean * s * (1.0 - s)).astype(BF16)
    q = ggated * s * inverse
    ge = extra * q * (v - mean)
    gkp[...] = ge
    gvp[...] = q * extra
    rate = jnp.exp(vec[5:6])
    an, ad = scan_up((q, -q * mean), rate, local, dist, T)
    keep = wide(((dist >= 1) & (local >= 1)).astype(F32), D)
    gno[...] = pltpu.roll(keep * an, an.shape[0] - 1, 0)
    gdo[...] = pltpu.roll(keep * ad, ad.shape[0] - 1, 0)
    joined = wide((dist >= 1).astype(F32), D)
    ends = (row_firsts(joined * an, T), row_firsts(joined * ad, T))
    for r in range(RB):
        direct[r] = jnp.concatenate([ends[0][r : r + 1], ends[1][r : r + 1]], axis=0)

    @pl.when(i == 0)
    def _():
        sums[...] = jnp.zeros_like(sums)

    sums[0:1] += ggain
    sums[1:2] += gbias
    sums[2:3] += colsum(ge)


def k_time_back(T, starts, base, x, edge, vec, wk, wv, wr, key, value, num, den, state,
                gkp, gvp, gno, gdo, after, gr,
                gk, gv, gn, first, sums):
    D = x.shape[1]
    i = pl.program_id(0)
    local, dist, tail = places(starts, base, i * RB, RB, T)
    rate = jnp.exp(vec[5:6])
    fade = wide((dist >= local + 1).astype(F32), D) * jnp.exp(
        -wide(local.astype(F32), D) * rate
    )
    st = state[...]
    full_n = num[...] + fade * per_row(st[:, 0], T, D)
    full_d = den[...] + fade * per_row(st[:, 1], T, D)
    left = wide(tail, D) * jnp.exp(-wide((T - 1 - local).astype(F32), D) * rate)
    af = after[...]
    grad_n = gno[...] + left * per_row(af[:, 0], T, D)
    grad_d = gdo[...] + left * per_row(af[:, 1], T, D)
    weight = jnp.exp(key[...])
    gk[...] = (gkp[...] + weight * (grad_n * value[...] + grad_d)).astype(BF16)
    gv[...] = (gvp[...] + weight * grad_n).astype(BF16)
    joined = (dist >= 1).astype(F32)
    gain, bias = vec[0:1], vec[1:2]
    normalized = norm_parts(x[...].astype(F32))[0] * gain + bias
    edge_norm = norm_parts(edge[0])[0] * gain + bias
    difference = normalized - shifted(normalized, edge_norm, local, joined, T)

    @pl.when(i == 0)
    def _():
        sums[...] = jnp.zeros_like(sums)

    sums[3:4] += -rate * jnp.exp(-rate) * colsum(grad_n * full_n + grad_d * full_d)
    grad_norm = jnp.zeros(x.shape, F32)
    grad_prev = jnp.zeros(x.shape, F32)
    for row, (g, w) in enumerate(((gk, wk), (gv, wv), (gr, wr))):
        mu = vec[2 + row : 3 + row]
        g_mix = dot_nt(g[...], w[...])
        sums[row : row + 1] += colsum(g_mix * difference)
        grad_norm = grad_norm + g_mix * mu
        grad_prev = grad_prev + g_mix * (1.0 - mu)
    masked = grad_prev * wide(joined, D)
    gn[...] = grad_norm + shift_up(masked, local, T)
    first[0] = row_firsts(masked, T)


def k_norm_back(T, x, gn, edge, gmid, vec, go, sums):
    i = pl.program_id(0)
    M = x.shape[0]
    at = lax.broadcasted_iota(jnp.int32, (T, 128), 0)
    local = jnp.concatenate([at] * (M // T), axis=0)
    total = with_edge(gn[...], edge[0], local, T)
    gx, ggain, gbias = norm_back(x[...].astype(F32), vec[0:1], total)
    go[...] = gmid[...] + gx

    @pl.when(i == 0)
    def _():
        sums[...] = jnp.zeros_like(sums)

    sums[0:1] += ggain
    sums[1:2] += gbias


def smem():
    return pl.BlockSpec(memory_space=pltpu.SMEM)


def rows_spec(T, D):
    return pl.BlockSpec((RB * T, D), lambda i: (i, 0))


def col_spec(rows, width, at):
    return pl.BlockSpec((rows, width), lambda i: (0, at))


def whole_spec(shape):
    zeros = (0,) * len(shape)
    return pl.BlockSpec(shape, lambda i: zeros)


def edge_spec(D):
    return pl.BlockSpec((1, RB, D), lambda i: (i, 0, 0))


def state_spec(D):
    return pl.BlockSpec((RB, 2, D), lambda i: (i, 0, 0))


def shape(dims, kind):
    return jax.ShapeDtypeStruct(dims, kind)


def run(kernel, T, grid, in_specs, out_specs, outs, args, flops, moved, scratch=()):
    def body(*refs):
        kernel(T, *refs)

    return pl.pallas_call(
        body,
        grid=(grid,),
        in_specs=in_specs,
        out_specs=out_specs,
        out_shape=outs,
        scratch_shapes=scratch,
        compiler_params=pltpu.CompilerParams(
            dimension_semantics=("arbitrary",), vmem_limit_bytes=VMEM
        ),
        cost_estimate=pl.CostEstimate(flops=flops, bytes_accessed=moved, transcendentals=0),
        name=kernel.__name__,
    )(*args)


def time_in(T, place, x, edge, vec, mats):
    N, D = x.shape
    R = N // T
    rs = rows_spec(T, D)
    return run(
        k_time_in, T, R // RB,
        [smem(), smem(), rs, edge_spec(D), whole_spec(vec.shape)]
        + [col_spec(D, D, c) for c in range(3)],
        [rs] * 8 + [state_spec(D)],
        [shape((N, D), BF16)] * 3 + [shape((N, D), F32)] * 2 + [shape((N, D), BF16)]
        + [shape((N, D), F32)] * 2 + [shape((R, 2, D), F32)],
        (*place, x, edge.reshape(R // RB, RB, D), vec, mats, mats, mats),
        6 * N * D * D, 40 * N * D,
    )


def time_out(T, place, x, kept, state, vec, mats):
    N, D = x.shape
    R = N // T
    rs = rows_spec(T, D)
    return run(
        k_time_out, T, R // RB,
        [smem(), smem()] + [rs] * 6 + [state_spec(D), whole_spec(vec.shape), col_spec(D, D, 4)],
        [rs] * 2,
        [shape((N, D), BF16), shape((N, D), F32)],
        (*place, x, *kept, state, vec, mats),
        2 * N * D * D, 30 * N * D,
    )


def feed(T, place, middle, edge, vec, mats, fk, fv):
    N, D = middle.shape
    F = fk.shape[1]
    B = D
    whole = whole_spec((N, D))
    wide_spec = pl.BlockSpec((N, B), lambda j: (0, j))
    return run(
        k_feed, T, F // B,
        [smem(), smem(), whole, whole_spec(edge.shape), whole_spec(vec.shape), col_spec(D, D, 3),
         pl.BlockSpec((D, B), lambda j: (0, j)), pl.BlockSpec((B, D), lambda j: (j, 0))],
        [whole, whole, wide_spec, wide_spec, whole, whole, whole],
        [shape((N, D), BF16)] * 2 + [shape((N, F), BF16)] * 2 + [shape((N, D), BF16)] * 2
        + [shape((N, D), F32)],
        (*place, middle, edge, vec, mats, fk, fv),
        4 * N * D * F + 2 * N * D * D, 20 * N * D + 4 * N * F + 4 * D * F,
        [pltpu.VMEM((N, D), F32)],
    )


def feed_back(T, place, grad, gl, vb, sp, middle, edge, vec, mats, fk, fv):
    N, D = middle.shape
    F = fk.shape[1]
    B = D
    R = N // T
    whole = whole_spec((N, D))
    wide_spec = pl.BlockSpec((N, B), lambda j: (0, j))
    return run(
        k_feed_back, T, F // B,
        [smem(), smem(), whole, whole, whole, wide_spec, whole, whole_spec(edge.shape),
         whole_spec(vec.shape), col_spec(D, D, 3),
         pl.BlockSpec((D, B), lambda j: (0, j)), pl.BlockSpec((B, D), lambda j: (j, 0))],
        [whole, whole, wide_spec, whole, whole_spec((R, D)), whole_spec((8, D))],
        [shape((N, D), BF16)] * 2 + [shape((N, F), BF16), shape((N, D), F32)]
        + [shape((R, D), F32), shape((8, D), F32)],
        (*place, grad, gl, vb, sp, middle, edge, vec, mats, fk, fv),
        4 * N * D * F + 2 * N * D * D, 20 * N * D + 4 * N * F + 4 * D * F,
        [pltpu.VMEM((N, D), F32)],
    )


def mid_back(T, place, gn, edge, middle, grad, vec, mats, kept, state):
    N, D = middle.shape
    R = N // T
    rs = rows_spec(T, D)
    return run(
        k_mid_back, T, R // RB,
        [smem(), smem(), rs, edge_spec(D), rs, rs, whole_spec(vec.shape), col_spec(D, D, 4)]
        + [rs] * 5 + [state_spec(D)],
        [rs] * 7 + [state_spec(D), whole_spec((8, D))],
        [shape((N, D), F32)] + [shape((N, D), BF16)] * 2 + [shape((N, D), F32)] * 4
        + [shape((R, 2, D), F32), shape((8, D), F32)],
        (*place, gn, edge.reshape(R // RB, RB, D), middle, grad, vec, mats, *kept, state),
        2 * N * D * D, 50 * N * D,
    )


def time_back(T, place, x, edge, vec, mats, kept, state, part, after, gr):
    N, D = x.shape
    R = N // T
    rs = rows_spec(T, D)
    key, value, num, den = kept
    return run(
        k_time_back, T, R // RB,
        [smem(), smem(), rs, edge_spec(D), whole_spec(vec.shape)]
        + [col_spec(D, D, c) for c in range(3)] + [rs] * 4 + [state_spec(D)] + [rs] * 4
        + [state_spec(D), rs],
        [rs] * 3 + [edge_spec(D), whole_spec((8, D))],
        [shape((N, D), BF16)] * 2 + [shape((N, D), F32)]
        + [shape((R // RB, RB, D), F32), shape((8, D), F32)],
        (*place, x, edge.reshape(R // RB, RB, D), vec, mats, mats, mats, key, value, num, den,
         state, *part, after, gr),
        6 * N * D * D, 50 * N * D,
    )


def norm_in_back(T, x, gn, edge, gmid, vec):
    N, D = x.shape
    R = N // T
    rs = rows_spec(T, D)
    return run(
        k_norm_back, T, R // RB,
        [rs, rs, edge_spec(D), rs, whole_spec(vec.shape)],
        [rs, whole_spec((8, D))],
        [shape((N, D), F32), shape((8, D), F32)],
        (x, gn, edge.reshape(R // RB, RB, D), gmid, vec),
        0, 16 * N * D,
    )


def from_behind(block, distance):
    devices = range(lax.axis_size("seq"))
    route = [(i - distance, i) for i in devices if i - distance in devices]
    return lax.ppermute(block, "seq", route)


def chain(mine, starts, rate, T, forward):
    S, i = lax.axis_size("seq"), lax.axis_index("seq")
    all_states = lax.all_gather(mine.astype(BF16), "seq").astype(F32)
    j = jnp.arange(S, dtype=jnp.int32)

    def document(at):
        return jnp.sum((starts[None] <= at[:, None, None]).astype(jnp.int32), axis=2)

    if forward:
        lag = i - 1 - j
        same = document((j + 1) * T - 1) == document((i * T - 1)[None])
    else:
        lag = j - 1 - i
        same = document(j * T - 1) == document(((i + 1) * T - 1)[None])
    keep = (same & (lag >= 0)[:, None]).astype(F32)
    fade = jnp.exp(-(T * jnp.maximum(lag, 0)).astype(F32)[:, None] * rate[None])
    weight = keep[:, :, None, None] * fade[:, None, None, :]
    return jnp.sum(weight * all_states, axis=0)


def layer_forward(T, place, starts, x, edge, vec, weights):
    mats, fk, fv = weights
    N, D = x.shape
    R = N // T
    rate = jnp.exp(vec[5])
    mk, mv, mr, key, value, recept, num, den, last = time_in(T, place, x, edge, vec, mats)
    state = chain(last, starts, rate, T, True)
    gated, middle = time_out(T, place, x, (key, value, recept, num, den), state, vec, mats)
    edge_two = from_behind(middle.reshape(R, T, D)[:, -1], 1)
    fm, gm, sp, hid, vb, gl, out = feed(T, place, middle, edge_two, vec, mats, fk, fv)
    saved = (x, edge, mk, mv, mr, key, value, recept, num, den, state, gated, middle, edge_two,
             fm, gm, sp, hid, vb, gl)
    return out, saved


def weight_grad(left, gradient):
    return lax.dot_general(
        left, gradient, (((0,), (0,)), ((), ())), preferred_element_type=F32
    ).astype(BF16)


def layer_backward(T, place, starts, grad, saved, vec, weights):
    mats, fk, fv = weights
    (x, edge, mk, mv, mr, key, value, recept, num, den, state, gated, middle, edge_two,
     fm, gm, sp, hid, vb, gl) = saved
    rate = jnp.exp(vec[5])
    gb, gg, gin, gn, first, sums_feed = feed_back(
        T, place, grad, gl, vb, sp, middle, edge_two, vec, mats, fk, fv
    )
    d_fv = weight_grad(hid, gb)
    d_fk = weight_grad(fm, gin)
    d_gate = weight_grad(gm, gg)
    behind = from_behind(first, -1)
    gmid, gblk, gr, gkp, gvp, gno, gdo, direct, sums_mid = mid_back(
        T, place, gn, behind, middle, grad, vec, mats, (key, value, recept, num, den), state
    )
    d_out = weight_grad(gated, gblk)
    d_recept = weight_grad(mr, gr)
    after = chain(direct, starts, rate, T, False)
    gk, gv, gn_one, first_one, sums_time = time_back(
        T, place, x, edge, vec, mats, (key, value, num, den), state, (gkp, gvp, gno, gdo), after, gr
    )
    d_key = weight_grad(mk, gk)
    d_value = weight_grad(mv, gv)
    behind_one = from_behind(first_one.reshape(edge.shape), -1)
    grad_in, sums_norm = norm_in_back(T, x, gn_one, behind_one, gmid, vec)
    d_vec = jnp.concatenate(
        [sums_norm[0:2], sums_time[0:4], sums_mid[2:3], sums_mid[0:2], sums_feed[0:2]], axis=0
    )
    return grad_in, (d_key, d_value, d_recept, d_gate, d_out), d_fk, d_fv, d_vec


def vector_rates(row_total):
    slot = jnp.arange(row_total)
    return jnp.where((slot == 5) | (slot == 6), rate_time, rate_main)[:, None]


def adam_step(parameter, gradient, first_moment, second_moment, learning_rates, decay_weight):
    new_first = beta_one * first_moment + (1.0 - beta_one) * gradient
    new_second = beta_two * second_moment + (1.0 - beta_two) * gradient * gradient
    step_ratio = (
        new_first
        / (1.0 - beta_one**step_count)
        / (jnp.sqrt(new_second / (1.0 - beta_two**step_count)) + adam_epsilon)
    )
    return (learning_rates * (step_ratio + decay_weight * parameter), new_first, new_second)


AXES = ("dp", "seq")


def body(tokens, cotangent, document_starts, *rest):
    weights, means, powers = rest[:5], rest[5:10], rest[10:15]
    vectors, matrices, time_output, feed_key, feed_value = weights
    R, T, D = tokens.shape
    layers, n = vectors.shape[0], matrices.shape[2]
    base = (lax.axis_index("seq") * T).astype(jnp.int32).reshape(1)
    place = (document_starts, base)

    def gather(part):
        return lax.all_gather(part.astype(BF16), AXES, axis=0, tiled=True)

    order = (0, 1, 2, 3)
    all_vectors = gather(vectors.transpose(2, 0, 1).reshape(n, layers * vectors.shape[1]))
    all_vectors = all_vectors.astype(F32).T.reshape(layers, vectors.shape[1], D)
    vecs = [jnp.pad(all_vectors[l], ((0, 5), (0, 0))) for l in range(layers)]
    gathered = []
    for l in range(layers):
        mats = jnp.concatenate([matrices[l, j] for j in order] + [time_output[l]], axis=1)
        gathered.append((gather(mats), gather(feed_key[l]), gather(feed_value[l])))

    x = tokens.reshape(R * T, D)
    saved = []
    for l in range(layers):
        edge = from_behind(x.reshape(R, T, D)[:, -1], 1).astype(F32)
        x, kept = layer_forward(T, place, document_starts, x, edge, vecs[l], gathered[l])
        saved.append(kept)
    block_out = x.astype(BF16).reshape(R, T, D)

    grad = cotangent.reshape(R * T, D)
    grads = [None] * layers
    for l in reversed(range(layers)):
        grad, d_mats, d_fk, d_fv, d_vec = layer_backward(
            T, place, document_starts, grad, saved[l], vecs[l], gathered[l]
        )
        vec_cols = jnp.pad(d_vec.T.astype(BF16), ((0, 0), (0, 128 - d_vec.shape[0])))

        def scatter(part):
            return lax.psum_scatter(part, AXES, scatter_dimension=0, tiled=True).astype(F32)

        g_fv = scatter(d_fv)
        g_fk = scatter(d_fk)
        g_mats = scatter(jnp.concatenate(list(d_mats) + [vec_cols], axis=1))
        grads[l] = (
            g_mats[:, 5 * D : 5 * D + vectors.shape[1]].T,
            jnp.stack([g_mats[:, j * D : (j + 1) * D] for j in range(4)]),
            g_mats[:, 4 * D : 5 * D],
            g_fk,
            g_fv,
        )
    shards = tuple(jnp.stack([g[m] for g in grads]) for m in range(5))
    rates = (vector_rates(vectors.shape[1]),) + (rate_main,) * 4
    decays = (0.0,) + (weight_decay,) * 4
    new = [adam_step(*z) for z in zip(weights, shards, means, powers, rates, decays)]
    return (
        block_out,
        grad.reshape(R, T, D),
        *shards,
        *[z[0] for z in new],
        *[z[1] for z in new],
        *[z[2] for z in new],
    )


def solution(mesh):
    tokens = P("dp", "seq", None)
    group = (
        P(None, None, AXES),
        P(None, None, AXES, None),
        P(None, AXES, None),
        P(None, AXES, None),
        P(None, AXES, None),
    )
    in_specs = (tokens, tokens, P("dp", None)) + group * 3
    out_specs = (tokens, tokens) + group * 4
    return jax.shard_map(body, mesh=mesh, in_specs=in_specs, out_specs=out_specs, check_vma=False)
```

time: 2460 us -> 1280 us (0.52); the launches traced: 2420 us -> 1270 us
  other arithmetic: 792 us -> 22.4 us
  local copies, waits for them, and re-layouts: 439 us -> 55.8 us
  Pallas kernels: 0 us -> 138 us
  matrix products: 159 us -> 38.3 us
  blocking collectives: 192 us -> 101 us
  waiting for transfers between devices: 796 us -> 886 us
    reduce_scatter x4, waiting for transfers between devices: 740 us -> 420 us  [scatter(): lax.psum_scatter(part, AXES, scatter_dimension=0, tiled=True).astype(F32)]
    all_gather x4 -> x6, waiting for transfers between devices: 0.06 us -> 267 us  [gather(): return lax.all_gather(part.astype(BF16), AXES, axis=0, tiled=True)]
    squeeze x320 -> x0, local copies, waits for them, and re-layouts: 257 us -> none  [decay_sums(): lax.scan(lambda carry_state, block_item: block_step(carry_state, block_it...]
    reduce_sum x468 -> x6, other arithmetic: 196 us -> 0.9 us  [the longest x4 0.46 us: chain(): return jnp.sum(weight * all_states, axis=0)]
    dynamic_update_slice x160 -> x0, other arithmetic: 154 us -> none  [decay_sums(): lax.scan(lambda carry_state, block_item: block_step(carry_state, block_it...]
    unnamed x10 -> x12, waiting for transfers between devices: 53.5 us -> 197 us
    pallas_call x0 -> x14, Pallas kernels: none -> 138 us  [run(): pl.pallas_call(body, grid=(grid,), in_specs=in_specs, out_specs=out_specs...]
    convert_element_type x341 -> x9, other arithmetic: 130 us -> 4.92 us  [the longest x2 3.84 us: scatter(): lax.psum_scatter(part, AXES, scatter_dimension=0, tiled=True).astype(F32)]
  transfers between devices with their start and end apart: 17 -> 19, of which waited for: 8 -> 14; matrix products, arithmetic and copies ran while one was open for 16% -> 6% of each run, Pallas kernels for 0% -> 3%
where the time goes in v1:
time: 1280 us; the launch traced here: 1270 us
  waiting for transfers between devices  886 us (69%)
  Pallas kernels  138 us (11%)
  blocking collectives  101 us (8%)
  local copies, waits for them, and re-layouts  55.8 us (4%)
  matrix products  38.3 us (3%)
  other arithmetic  22.4 us (2%)
  starting transfers between devices  16.4 us (1%)
  between operations  15.6 us (1%)
    reduce_scatter x4, waiting for transfers between devices, scatter(): lax.psum_scatter(part, AXES, scatter_dimension=0, tiled=True).astype(F32)  420 us
    all_gather x6, waiting for transfers between devices, gather(): return lax.all_gather(part.astype(BF16), AXES, axis=0, tiled=True)  267 us
    unnamed x12, waiting for transfers between devices  197 us
    pallas_call x14, Pallas kernels, run(): pl.pallas_call(body, grid=(grid,), in_specs=in_specs, out_specs=out_specs...  138 us
    all_gather x4, blocking collectives, chain(): all_states = lax.all_gather(mine.astype(BF16), 'seq').astype(F32)  57.2 us
    all_gather x1, blocking collectives, gather(): return lax.all_gather(part.astype(BF16), AXES, axis=0, tiled=True)  43.7 us
    unnamed x198, local copies, waits for them, and re-layouts  39.5 us
    dot_general x14, matrix products, weight_grad(): lax.dot_general(left, gradient, (((0,), (0,)), ((), ())), preferred_eleme...  38.3 us
  transfers between devices with their start and end apart: 19, of which 14 were waited for; matrix products, arithmetic and copies ran while one was open for 6% of the time, Pallas kernels for 3%

profile of v1, /device:TPU:0, one launch (start us, length us, event | category | flops | bytes accessed | tf_op | source)
XLA Modules:
  0.0 1273.9 jit_solution(2223783459990846879)
XLA Ops:
  17.4 43.7 %all_gather.45 = bf16[768,22]{1,0:T(8,128)(2,1)S(1)} all-gather(bf16[24,22]{1,0:T(8,128)(2,1)S(1)} %reshape.375), channel_id=1, replica_groups=mesh['dp'=4,'seq'=8] {'dp','seq'}, dimensions={0}, use_global_device_ids=true | all-gather | bytes 34848 | tf_op jit(solution)/shard_map/all_gather | solution.py:632
  62.9 19.4 %all-gather.15.cloned.1.call-done.refs_5_.refs_6_.refs_7_.refs_10_.refs_9_ = bf16[768,3840]{1,0:T(8,128)(2,1)} async-done(((bf16[24,3840]{1,0:T(8,128)(2,1)}), bf16[768,3840]{1,0:T(8,128)(2,1)}) %all-gather.15.cloned.1.call-update) | async-done | bytes 5898256 | tf_op jit(solution)/shard_map/all_gather | solution.py:632
  82.3 9.1 k_time_in.2
  91.5 14.1 %all-gather = bf16[32,2,768]{2,1,0:T(2,128)(2,1)S(1)} all-gather(bf16[4,2,768]{2,1,0:T(2,128)(2,1)S(1)} %convert_element_type.179), channel_id=2, replica_groups=mesh['dp'=4,'seq'=8] {'seq'}, dimensions={0}, use_global_device_ids=true | all-gather | bytes 110592 | tf_op jit(solution)/shard_map/all_gather | solution.py:534
  105.7 4.4 k_time_out.2
  114.4 34.2 %all-gather.19.cloned.1.call-done = bf16[1,768,3072]{2,1,0:T(8,128)(2,1)} async-done(((bf16[1,24,3072]{2,1,0:T(8,128)(2,1)}), bf16[1,768,3072]{2,1,0:T(8,128)(2,1)}) %all-gather.19.cloned.1.call-update) | async-done | bytes 4718608 | tf_op jit(solution)/shard_map/all_gather | solution.py:632
  148.7 66.1 %all-gather.21.cloned.1.call-done = bf16[1,3072,768]{2,1,0:T(8,128)(2,1)} async-done(((bf16[1,96,768]{2,1,0:T(8,128)(2,1)}), bf16[1,3072,768]{2,1,0:T(8,128)(2,1)}) %all-gather.21.cloned.1.call-update) | async-done | bytes 4718608 | tf_op jit(solution)/shard_map/all_gather | solution.py:632
  214.8 14.5 %k_feed.2 = (bf16[512,768]{1,0:T(8,128)(2,1)S(1)}, bf16[512,768]{1,0:T(8,128)(2,1)S(1)}, bf16[512,3072]{1,0:T(8,128)(2,1)}, bf16[512,3072]{1,0:T(8,128)(2,1)}, b...) custom-call(s32[4,8]{1,0:T(4,128)S(1)} %copy-done.32, s32[1]{0:T(128)} %bitcast.refs_1_, ...), custom_call_target="tpu_custom_call" | custom-call | flops 5435817984 | bytes 23592960 | tf_op jit(solution)/shard_map/k_feed/pallas_call | solution.py:392
  235.0 49.8 %all-gather.17.cloned.1.call-done.refs_5_.refs_6_.refs_7_.refs_10_.refs_9_ = bf16[768,3840]{1,0:T(8,128)(2,1)} async-done(((bf16[24,3840]{1,0:T(8,128)(2,1)}), bf16[768,3840]{1,0:T(8,128)(2,1)}) %all-gather.17.cloned.1.call-update) | async-done | bytes 5898256 | tf_op jit(solution)/shard_map/all_gather | solution.py:632
  284.8 9.5 k_time_in.3
  296.4 14.0 %all-gather.3 = bf16[32,2,768]{2,1,0:T(2,128)(2,1)S(1)} all-gather(bf16[4,2,768]{2,1,0:T(2,128)(2,1)S(1)} %convert_element_type.183), channel_id=5, replica_groups=mesh['dp'=4,'seq'=8] {'seq'}, dimensions={0}, use_global_device_ids=true | all-gather | bytes 110592 | tf_op jit(solution)/shard_map/all_gather | solution.py:534
  312.0 4.8 k_time_out.3
  320.0 31.2 %all-gather.23.cloned.1.call-done = bf16[1,768,3072]{2,1,0:T(8,128)(2,1)} async-done(((bf16[1,24,3072]{2,1,0:T(8,128)(2,1)}), bf16[1,768,3072]{2,1,0:T(8,128)(2,1)}) %all-gather.23.cloned.1.call-update) | async-done | bytes 4718608 | tf_op jit(solution)/shard_map/all_gather | solution.py:632
  351.2 66.0 %all-gather.25.cloned.1.call-done = bf16[1,3072,768]{2,1,0:T(8,128)(2,1)} async-done(((bf16[1,96,768]{2,1,0:T(8,128)(2,1)}), bf16[1,3072,768]{2,1,0:T(8,128)(2,1)}) %all-gather.25.cloned.1.call-update) | async-done | bytes 4718608 | tf_op jit(solution)/shard_map/all_gather | solution.py:632
  417.2 14.6 %k_feed.3 = (bf16[512,768]{1,0:T(8,128)(2,1)S(1)}, bf16[512,768]{1,0:T(8,128)(2,1)S(1)}, bf16[512,3072]{1,0:T(8,128)(2,1)}, bf16[512,3072]{1,0:T(8,128)(2,1)}, b...) custom-call(s32[4,8]{1,0:T(4,128)S(1)} %copy-done.32, s32[1]{0:T(128)} %bitcast.refs_1_, ...), custom_call_target="tpu_custom_call" | custom-call | flops 5435817984 | bytes 23592960 | tf_op jit(solution)/shard_map/k_feed/pallas_call | solution.py:392
  433.8 14.3 %k_feed_back.2 = (bf16[512,768]{1,0:T(8,128)(2,1)S(1)}, bf16[512,768]{1,0:T(8,128)(2,1)S(1)}, bf16[512,3072]{1,0:T(8,128)(2,1)}, f32[512,768]{1,0:T(8,128)S(1)},...) custom-call(s32[4,8]{1,0:T(4,128)S(1)} %copy-done.32, s32[1]{0:T(128)} %bitcast.refs_1_, bf16[512,768]{1,0:T(8,128)(2,1)S(1)} %bitcast.153, ...), custom_call_target="tpu_custom_call" | custom-call | flops 5435817984 | bytes 23592960 | tf_op jit(solution)/shard_map/k_feed_back/pallas_call | solution.py:392
  454.2 12.2 k_mid_back.2
  467.7 15.0 %all-gather.6 = bf16[32,2,768]{2,1,0:T(2,128)(2,1)S(1)} all-gather(bf16[4,2,768]{2,1,0:T(2,128)(2,1)S(1)} %convert_element_type.192), channel_id=8, replica_groups=mesh['dp'=4,'seq'=8] {'seq'}, dimensions={0}, use_global_device_ids=true | all-gather | bytes 110592 | tf_op jit(solution)/shard_map/all_gather | solution.py:534
  482.8 11.7 k_time_back.2
  509.9 14.3 %k_feed_back.3 = (bf16[512,768]{1,0:T(8,128)(2,1)S(1)}, bf16[512,768]{1,0:T(8,128)(2,1)S(1)}, bf16[512,3072]{1,0:T(8,128)(2,1)}, f32[512,768]{1,0:T(8,128)S(1)},...) custom-call(s32[4,8]{1,0:T(4,128)S(1)} %copy-done.32, s32[1]{0:T(128)} %bitcast.refs_1_, f32[512,768]{1,0:T(8,128)} %copy-done.9, ...), custom_call_target="tpu_custom_call" | custom-call | flops 5435817984 | bytes 23592960 | tf_op jit(solution)/shard_map/k_feed_back/pallas_call | solution.py:392
  530.9 12.4 k_mid_back.3
  544.5 14.2 %all-gather.7 = bf16[32,2,768]{2,1,0:T(2,128)(2,1)S(1)} all-gather(bf16[4,2,768]{2,1,0:T(2,128)(2,1)S(1)} %convert_element_type.194), channel_id=9, replica_groups=mesh['dp'=4,'seq'=8] {'seq'}, dimensions={0}, use_global_device_ids=true | all-gather | bytes 110592 | tf_op jit(solution)/shard_map/all_gather | solution.py:534
  558.8 11.7 k_time_back.3
  589.4 6.2 convolution_convert_fusion.2
  596.6 6.1 convolution_convert_fusion.3
  603.9 6.7 convolution_convert_fusion
  611.8 6.7 convolution_convert_fusion.1
  620.9 195.1 %all-reduce.8.cloned.1.call-done = (bf16[768,3968]{0,1:T(8,128)(2,1)}, bf16[768,3968]{0,1:T(8,128)(2,1)}) async-done(((bf16[768,3968]{0,1:T(8,128)(2,1)}, bf16[768,3968]{0,1:T(8,128)(2,1)}), (bf16[768,3968]{0,1:T(8,128)(2,1)}, bf16[768,3968]{0,1:T(8,128)(2,1)})) %all-reduce.8.cloned.1.call-update) | async-done | bytes 12189712
  841.4 87.4 %reduce-scatter.9.cloned.1.call-done = bf16[24,3072]{1,0:T(8,128)(2,1)} async-done(((bf16[768,3072]{1,0:T(8,128)(2,1)}), bf16[24,3072]{1,0:T(8,128)(2,1)}) %reduce-scatter.9.cloned.1.call-update) | async-done | bytes 147472 | tf_op jit(solution)/shard_map/reduce_scatter | solution.py:660
  928.8 111.6 %reduce-scatter.7.cloned.1.call-done = bf16[24,3072]{1,0:T(8,128)(2,1)} async-done(((bf16[768,3072]{1,0:T(8,128)(2,1)}), bf16[24,3072]{1,0:T(8,128)(2,1)}) %reduce-scatter.7.cloned.1.call-update) | async-done | bytes 147472 | tf_op jit(solution)/shard_map/reduce_scatter | solution.py:660
  1042.9 109.9 %reduce-scatter.13.cloned.1.call-done = bf16[96,768]{1,0:T(8,128)(2,1)} async-done(((bf16[3072,768]{1,0:T(8,128)(2,1)}), bf16[96,768]{1,0:T(8,128)(2,1)}) %reduce-scatter.13.cloned.1.call-update) | async-done | bytes 147472 | tf_op jit(solution)/shard_map/reduce_scatter | solution.py:660
  1152.8 111.6 %reduce-scatter.11.cloned.1.call-done = bf16[96,768]{1,0:T(8,128)(2,1)} async-done(((bf16[3072,768]{1,0:T(8,128)(2,1)}), bf16[96,768]{1,0:T(8,128)(2,1)}) %reduce-scatter.11.cloned.1.call-update) | async-done | bytes 147472 | tf_op jit(solution)/shard_map/reduce_scatter | solution.py:660
  (338 shorter events, 115.9 us)
Async XLA Ops:
  7.2 54.1 %copy-start.32 = (s32[4,8]{1,0:T(4,128)S(1)}, s32[4,8]{1,0:T(4,128)}, u32[]{:S(2)}) copy-start(s32[4,8]{1,0:T(4,128)} %refs_0_.23) | copy-start | bytes 388
  7.2 75.0 %all-gather.15.cloned.1.call-start = ((), (), s32[]{:S(2)}) async-start(), calls=%async_computation.4 | async-start | bytes 6082560 | tf_op jit(solution)/shard_map/all_gather | solution.py:632
  8.5 54.3 %copy-start.92 = (pred[16]{0:T(512)(128)(4,1)S(1)}, pred[16]{0:T(512)(128)(4,1)}, u32[]{:S(2)}) copy-start(pred[16]{0:T(512)(128)(4,1)} %constant.22.clone.1) | copy-start | bytes 52
  10.2 138.5 %all-gather.19.cloned.1.call-start = ((), (), s32[]{:S(2)}) async-start(), calls=%async_computation.10 | async-start | bytes 4866048 | tf_op jit(solution)/shard_map/all_gather | solution.py:632
  12.1 202.7 %all-gather.21.cloned.1.call-start = ((), (), s32[]{:S(2)}) async-start(), calls=%async_computation.11 | async-start | bytes 4866048 | tf_op jit(solution)/shard_map/all_gather | solution.py:632
  13.0 271.9 %all-gather.17.cloned.1.call-start = ((), (), s32[]{:S(2)}) async-start(), calls=%async_computation.5 | async-start | bytes 6082560 | tf_op jit(solution)/shard_map/all_gather | solution.py:632
  13.5 337.7 %all-gather.23.cloned.1.call-start = ((), (), s32[]{:S(2)}) async-start(), calls=%async_computation.12 | async-start | bytes 4866048 | tf_op jit(solution)/shard_map/all_gather | solution.py:632
  14.1 403.0 %all-gather.25.cloned.1.call-start = ((), (), s32[]{:S(2)}) async-start(), calls=%async_computation.13 | async-start | bytes 4866048 | tf_op jit(solution)/shard_map/all_gather | solution.py:632
  14.7 801.3 %all-reduce.8.cloned.1.call-start = ((), (), s32[]{:S(2)}) async-start(), calls=%async_computation.14 | async-start | bytes 24379392
  14.8 48.1 %collective-permute-start = (bf16[4,768]{1,0:T(4,128)(2,1)S(1)}, bf16[4,768]{1,0:T(4,128)(2,1)S(1)}, u32[]{:S(2)}, u32[]{:S(2)}) collective-permute-start(bf16[4,768]{1,0:T(4,128)(2,1)S(1)} %bitcast.177), channel_id=1, source_target_pairs={{0,1},{1,2},{2,3},{3,4},{4,5},{5,6},{6,7},{8,9},{9,10},{10,11},{11... | collective-permute-start | bytes 18440 | tf_op jit(solution)/shard_map/ppermute | solution.py:529
  112.2 102.6 %collective-permute-start.1 = (f32[4,768]{1,0:T(4,128)S(1)}, f32[4,768]{1,0:T(4,128)S(1)}, u32[]{:S(2)}, u32[]{:S(2)}) collective-permute-start(f32[4,768]{1,0:T(4,128)S(1)} %bitcast.175), channel_id=1, source_target_pairs={{0,1},{1,2},{2,3},{3,4},{4,5},{5,6},{6,7},{8,9},{9,10},{10,11},{11... | collective-permute-start | bytes 36872 | tf_op jit(solution)/shard_map/ppermute | solution.py:529
  232.0 62.4 %copy-start.26 = (bf16[512,768]{1,0:T(8,128)(2,1)}, bf16[512,768]{1,0:T(8,128)(2,1)S(1)}, u32[]{:S(2)}) copy-start(bf16[512,768]{1,0:T(8,128)(2,1)S(1)} %get-tuple-element.133.refs_3_) | copy-start | bytes 2359300
  232.0 3.0 collective-permute-start.2
  317.6 99.5 %copy-start.7 = (f32[512,768]{1,0:T(8,128)}, f32[512,768]{1,0:T(8,128)S(1)}, u32[]{:S(2)}) copy-start(f32[512,768]{1,0:T(8,128)S(1)} %get-tuple-element.116.refs_2_.refs_6_.refs_4_) | copy-start | bytes 4718596
  317.7 99.5 %collective-permute-start.3 = (f32[4,768]{1,0:T(4,128)S(1)}, f32[4,768]{1,0:T(4,128)S(1)}, u32[]{:S(2)}, u32[]{:S(2)}) collective-permute-start(f32[4,768]{1,0:T(4,128)S(1)} %bitcast.174), channel_id=1, source_target_pairs={{0,1},{1,2},{2,3},{3,4},{4,5},{5,6},{6,7},{8,9},{9,10},{10,11},{11... | collective-permute-start | bytes 36872 | tf_op jit(solution)/shard_map/ppermute | solution.py:529
  451.1 3.1 collective-permute-start.4
  496.3 10.0 collective-permute-start.5
  527.2 3.7 collective-permute-start.6
  572.6 11.3 collective-permute-start.7
  588.2 340.5 %reduce-scatter.9.cloned.1.call-start = ((), (), s32[]{:S(2)}) async-start(), calls=%async_computation.7 | async-start | bytes 4866048 | tf_op jit(solution)/shard_map/reduce_scatter | solution.py:660
  595.5 444.9 %reduce-scatter.7.cloned.1.call-start = ((), (), s32[]{:S(2)}) async-start(), calls=%async_computation.6 | async-start | bytes 4866048 | tf_op jit(solution)/shard_map/reduce_scatter | solution.py:660
  602.8 550.0 %reduce-scatter.13.cloned.1.call-start = ((), (), s32[]{:S(2)}) async-start(), calls=%async_computation.9 | async-start | bytes 4866048 | tf_op jit(solution)/shard_map/reduce_scatter | solution.py:660
  610.7 653.7 %reduce-scatter.11.cloned.1.call-start = ((), (), s32[]{:S(2)}) async-start(), calls=%async_computation.8 | async-start | bytes 4866048 | tf_op jit(solution)/shard_map/reduce_scatter | solution.py:660
  620.9 199.0 %copy-start.89 = (f32[2,11,24]{2,0,1:T(2,128)S(1)}, f32[2,11,24]{2,0,1:T(2,128)}, u32[]{:S(2)}) copy-start(f32[2,11,24]{2,0,1:T(2,128)} %param.21) | copy-start | bytes 6340
  620.9 199.0 %copy-start.90 = (f32[2,11,24]{2,0,1:T(2,128)S(1)}, f32[2,11,24]{2,0,1:T(2,128)}, u32[]{:S(2)}) copy-start(f32[2,11,24]{2,0,1:T(2,128)} %param.26) | copy-start | bytes 6340
  620.9 199.0 %copy-start.91 = (f32[2,11,24]{2,0,1:T(2,128)S(1)}, f32[2,11,24]{2,0,1:T(2,128)}, u32[]{:S(2)}) copy-start(f32[2,11,24]{2,0,1:T(2,128)} %param.31) | copy-start | bytes 6340
  835.7 204.7 %copy-start.75 = (f32[2,24,3072]{2,1,0:T(8,128)S(1)}, f32[2,24,3072]{2,1,0:T(8,128)}, u32[]{:S(2)}) copy-start(f32[2,24,3072]{2,1,0:T(8,128)} %param.24) | copy-start | bytes 1769476
  835.8 204.7 %copy-start.79 = (f32[2,24,3072]{2,1,0:T(8,128)S(1)}, f32[2,24,3072]{2,1,0:T(8,128)}, u32[]{:S(2)}) copy-start(f32[2,24,3072]{2,1,0:T(8,128)} %param.29) | copy-start | bytes 1769476
  835.8 204.7 %copy-start.80 = (f32[2,24,3072]{2,1,0:T(8,128)S(1)}, f32[2,24,3072]{2,1,0:T(8,128)}, u32[]{:S(2)}) copy-start(f32[2,24,3072]{2,1,0:T(8,128)} %param.34) | copy-start | bytes 1769476
  841.4 423.0 %copy-start.77 = (f32[2,96,768]{2,1,0:T(8,128)S(1)}, f32[2,96,768]{2,1,0:T(8,128)}, u32[]{:S(2)}) copy-start(f32[2,96,768]{2,1,0:T(8,128)} %param.25) | copy-start | bytes 1769476
  841.4 423.0 %copy-start.81 = (f32[2,96,768]{2,1,0:T(8,128)S(1)}, f32[2,96,768]{2,1,0:T(8,128)}, u32[]{:S(2)}) copy-start(f32[2,96,768]{2,1,0:T(8,128)} %param.30) | copy-start | bytes 1769476
  841.4 423.0 %copy-start.82 = (f32[2,96,768]{2,1,0:T(8,128)S(1)}, f32[2,96,768]{2,1,0:T(8,128)}, u32[]{:S(2)}) copy-start(f32[2,96,768]{2,1,0:T(8,128)} %param.35) | copy-start | bytes 1769476
  (80 other events, 650.9 us)
Sparse Core Ops, SparseCore 0:
  11.7 70.5 all-gather.14
  85.8 62.7 all-gather.18
  152.3 62.4 all-gather.20
  218.2 66.5 all-gather.16
  288.3 62.8 all-gather.22
  354.6 62.4 all-gather.24
  588.4 227.6 all-reduce.7
  822.4 106.3 reduce-scatter.8
  934.3 106.0 reduce-scatter.6
  1046.6 106.1 reduce-scatter.12
  1158.3 106.0 reduce-scatter.10

commit v2 on v1

--- a/solution.py
+++ b/solution.py
@@ -3,7 +3,7 @@
 from jax import lax
 from jax.experimental import pallas as pl
 from jax.experimental.pallas import tpu as pltpu
-from jax.sharding import PartitionSpec as P
+from jax.sharding import Mesh, PartitionSpec as P
 
 norm_epsilon = 1e-05
 beta_one = 0.9
@@ -15,6 +15,7 @@
 weight_decay = 0.1
 
 RB = 2
+COST = 20
 VMEM = 48 * 1024 * 1024
 F32, BF16 = jnp.float32, jnp.bfloat16
 
@@ -114,10 +115,54 @@
     )
 
 
-def k_time_in(T, starts, base, x, edge, vec, wk, wv, wr,
-              mk, mv, mr, ko, vo, ro, no, do, last):
+def piece_copies(base, pieces, item, target, sems, at):
+    count, first_in_block, first, width, rows, bits = item
+    columns = pl.ds(first, width)
+    if count == 1:
+        return [(0, pltpu.make_async_copy(pieces[0].at[:, pl.ds(first_in_block, width)], target, sems.at[at]))]
+    block, one, two, other_one, other_two = pieces
+    d, c = base[1], base[2]
+    copies = []
+    for half, first_ref, second_ref in ((c, one, two), (1 - c, other_one, other_two)):
+        start = pl.multiple_of(half * rows, rows)
+        for source, m in (
+            (block.at[pl.ds(start, rows), pl.ds(first_in_block, width)], 0),
+            (first_ref.at[:, columns], bits[0]),
+            (second_ref.at[0, :, columns], bits[1]),
+            (second_ref.at[1, :, columns], bits[0] | bits[1]),
+        ):
+            row = pl.multiple_of(((d ^ m) * 2 + half) * rows, rows)
+            copies.append(
+                (m, pltpu.make_async_copy(
+                    source, target.at[pl.ds(row, rows)], sems.at[at + len(copies)]
+                ))
+            )
+    return copies
+
+
+def split_refs(items, refs):
+    groups, at = [], 0
+    for count in items:
+        groups.append(refs[at : at + count])
+        at += count
+    return groups, refs[at:]
+
+
+def k_time_in(items, T, starts, base, x, edge, vec, *refs):
+    (pieces,), (mk, mv, mr, ko, vo, ro, no, do, last, w, sems) = split_refs([items[0][0]], refs)
     D = x.shape[1]
     i = pl.program_id(0)
+    copies = [
+        copy
+        for s, item in enumerate(items)
+        for copy in piece_copies(base, pieces, item, w.at[s], sems, 8 * s)
+    ]
+
+    @pl.when(i == 0)
+    def _():
+        for _, copy in copies:
+            copy.start()
+
     local, dist, _ = places(starts, base, i * RB, RB, T)
     joined = (dist >= 1).astype(F32)
     gain, bias = vec[0:1], vec[1:2]
@@ -127,11 +172,17 @@
     for j, out in ((2, mk), (3, mv), (4, mr)):
         mu = vec[j : j + 1]
         out[...] = (normalized * mu + previous * (1.0 - mu)).astype(BF16)
-    key = dot_nn(mk[...], wk[...])
-    value = dot_nn(mv[...], wv[...])
+
+    @pl.when(i == 0)
+    def _():
+        for _, copy in copies:
+            copy.wait()
+
+    key = dot_nn(mk[...], w[0])
+    value = dot_nn(mv[...], w[1])
     ko[...] = key
     vo[...] = value
-    ro[...] = dot_nn(mr[...], wr[...]).astype(ro.dtype)
+    ro[...] = dot_nn(mr[...], w[2]).astype(ro.dtype)
     rate = jnp.exp(vec[5:6])
     weight = jnp.exp(key)
     num, den = scan_down((weight * value, weight), rate, local, dist, T)
@@ -157,24 +208,73 @@
     return full_n, full_d, extra, inverse, mean
 
 
-def k_time_out(T, starts, base, x, key, value, recept, num, den, state, vec, wo,
-               gated, middle):
+def k_time_out(items, T, starts, base, x, key, value, recept, num, den, state, vec, *refs):
+    (pieces,), (gated, middle, w, sems) = split_refs([items[0][0]], refs)
     i = pl.program_id(0)
+    copies = piece_copies(base, pieces, items[0], w, sems, 0)
+
+    @pl.when(i == 0)
+    def _():
+        for _, copy in copies:
+            copy.start()
+
     local, dist, _ = places(starts, base, i * RB, RB, T)
     mean = decay_state(
         vec, key[...], value[...], num[...], den[...], state[...], local, dist, T
     )[4]
     gated[...] = (jax.nn.sigmoid(recept[...].astype(F32)) * mean).astype(BF16)
-    middle[...] = x[...].astype(F32) + dot_nn(gated[...], wo[...])
-
-
-def k_feed(T, starts, base, middle, edge, vec, wg, wk, wv,
-           fm, gm, sp, hid, vb, gl, xo, acc):
+
+    @pl.when(i == 0)
+    def _():
+        for _, copy in copies:
+            copy.wait()
+
+    middle[...] = x[...].astype(F32) + dot_nn(gated[...], w[...])
+
+
+def feed_copies(items, base, gate_pieces, key_pieces, value_pieces, wg, wk, wv, sems):
+    gate = piece_copies(base, gate_pieces, items[0], wg, sems, 0)
+    keys = [
+        piece_copies(base, key_pieces, item, wk.at[b], sems, 8 + 8 * b)
+        for b, item in enumerate(items[1:-1])
+    ]
+    values = piece_copies(base, value_pieces, items[-1], wv, sems, 8 * len(items) - 8)
+    return gate, keys, values
+
+
+def feed_start(copies):
+    gate, keys, values = copies
+    for _, copy in keys[0] + values + [z for block in keys[1:] for z in block] + gate:
+        copy.start()
+
+
+def feed_wait(copies, base, j):
+    gate, keys, values = copies
+    for b, block in enumerate(keys):
+
+        @pl.when(j == b)
+        def _():
+            for _, copy in block:
+                copy.wait()
+
+    whole = len(values) == 1
+    for m, copy in values:
+
+        @pl.when((j == 0) if whole else ((base[1] ^ m) == j))
+        def _():
+            copy.wait()
+
+
+def k_feed(items, T, starts, base, middle, edge, vec, *refs):
+    counts = [items[0][0], items[1][0], items[-1][0]]
+    pieces, (fm, gm, sp, hid, vb, gl, xo, acc, wg, wk, wv, sems) = split_refs(counts, refs)
     M, D = middle.shape
     j = pl.program_id(0)
+    copies = feed_copies(items, base, *pieces, wg, wk, wv, sems)
 
     @pl.when(j == 0)
     def _():
+        feed_start(copies)
         local, dist, _ = places(starts, base, 0, M // T, T)
         gain, bias = vec[7:8], vec[8:9]
         normalized = norm_parts(middle[...])[0] * gain + bias
@@ -185,39 +285,47 @@
             out[...] = (normalized * mu + previous * (1.0 - mu)).astype(BF16)
         acc[...] = jnp.zeros_like(acc)
 
-    pre = dot_nn(fm[...], wk[...])
+    feed_wait(copies, base, j)
+    block = pl.ds(pl.multiple_of(j * D, D), D)
+    pre = dot_nn(fm[...], wk[j])
     soft = jnp.maximum(pre, 0.0) + jnp.log1p(jnp.exp(-jnp.abs(pre)))
     sp[...] = soft.astype(BF16)
     hidden = (soft * soft).astype(BF16)
     hid[...] = hidden
-    acc[...] += dot_nn(hidden, wv[...])
+    acc[...] += dot_nn(hidden, wv[block])
 
     @pl.when(j == pl.num_programs(0) - 1)
     def _():
+        for _, copy in copies[0]:
+            copy.wait()
         gate = dot_nn(gm[...], wg[...])
         gl[...] = gate.astype(BF16)
         vb[...] = acc[...].astype(BF16)
         xo[...] = middle[...] + jax.nn.sigmoid(gate) * acc[...]
 
 
-def k_feed_back(T, starts, base, grad, gl, vb, sp, middle, edge, vec, wg, wk, wv,
-                gb, gg, gin, gn, first, sums, acc):
+def k_feed_back(items, T, starts, base, grad, gl, vb, sp, middle, edge, vec, *refs):
+    counts = [items[0][0], items[1][0], items[-1][0]]
+    pieces, (gb, gg, gin, gn, first, sums, acc, wg, wk, wv, sems) = split_refs(counts, refs)
     M, D = middle.shape
     j = pl.program_id(0)
+    copies = feed_copies(items, base, *pieces, wg, wk, wv, sems)
 
     @pl.when(j == 0)
     def _():
+        feed_start(copies)
         g = grad[...].astype(F32)
         s = jax.nn.sigmoid(gl[...].astype(F32))
         gb[...] = (g * s).astype(BF16)
         gg[...] = (g * vb[...].astype(F32) * s * (1.0 - s)).astype(BF16)
         acc[...] = jnp.zeros_like(acc)
 
+    feed_wait(copies, base, j)
     soft = sp[...].astype(F32)
-    gh = dot_nt(gb[...], wv[...])
+    gh = dot_nt(gb[...], wv[pl.ds(pl.multiple_of(j * D, D), D)])
     pre = (gh * (2.0 * soft * (1.0 - jnp.exp(-soft)))).astype(BF16)
     gin[...] = pre
-    acc[...] += dot_nt(pre, wk[...])
+    acc[...] += dot_nt(pre, wk[j])
 
     @pl.when(j == pl.num_programs(0) - 1)
     def _():
@@ -228,6 +336,8 @@
         edge_norm = norm_parts(edge[...])[0] * gain + bias
         difference = normalized - shifted(normalized, edge_norm, local, joined, T)
         ga = acc[...]
+        for _, copy in copies[0]:
+            copy.wait()
         gc = dot_nt(gg[...], wg[...])
         sums[0:1] = colsum(ga * difference)
         sums[1:2] = colsum(gc * difference)
@@ -254,18 +364,33 @@
     return gn + jnp.where(wide(local, D) == T - 1, per_row(edge, T, D), 0.0)
 
 
-def k_mid_back(T, starts, base, gn, edge, middle, grad, vec, wo,
-               key, value, recept, num, den, state,
-               gm, gblk, gr, gkp, gvp, gno, gdo, direct, sums):
+def k_mid_back(items, T, starts, base, gn, edge, middle, grad, vec,
+               key, value, recept, num, den, state, *refs):
+    (pieces,), (gm, gblk, gr, gkp, gvp, gno, gdo, direct, sums, w, sems) = split_refs(
+        [items[0][0]], refs
+    )
     D = middle.shape[1]
     i = pl.program_id(0)
+    copies = piece_copies(base, pieces, items[0], w, sems, 0)
+
+    @pl.when(i == 0)
+    def _():
+        for _, copy in copies:
+            copy.start()
+
     local, dist, _ = places(starts, base, i * RB, RB, T)
     total = with_edge(gn[...], edge[0], local, T)
     gx, ggain, gbias = norm_back(middle[...], vec[7:8], total)
     gmid = grad[...].astype(F32) + gx
     gm[...] = gmid
     gblk[...] = gmid.astype(BF16)
-    ggated = dot_nt(gblk[...], wo[...])
+
+    @pl.when(i == 0)
+    def _():
+        for _, copy in copies:
+            copy.wait()
+
+    ggated = dot_nt(gblk[...], w[...])
     v = value[...]
     _, _, extra, inverse, mean = decay_state(
         vec, key[...], v, num[...], den[...], state[...], local, dist, T
@@ -295,11 +420,22 @@
     sums[2:3] += colsum(ge)
 
 
-def k_time_back(T, starts, base, x, edge, vec, wk, wv, wr, key, value, num, den, state,
-                gkp, gvp, gno, gdo, after, gr,
-                gk, gv, gn, first, sums):
+def k_time_back(items, T, starts, base, x, edge, vec, key, value, num, den, state,
+                gkp, gvp, gno, gdo, after, gr, *refs):
+    (pieces,), (gk, gv, gn, first, sums, w, sems) = split_refs([items[0][0]], refs)
     D = x.shape[1]
     i = pl.program_id(0)
+    copies = [
+        copy
+        for s, item in enumerate(items)
+        for copy in piece_copies(base, pieces, item, w.at[s], sems, 8 * s)
+    ]
+
+    @pl.when(i == 0)
+    def _():
+        for _, copy in copies:
+            copy.start()
+
     local, dist, tail = places(starts, base, i * RB, RB, T)
     rate = jnp.exp(vec[5:6])
     fade = wide((dist >= local + 1).astype(F32), D) * jnp.exp(
@@ -328,9 +464,15 @@
     sums[3:4] += -rate * jnp.exp(-rate) * colsum(grad_n * full_n + grad_d * full_d)
     grad_norm = jnp.zeros(x.shape, F32)
     grad_prev = jnp.zeros(x.shape, F32)
-    for row, (g, w) in enumerate(((gk, wk), (gv, wv), (gr, wr))):
+
+    @pl.when(i == 0)
+    def _():
+        for _, copy in copies:
+            copy.wait()
+
+    for row, g in enumerate((gk, gv, gr)):
         mu = vec[2 + row : 3 + row]
-        g_mix = dot_nt(g[...], w[...])
+        g_mix = dot_nt(g[...], w[row])
         sums[row : row + 1] += colsum(g_mix * difference)
         grad_norm = grad_norm + g_mix * mu
         grad_prev = grad_prev + g_mix * (1.0 - mu)
@@ -356,6 +498,35 @@
     sums[1:2] += gbias
 
 
+def k_weight_grad(count, T, *refs):
+    lefts, grads, (out, left, grad, sems) = refs[:count], refs[count : 2 * count], refs[2 * count :]
+    i = pl.program_id(0)
+    pairs = [
+        [
+            pltpu.make_async_copy(source, target.at[n], sems.at[2 * n + side])
+            for side, (source, target) in enumerate(((lefts[n], left), (grads[n], grad)))
+        ]
+        for n in range(count)
+    ]
+
+    @pl.when(i == 0)
+    def _():
+        for pair in pairs:
+            for copy in pair:
+                copy.start()
+
+    for n, pair in enumerate(pairs):
+
+        @pl.when(i == n)
+        def _():
+            for copy in pair:
+                copy.wait()
+
+    out[0] = lax.dot_general(
+        left[i], grad[i], (((0,), (0,)), ((), ())), preferred_element_type=F32
+    ).astype(BF16)
+
+
 def smem():
     return pl.BlockSpec(memory_space=pltpu.SMEM)
 
@@ -385,9 +556,14 @@
     return jax.ShapeDtypeStruct(dims, kind)
 
 
-def run(kernel, T, grid, in_specs, out_specs, outs, args, flops, moved, scratch=()):
+def run(kernel, T, grid, in_specs, out_specs, outs, args, flops, moved, scratch=(), items=(),
+        after=()):
+    count = len(args)
+    in_specs = in_specs + anywhere(len(after))
+    args = args + tuple(after)
+
     def body(*refs):
-        kernel(T, *refs)
+        kernel(*((items,) if items else ()), T, *refs[:count], *refs[count + len(after) :])
 
     return pl.pallas_call(
         body,
@@ -399,117 +575,142 @@
         compiler_params=pltpu.CompilerParams(
             dimension_semantics=("arbitrary",), vmem_limit_bytes=VMEM
         ),
-        cost_estimate=pl.CostEstimate(flops=flops, bytes_accessed=moved, transcendentals=0),
+        cost_estimate=pl.CostEstimate(
+            flops=flops // COST, bytes_accessed=moved // COST, transcendentals=0
+        ),
         name=kernel.__name__,
     )(*args)
 
 
-def time_in(T, place, x, edge, vec, mats):
+def anywhere(count):
+    return [pl.BlockSpec(memory_space=pl.ANY)] * count
+
+
+def weight_room(shapes, copies):
+    return [pltpu.VMEM(s, BF16) for s in shapes] + [pltpu.SemaphoreType.DMA((copies,))]
+
+
+def time_in(T, place, x, edge, vec, weights, after=()):
     N, D = x.shape
     R = N // T
     rs = rows_spec(T, D)
+    pieces = weights["key"][0]
+    items = [weights[name][1] for name in ("key", "value", "recept")]
     return run(
         k_time_in, T, R // RB,
-        [smem(), smem(), rs, edge_spec(D), whole_spec(vec.shape)]
-        + [col_spec(D, D, c) for c in range(3)],
+        [smem(), smem(), rs, edge_spec(D), whole_spec(vec.shape)] + anywhere(len(pieces)),
         [rs] * 8 + [state_spec(D)],
         [shape((N, D), BF16)] * 3 + [shape((N, D), F32)] * 2 + [shape((N, D), BF16)]
         + [shape((N, D), F32)] * 2 + [shape((R, 2, D), F32)],
-        (*place, x, edge.reshape(R // RB, RB, D), vec, mats, mats, mats),
+        (*place, x, edge.reshape(R // RB, RB, D), vec, *pieces),
         6 * N * D * D, 40 * N * D,
-    )
-
-
-def time_out(T, place, x, kept, state, vec, mats):
+        weight_room([(3, D, D)], 24), items, after,
+    )
+
+
+def time_out(T, place, x, kept, state, vec, weights, after=()):
     N, D = x.shape
     R = N // T
     rs = rows_spec(T, D)
+    pieces, item = weights["output"]
     return run(
         k_time_out, T, R // RB,
-        [smem(), smem()] + [rs] * 6 + [state_spec(D), whole_spec(vec.shape), col_spec(D, D, 4)],
+        [smem(), smem()] + [rs] * 6 + [state_spec(D), whole_spec(vec.shape)] + anywhere(len(pieces)),
         [rs] * 2,
         [shape((N, D), BF16), shape((N, D), F32)],
-        (*place, x, *kept, state, vec, mats),
+        (*place, x, *kept, state, vec, *pieces),
         2 * N * D * D, 30 * N * D,
-    )
-
-
-def feed(T, place, middle, edge, vec, mats, fk, fv):
+        weight_room([(D, D)], 8), [item], after,
+    )
+
+
+def feed_weights(weights):
+    blocks = sorted(name for name in weights if name.startswith("feed_key"))
+    items = [weights[name][1] for name in ["gate"] + blocks + ["feed_value"]]
+    pieces = weights["gate"][0] + weights[blocks[0]][0] + weights["feed_value"][0]
+    return items, pieces
+
+
+def feed(T, place, middle, edge, vec, weights, after=()):
     N, D = middle.shape
-    F = fk.shape[1]
-    B = D
+    items, pieces = feed_weights(weights)
+    B = len(items) - 2
+    F = B * D
     whole = whole_spec((N, D))
-    wide_spec = pl.BlockSpec((N, B), lambda j: (0, j))
+    wide_spec = pl.BlockSpec((N, D), lambda j: (0, j))
     return run(
-        k_feed, T, F // B,
-        [smem(), smem(), whole, whole_spec(edge.shape), whole_spec(vec.shape), col_spec(D, D, 3),
-         pl.BlockSpec((D, B), lambda j: (0, j)), pl.BlockSpec((B, D), lambda j: (j, 0))],
+        k_feed, T, B,
+        [smem(), smem(), whole, whole_spec(edge.shape), whole_spec(vec.shape)] + anywhere(len(pieces)),
         [whole, whole, wide_spec, wide_spec, whole, whole, whole],
         [shape((N, D), BF16)] * 2 + [shape((N, F), BF16)] * 2 + [shape((N, D), BF16)] * 2
         + [shape((N, D), F32)],
-        (*place, middle, edge, vec, mats, fk, fv),
+        (*place, middle, edge, vec, *pieces),
         4 * N * D * F + 2 * N * D * D, 20 * N * D + 4 * N * F + 4 * D * F,
-        [pltpu.VMEM((N, D), F32)],
-    )
-
-
-def feed_back(T, place, grad, gl, vb, sp, middle, edge, vec, mats, fk, fv):
+        [pltpu.VMEM((N, D), F32)]
+        + weight_room([(D, D), (B, D, D), (F, D)], 8 * len(items)), items, after,
+    )
+
+
+def feed_back(T, place, grad, gl, vb, sp, middle, edge, vec, weights, after=()):
     N, D = middle.shape
-    F = fk.shape[1]
-    B = D
+    items, pieces = feed_weights(weights)
+    B = len(items) - 2
+    F = B * D
     R = N // T
     whole = whole_spec((N, D))
-    wide_spec = pl.BlockSpec((N, B), lambda j: (0, j))
+    wide_spec = pl.BlockSpec((N, D), lambda j: (0, j))
     return run(
-        k_feed_back, T, F // B,
+        k_feed_back, T, B,
         [smem(), smem(), whole, whole, whole, wide_spec, whole, whole_spec(edge.shape),
-         whole_spec(vec.shape), col_spec(D, D, 3),
-         pl.BlockSpec((D, B), lambda j: (0, j)), pl.BlockSpec((B, D), lambda j: (j, 0))],
+         whole_spec(vec.shape)] + anywhere(len(pieces)),
         [whole, whole, wide_spec, whole, whole_spec((R, D)), whole_spec((8, D))],
         [shape((N, D), BF16)] * 2 + [shape((N, F), BF16), shape((N, D), F32)]
         + [shape((R, D), F32), shape((8, D), F32)],
-        (*place, grad, gl, vb, sp, middle, edge, vec, mats, fk, fv),
+        (*place, grad, gl, vb, sp, middle, edge, vec, *pieces),
         4 * N * D * F + 2 * N * D * D, 20 * N * D + 4 * N * F + 4 * D * F,
-        [pltpu.VMEM((N, D), F32)],
-    )
-
-
-def mid_back(T, place, gn, edge, middle, grad, vec, mats, kept, state):
+        [pltpu.VMEM((N, D), F32)]
+        + weight_room([(D, D), (B, D, D), (F, D)], 8 * len(items)), items, after,
+    )
+
+
+def mid_back(T, place, gn, edge, middle, grad, vec, weights, kept, state, after=()):
     N, D = middle.shape
     R = N // T
     rs = rows_spec(T, D)
+    pieces, item = weights["output"]
     return run(
         k_mid_back, T, R // RB,
-        [smem(), smem(), rs, edge_spec(D), rs, rs, whole_spec(vec.shape), col_spec(D, D, 4)]
-        + [rs] * 5 + [state_spec(D)],
+        [smem(), smem(), rs, edge_spec(D), rs, rs, whole_spec(vec.shape)]
+        + [rs] * 5 + [state_spec(D)] + anywhere(len(pieces)),
         [rs] * 7 + [state_spec(D), whole_spec((8, D))],
         [shape((N, D), F32)] + [shape((N, D), BF16)] * 2 + [shape((N, D), F32)] * 4
         + [shape((R, 2, D), F32), shape((8, D), F32)],
-        (*place, gn, edge.reshape(R // RB, RB, D), middle, grad, vec, mats, *kept, state),
+        (*place, gn, edge.reshape(R // RB, RB, D), middle, grad, vec, *kept, state, *pieces),
         2 * N * D * D, 50 * N * D,
-    )
-
-
-def time_back(T, place, x, edge, vec, mats, kept, state, part, after, gr):
+        weight_room([(D, D)], 8), [item], after,
+    )
+
+
+def time_back(T, place, x, edge, vec, weights, kept, state, part, later, gr, after=()):
     N, D = x.shape
     R = N // T
     rs = rows_spec(T, D)
-    key, value, num, den = kept
+    pieces = weights["key"][0]
+    items = [weights[name][1] for name in ("key", "value", "recept")]
     return run(
         k_time_back, T, R // RB,
         [smem(), smem(), rs, edge_spec(D), whole_spec(vec.shape)]
-        + [col_spec(D, D, c) for c in range(3)] + [rs] * 4 + [state_spec(D)] + [rs] * 4
-        + [state_spec(D), rs],
+        + [rs] * 4 + [state_spec(D)] + [rs] * 4 + [state_spec(D), rs] + anywhere(len(pieces)),
         [rs] * 3 + [edge_spec(D), whole_spec((8, D))],
         [shape((N, D), BF16)] * 2 + [shape((N, D), F32)]
         + [shape((R // RB, RB, D), F32), shape((8, D), F32)],
-        (*place, x, edge.reshape(R // RB, RB, D), vec, mats, mats, mats, key, value, num, den,
-         state, *part, after, gr),
+        (*place, x, edge.reshape(R // RB, RB, D), vec, *kept, state, *part, later, gr, *pieces),
         6 * N * D * D, 50 * N * D,
-    )
-
-
-def norm_in_back(T, x, gn, edge, gmid, vec):
+        weight_room([(3, D, D)], 24), items, after,
+    )
+
+
+def norm_in_back(T, x, gn, edge, gmid, vec, after=()):
     N, D = x.shape
     R = N // T
     rs = rows_spec(T, D)
@@ -519,19 +720,113 @@
         [rs, whole_spec((8, D))],
         [shape((N, D), F32), shape((8, D), F32)],
         (x, gn, edge.reshape(R // RB, RB, D), gmid, vec),
-        0, 16 * N * D,
-    )
+        0, 16 * N * D, after=after,
+    )
+
+
+SEQ = ("z", "c")
+SWAP = [(0, 1), (1, 0)]
+
+
+def by_bit(block, bit):
+    return lax.ppermute(block, "dp", [(i, i ^ bit) for i in range(lax.axis_size("dp"))])
+
+
+def after(value, *others):
+    return lax.optimization_barrier((value, *others))[0]
+
+
+def gather_seq(part, *gate):
+    return lax.all_gather(after(part, *gate), SEQ, axis=0, tiled=True)
+
+
+class Exchange:
+    def __init__(self, block, names, start, bits):
+        self.block, self.names, self.start, self.bits = block, names, start, bits
+        self.width = sum(width for _, width in names)
+        self.rows = block.shape[0] // 2
+
+    def first(self, *gate):
+        block = after(self.block, *gate)
+        self.own = lax.dynamic_slice(
+            block, (lax.axis_index("c") * self.rows, self.start), (self.rows, self.width)
+        )
+        self.one = by_bit(self.own, self.bits[0])
+        return self.one
+
+    def second(self, *gate):
+        one = after(self.one, *gate)
+        self.two = by_bit(jnp.stack([self.own, one]), self.bits[1])
+        return self.two
+
+    def cores(self, *gate):
+        one, two = after((self.one, self.two), *gate)
+        self.other_one = lax.ppermute(one, "c", SWAP)
+        self.other_two = lax.ppermute(two, "c", SWAP)
+
+    def weights(self):
+        pieces = (self.block, self.one, self.two, self.other_one, self.other_two)
+        at, found = 0, {}
+        for name, width in self.names:
+            found[name] = (pieces, (5, self.start + at, at, width, self.rows, self.bits))
+            at += width
+        return found
+
+
+class Scatter:
+    def __init__(self, grads, bits):
+        I, _, C = grads.shape
+        self.bits = bits
+        self.view = grads.reshape(I, 2, 2, lax.axis_size("z"), 2, -1, C)
+
+    def pick(self, which):
+        return lax.dynamic_index_in_dim(self.view, which, 4, keepdims=False)
+
+    def cores(self):
+        c, d = lax.axis_index("c"), lax.axis_index("dp")
+        self.received = lax.ppermute(self.pick(1 - c), "c", SWAP)
+        self.axis, self.me, self.then = (
+            (1, d // 2, d % 2) if self.bits[1] == 2 else (2, d % 2, d // 2)
+        )
+        return self.received
+
+    def part(self, a, axis, which):
+        return lax.dynamic_index_in_dim(a, which, axis, keepdims=False).astype(F32)
+
+    def first(self):
+        mine = self.pick(lax.axis_index("c"))
+        give = 1 - self.me
+        send = self.part(mine, self.axis, give) + self.part(self.received, self.axis, give)
+        got = by_bit(send.astype(BF16), self.bits[1])
+        keep = self.part(mine, self.axis, self.me) + self.part(self.received, self.axis, self.me)
+        self.kept = keep + got.astype(F32)
+        return got
+
+    def second(self):
+        got = by_bit(self.part(self.kept, 1, 1 - self.then).astype(BF16), self.bits[0])
+        total = (self.part(self.kept, 1, self.then) + got.astype(F32)).astype(BF16)
+        I, C = total.shape[0], total.shape[-1]
+        self.total = total.transpose(1, 0, 2, 3).reshape(-1, C)
+        self.count = I
+        return got
+
+    def last(self):
+        if hasattr(self, "out"):
+            return self.out
+        out = lax.psum_scatter(self.total, "z", scatter_dimension=0, tiled=True)
+        self.out = out.reshape(self.count, -1, out.shape[1])
+        return self.out
 
 
 def from_behind(block, distance):
-    devices = range(lax.axis_size("seq"))
+    devices = range(lax.axis_size(SEQ))
     route = [(i - distance, i) for i in devices if i - distance in devices]
-    return lax.ppermute(block, "seq", route)
+    return lax.ppermute(block, SEQ, route)
 
 
 def chain(mine, starts, rate, T, forward):
-    S, i = lax.axis_size("seq"), lax.axis_index("seq")
-    all_states = lax.all_gather(mine.astype(BF16), "seq").astype(F32)
+    S, i = lax.axis_size(SEQ), lax.axis_index(SEQ)
+    all_states = lax.all_gather(mine.astype(BF16), SEQ).astype(F32)
     j = jnp.arange(S, dtype=jnp.int32)
 
     def document(at):
@@ -549,19 +844,35 @@
     return jnp.sum(weight * all_states, axis=0)
 
 
-def layer_forward(T, place, starts, x, edge, vec, weights):
-    mats, fk, fv = weights
+def layer_forward(T, place, starts, x, edge, vec, weights, hook):
     N, D = x.shape
     R = N // T
     rate = jnp.exp(vec[5])
-    mk, mv, mr, key, value, recept, num, den, last = time_in(T, place, x, edge, vec, mats)
+    x = hook("start", x)
+    mk, mv, mr, key, value, recept, num, den, last = time_in(T, place, x, edge, vec, weights())
+    last = hook("time in", last)
     state = chain(last, starts, rate, T, True)
-    gated, middle = time_out(T, place, x, (key, value, recept, num, den), state, vec, mats)
+    state = hook("chain", state)
+    gated, middle = time_out(T, place, x, (key, value, recept, num, den), state, vec, weights())
+    middle = hook("time out", middle)
     edge_two = from_behind(middle.reshape(R, T, D)[:, -1], 1)
-    fm, gm, sp, hid, vb, gl, out = feed(T, place, middle, edge_two, vec, mats, fk, fv)
+    edge_two = hook("edge", edge_two)
+    fm, gm, sp, hid, vb, gl, out = feed(T, place, middle, edge_two, vec, weights())
+    out = hook("feed", out)
     saved = (x, edge, mk, mv, mr, key, value, recept, num, den, state, gated, middle, edge_two,
              fm, gm, sp, hid, vb, gl)
     return out, saved
+
+
+def weight_grads(lefts, gradients):
+    count, (N, D), C = len(lefts), lefts[0].shape, gradients[0].shape[1]
+    return run(
+        k_weight_grad, 0, count, anywhere(2 * count),
+        [pl.BlockSpec((1, D, C), lambda i: (i, 0, 0))], [shape((count, D, C), BF16)],
+        (*lefts, *gradients), 2 * count * N * D * C, 2 * count * (N * (D + C) + D * C),
+        [pltpu.VMEM((count, N, D), BF16), pltpu.VMEM((count, N, C), BF16),
+         pltpu.SemaphoreType.DMA((2 * count,))], count,
+    )[0]
 
 
 def weight_grad(left, gradient):
@@ -570,35 +881,31 @@
     ).astype(BF16)
 
 
-def layer_backward(T, place, starts, grad, saved, vec, weights):
-    mats, fk, fv = weights
+def layer_backward(T, place, starts, grad, saved, vec, weights, work):
     (x, edge, mk, mv, mr, key, value, recept, num, den, state, gated, middle, edge_two,
      fm, gm, sp, hid, vb, gl) = saved
     rate = jnp.exp(vec[5])
     gb, gg, gin, gn, first, sums_feed = feed_back(
-        T, place, grad, gl, vb, sp, middle, edge_two, vec, mats, fk, fv
-    )
-    d_fv = weight_grad(hid, gb)
-    d_fk = weight_grad(fm, gin)
-    d_gate = weight_grad(gm, gg)
+        T, place, grad, gl, vb, sp, middle, edge_two, vec, weights, work("feed")
+    )
     behind = from_behind(first, -1)
+    work("feed done", hid=hid, gb=gb, fm=fm, gin=gin)
     gmid, gblk, gr, gkp, gvp, gno, gdo, direct, sums_mid = mid_back(
-        T, place, gn, behind, middle, grad, vec, mats, (key, value, recept, num, den), state
-    )
-    d_out = weight_grad(gated, gblk)
-    d_recept = weight_grad(mr, gr)
-    after = chain(direct, starts, rate, T, False)
+        T, place, gn, behind, middle, grad, vec, weights, (key, value, recept, num, den), state,
+        work("mid"),
+    )
+    after_state = chain(direct, starts, rate, T, False)
     gk, gv, gn_one, first_one, sums_time = time_back(
-        T, place, x, edge, vec, mats, (key, value, num, den), state, (gkp, gvp, gno, gdo), after, gr
-    )
-    d_key = weight_grad(mk, gk)
-    d_value = weight_grad(mv, gv)
+        T, place, x, edge, vec, weights, (key, value, num, den), state, (gkp, gvp, gno, gdo),
+        after_state, gr, work("time"),
+    )
     behind_one = from_behind(first_one.reshape(edge.shape), -1)
-    grad_in, sums_norm = norm_in_back(T, x, gn_one, behind_one, gmid, vec)
+    work("time done", lefts=(mk, mv, mr, gm, gated), grads=(gk, gv, gr, gg, gblk))
+    grad_in, sums_norm = norm_in_back(T, x, gn_one, behind_one, gmid, vec, work("norm"))
     d_vec = jnp.concatenate(
         [sums_norm[0:2], sums_time[0:4], sums_mid[2:3], sums_mid[0:2], sums_feed[0:2]], axis=0
     )
-    return grad_in, (d_key, d_value, d_recept, d_gate, d_out), d_fk, d_fv, d_vec
+    return grad_in, d_vec
 
 
 def vector_rates(row_total):
@@ -617,60 +924,197 @@
     return (learning_rates * (step_ratio + decay_weight * parameter), new_first, new_second)
 
 
-AXES = ("dp", "seq")
+AXES = ("dp", "z", "c")
+XY, YX = (1, 2), (2, 1)
 
 
 def body(tokens, cotangent, document_starts, *rest):
     weights, means, powers = rest[:5], rest[5:10], rest[10:15]
     vectors, matrices, time_output, feed_key, feed_value = weights
     R, T, D = tokens.shape
-    layers, n = vectors.shape[0], matrices.shape[2]
-    base = (lax.axis_index("seq") * T).astype(jnp.int32).reshape(1)
+    layers, kinds, n = vectors.shape
+    blocks = feed_key.shape[2] // D
+    base = jnp.stack(
+        [lax.axis_index(SEQ) * T, lax.axis_index("dp"), lax.axis_index("c")]
+    ).astype(jnp.int32)
     place = (document_starts, base)
 
-    def gather(part):
-        return lax.all_gather(part.astype(BF16), AXES, axis=0, tiled=True)
-
-    order = (0, 1, 2, 3)
-    all_vectors = gather(vectors.transpose(2, 0, 1).reshape(n, layers * vectors.shape[1]))
-    all_vectors = all_vectors.astype(F32).T.reshape(layers, vectors.shape[1], D)
-    vecs = [jnp.pad(all_vectors[l], ((0, 5), (0, 0))) for l in range(layers)]
-    gathered = []
-    for l in range(layers):
-        mats = jnp.concatenate([matrices[l, j] for j in order] + [time_output[l]], axis=1)
-        gathered.append((gather(mats), gather(feed_key[l]), gather(feed_value[l])))
-
+    keys = [(f"feed_key{b}", D) for b in range(blocks)]
+    time_names = [("key", D), ("value", D), ("recept", D)]
+    rest_names = [("gate", D), ("output", D)]
+    values = [("feed_value", D)]
+    layout = [[time_names + [("vectors", 128)], rest_names + keys, values]]
+    layout += [[time_names + rest_names, keys, values]] * (layers - 1)
+
+    vector_columns = jnp.pad(
+        vectors.reshape(layers * kinds, n).T, ((0, 0), (0, 128 - layers * kinds))
+    )
+
+    def shard(l, names):
+        found = {
+            "key": matrices[l, 0], "value": matrices[l, 1], "recept": matrices[l, 2],
+            "gate": matrices[l, 3], "output": time_output[l], "feed_value": feed_value[l],
+            "vectors": vector_columns,
+        }
+        for b in range(blocks):
+            found[f"feed_key{b}"] = feed_key[l, :, b * D : (b + 1) * D]
+        return jnp.concatenate([found[name].astype(BF16) for name, _ in names], axis=1)
+
+    def sets_of(l, k, gate, *split):
+        block = gather_seq(shard(l, layout[l][k]), *gate)
+        sets, at = [], 0
+        for count, bits in split:
+            names = layout[l][k][at : at + count]
+            sets.append(Exchange(block, names, sum(w for _, w in layout[l][k][:at]), bits))
+            at += count
+        return sets
+
+    def weights_of(l):
+        def found():
+            have = {}
+            for exchange in here[l]:
+                if hasattr(exchange, "other_two"):
+                    have.update(exchange.weights())
+            return have
+
+        return found
+
+    here = [[] for _ in range(layers)]
+    A = sets_of(0, 0, (), (4, XY))[0]
+    B = sets_of(0, 1, (), (2 + blocks, XY)) + sets_of(0, 2, (), (1, YX))
+    here[0] = [A] + B
+    A.first()
+    A.second()
+    A.cores()
+    pieces, item = A.weights()["vectors"]
+    d, c = lax.axis_index("dp"), lax.axis_index("c")
+    block, one, two, other_one, other_two = (a[..., item[2] : item[2] + 128] for a in pieces)
+    bits, half = item[5], item[4]
+    mine = lax.dynamic_slice_in_dim(block, c * half, half, axis=0)
+    other = lax.dynamic_slice_in_dim(block, (1 - c) * half, half, axis=0)
+    by_m = {
+        0: (mine, other), bits[0]: (one, other_one), bits[1]: (two[0], other_two[0]),
+        bits[0] | bits[1]: (two[1], other_two[1]),
+    }
+    rel = jnp.stack([jnp.stack(by_m[m]) for m in range(4)])
+    rel = jnp.where(c == 0, rel, rel[:, ::-1])
+    columns = jnp.stack([lax.dynamic_index_in_dim(rel, d ^ j, 0, keepdims=False) for j in range(4)])
+    spread = columns.reshape(D, 128)[:, : layers * kinds].astype(F32).T.reshape(layers, kinds, D)
+    vecs = [jnp.pad(spread[l], ((0, 16 - kinds), (0, 0))) for l in range(layers)]
+
+    def hook_of(l):
+        more = l + 1 < layers
+
+        def hook(name, value):
+            nonlocal B
+            if name == "start":
+                if l > 0:
+                    F = here[l][2:]
+                    hook.F = F
+                    for e in F:
+                        e.first(value)
+                    return value
+                for e in B:
+                    e.first(A.two)
+            elif name == "time in":
+                if l == 0:
+                    value = after(value, *[e.one for e in B])
+                    for e in B:
+                        e.second(value)
+                else:
+                    value = after(value, *[e.one for e in hook.F])
+                    for e in hook.F:
+                        e.second(value)
+            elif name == "chain":
+                F = B if l == 0 else hook.F
+                value = after(value, *[e.two for e in F])
+                for e in F:
+                    e.cores(value)
+                if more:
+                    hook.M = here[l + 1][:2]
+                    for e in hook.M:
+                        e.first(value)
+            elif name == "time out" and more:
+                value = after(value, *[e.one for e in hook.M])
+            elif name == "edge" and more:
+                for e in hook.M:
+                    e.second(value)
+            elif name == "feed" and more:
+                value = after(value, *[e.two for e in hook.M])
+                for e in hook.M:
+                    e.cores(value)
+            return value
+
+        return hook
+
+    for l in range(1, layers):
+        here[l] = (
+            sets_of(l, 0, (A.one,), (3, XY), (2, YX))
+            + sets_of(l, 1, (A.two,), (blocks, XY))
+            + sets_of(l, 2, (A.two,), (1, YX))
+        )
     x = tokens.reshape(R * T, D)
     saved = []
     for l in range(layers):
         edge = from_behind(x.reshape(R, T, D)[:, -1], 1).astype(F32)
-        x, kept = layer_forward(T, place, document_starts, x, edge, vecs[l], gathered[l])
+        x, kept = layer_forward(
+            T, place, document_starts, x, edge, vecs[l], weights_of(l), hook_of(l)
+        )
         saved.append(kept)
     block_out = x.astype(BF16).reshape(R, T, D)
 
     grad = cotangent.reshape(R * T, D)
-    grads = [None] * layers
+    scatters = [None] * layers
+    vec_grads = [None] * layers
+    running = []
+
+    def advance():
+        nonlocal running
+        waits = []
+        for entry in running:
+            scatter = entry[0]
+            waits.append((scatter.cores, scatter.first, scatter.second, scatter.last)[entry[1]]())
+            entry[1] += 1
+        running = [entry for entry in running if entry[1] < 4]
+        return waits
+
+    def work_of(l):
+        def work(place_name, **have):
+            nonlocal running
+            if place_name == "feed done":
+                fv = Scatter(weight_grad(have["hid"], have["gb"])[None], YX)
+                fk = Scatter(weight_grad(have["fm"], have["gin"])[None], XY)
+                scatters[l] = [fv, fk]
+                running += [[fv, 0], [fk, 0]]
+                return ()
+            if place_name == "time done":
+                m = Scatter(weight_grads(have["lefts"], have["grads"]), XY)
+                scatters[l].append(m)
+                running += [[m, 0]]
+                return ()
+            if place_name == "norm":
+                return ()
+            return advance()
+
+        return work
+
     for l in reversed(range(layers)):
-        grad, d_mats, d_fk, d_fv, d_vec = layer_backward(
-            T, place, document_starts, grad, saved[l], vecs[l], gathered[l]
+        grad, vec_grads[l] = layer_backward(
+            T, place, document_starts, grad, saved[l], vecs[l], weights_of(l)(), work_of(l)
         )
-        vec_cols = jnp.pad(d_vec.T.astype(BF16), ((0, 0), (0, 128 - d_vec.shape[0])))
-
-        def scatter(part):
-            return lax.psum_scatter(part, AXES, scatter_dimension=0, tiled=True).astype(F32)
-
-        g_fv = scatter(d_fv)
-        g_fk = scatter(d_fk)
-        g_mats = scatter(jnp.concatenate(list(d_mats) + [vec_cols], axis=1))
-        grads[l] = (
-            g_mats[:, 5 * D : 5 * D + vectors.shape[1]].T,
-            jnp.stack([g_mats[:, j * D : (j + 1) * D] for j in range(4)]),
-            g_mats[:, 4 * D : 5 * D],
-            g_fk,
-            g_fv,
-        )
+    vec_columns = jnp.concatenate([g.T for g in vec_grads], axis=1).astype(BF16)
+    vec_columns = jnp.pad(vec_columns, ((0, 0), (0, 128 - layers * kinds)))
+    vec_scatter = Scatter(vec_columns[None], XY)
+    running += [[vec_scatter, 0]]
+    while running:
+        advance()
+    g_vec = vec_scatter.last()[0].astype(F32)
+    grads = []
+    for l in range(layers):
+        g_fv, g_fk, g_m = (s.last().astype(F32) for s in scatters[l])
+        grads.append((g_vec[:, l * kinds : (l + 1) * kinds].T, g_m[:4], g_m[4], g_fk[0], g_fv[0]))
     shards = tuple(jnp.stack([g[m] for g in grads]) for m in range(5))
-    rates = (vector_rates(vectors.shape[1]),) + (rate_main,) * 4
+    rates = (vector_rates(kinds),) + (rate_main,) * 4
     decays = (0.0,) + (weight_decay,) * 4
     new = [adam_step(*z) for z in zip(weights, shards, means, powers, rates, decays)]
     return (
@@ -684,7 +1128,9 @@
 
 
 def solution(mesh):
-    tokens = P("dp", "seq", None)
+    dp, seq = mesh.shape["dp"], mesh.shape["seq"]
+    mesh = Mesh(mesh.devices.reshape(dp, seq // 2, 2), AXES)
+    tokens = P("dp", SEQ, None)
     group = (
         P(None, None, AXES),
         P(None, None, AXES, None),

time: 1280 us -> 684 us (0.53)
  waiting for transfers between devices: 886 us -> 184 us
  other arithmetic: 22.4 us -> 70.6 us
  starting transfers between devices: 16.4 us -> 57.2 us
  local copies, waits for them, and re-layouts: 55.8 us -> 92.9 us
  matrix products: 38.3 us -> 11.8 us
  Pallas kernels: 138 us -> 161 us
  blocking collectives: 101 us -> 80.1 us
    reduce_scatter x4 -> x6, waiting for transfers between devices: 420 us -> 28.8 us  [last(): out = lax.psum_scatter(self.total, 'z', scatter_dimension=0, tiled=True)]
    all_gather x6 -> x5, waiting for transfers between devices: 267 us -> 0.1 us  [gather_seq(): return lax.all_gather(after(part, *gate), SEQ, axis=0, tiled=True)]
    unnamed x12 -> x13, waiting for transfers between devices: 197 us -> 0.22 us
    ppermute x8 -> x57, waiting for transfers between devices: 2.53 us -> 154 us  [the longest x28 142 us: by_bit(): lax.ppermute(block, 'dp', [(i, i ^ bit) for i in range(lax.axis_size('dp'...]
    ppermute x8 -> x57, starting transfers between devices: 15.7 us -> 56.7 us  [the longest x28 33.6 us: by_bit(): lax.ppermute(block, 'dp', [(i, i ^ bit) for i in range(lax.axis_size('dp'...]
    dot_general x14 -> x4, matrix products: 38.3 us -> 11.8 us  [weight_grad(): lax.dot_general(left, gradient, (((0,), (0,)), ((), ())), preferred_eleme...]
    pallas_call x14 -> x16, Pallas kernels: 138 us -> 161 us  [run(): pl.pallas_call(body, grid=(grid,), in_specs=in_specs, out_specs=out_specs...]
    convert_element_type x7 -> x19, other arithmetic: 3.89 us -> 26.2 us  [the longest x7 18.4 us: first(): got = by_bit(send.astype(BF16), self.bits[1])]
  transfers between devices with their start and end apart: 19 -> 69, of which waited for: 14 -> 24; matrix products, arithmetic and copies ran while one was open for 6% -> 17% of each run, Pallas kernels for 3% -> 12%
where the time goes in v2:
time: 684 us; the launch traced here: 674 us
  waiting for transfers between devices  184 us (27%)
  Pallas kernels  161 us (24%)
  local copies, waits for them, and re-layouts  92.9 us (14%)
  blocking collectives  80.1 us (12%)
  other arithmetic  70.6 us (10%)
  starting transfers between devices  57.2 us (8%)
  between operations  17 us (2%)
  matrix products  11.8 us (2%)
    pallas_call x16, Pallas kernels, run(): pl.pallas_call(body, grid=(grid,), in_specs=in_specs, out_specs=out_specs...  161 us
    ppermute x28, waiting for transfers between devices, by_bit(): lax.ppermute(block, 'dp', [(i, i ^ bit) for i in range(lax.axis_size('dp'...  142 us
    all_gather x4, blocking collectives, chain(): all_states = lax.all_gather(mine.astype(BF16), SEQ).astype(F32)  57.8 us
    unnamed x333, local copies, waits for them, and re-layouts  33.9 us
    ppermute x28, starting transfers between devices, by_bit(): lax.ppermute(block, 'dp', [(i, i ^ bit) for i in range(lax.axis_size('dp'...  33.6 us
    reduce_scatter x6, waiting for transfers between devices, last(): out = lax.psum_scatter(self.total, 'z', scatter_dimension=0, tiled=True)  28.8 us
    all_gather x1, blocking collectives, gather_seq(): return lax.all_gather(after(part, *gate), SEQ, axis=0, tiled=True)  22.3 us
    convert_element_type x7, other arithmetic, first(): got = by_bit(send.astype(BF16), self.bits[1])  18.4 us
  transfers between devices with their start and end apart: 69, of which 24 were waited for; matrix products, arithmetic and copies ran while one was open for 17% of the time, Pallas kernels for 12%

profile of v2, /device:TPU:0, one launch (start us, length us, event | category | flops | bytes accessed | tf_op | source)
XLA Modules:
  0.0 674.3 jit_solution(7802550874964486699)
XLA Ops:
  13.0 22.3 %all_gather.42.refs_5_.refs_16_ = bf16[192,2432]{1,0:T(8,128)(2,1)S(1)} all-gather(bf16[24,2432]{1,0:T(8,128)(2,1)S(1)} %fusion.35), channel_id=1, replica_groups=mesh['dp'=4,'z'=4,'c'=2] {'z','c'}, dimensions={0}, use_global_device_ids=true | all-gather | bytes 1050624 | tf_op jit(solution)/shard_map/all_gather | solution.py:740
  37.0 11.4 %collective-permute-done.1.refs_6_.refs_17_ = bf16[96,2432]{1,0:T(8,128)(2,1)S(1)} collective-permute-done((bf16[96,2432]{1,0:T(8,128)(2,1)S(1)}, bf16[96,2432]{1,0:T(8,128)(2,1)S(1)}, u32[]{:S(2)}, u32[]{:S(2)}) %collective-permute-start.1) | collective-permute-done | bytes 466976 | tf_op jit(solution)/shard_map/ppermute | solution.py:732
  52.9 19.1 %collective-permute-done.2.refs_7_.refs_18_ = bf16[2,96,2432]{2,1,0:T(8,128)(2,1)} collective-permute-done((bf16[2,96,2432]{2,1,0:T(8,128)(2,1)}, bf16[2,96,2432]{2,1,0:T(8,128)(2,1)}, u32[]{:S(2)}, u32[]{:S(2)}) %collective-permute-start.2) | collective-permute-done | bytes 933920 | tf_op jit(solution)/shard_map/ppermute | solution.py:732
  83.7 9.6 %k_time_in.2 = (bf16[512,768]{1,0:T(8,128)(2,1)S(1)}, bf16[512,768]{1,0:T(8,128)(2,1)S(1)}, bf16[512,768]{1,0:T(8,128)(2,1)S(1)}, f32[512,768]{1,0:T(8,128)}, f3...) custom-call(s32[4,8]{1,0:T(4,128)S(1)} %copy-done.78, ...), custom_call_target="tpu_custom_call" | custom-call | flops 90596968 | bytes 786432 | tf_op jit(solution)/shard_map/k_time_in/pallas_call | solution.py:568
  93.5 8.4 %collective-permute-done.5.refs_11_.refs_6_.refs_10_.refs_15_.refs_14_ = bf16[96,4608]{1,0:T(8,128)(2,1)S(1)} collective-permute-done((bf16[96,4608]{1,0:T(8,128)(2,1)S(1)}, bf16[96,4608]{1,0:T(8,128)(2,1)S(1)}, u32[]{:S(2)}, u32[]{:S(2)}) %collective-permute-start.5) | collective-permute-done | bytes 884768 | tf_op jit(solution)/shard_map/ppermute | solution.py:732
  111.7 14.1 %all-gather = bf16[32,2,768]{2,1,0:T(2,128)(2,1)S(1)} all-gather(bf16[4,2,768]{2,1,0:T(2,128)(2,1)S(1)} %convert_element_type.751), channel_id=2, replica_groups=mesh['dp'=4,'z'=4,'c'=2] {'z','c'}, dimensions={0}, use_global_device_ids=true | all-gather | bytes 110592 | tf_op jit(solution)/shard_map/all_gather | solution.py:829
  126.5 8.0 %collective-permute-done.8.refs_17_.refs_21_ = bf16[2,384,768]{2,1,0:T(8,128)(2,1)S(1)} collective-permute-done((bf16[2,384,768]{2,1,0:T(8,128)(2,1)}, bf16[2,384,768]{2,1,0:T(8,128)(2,1)S(1)}, u32[]{:S(2)}, u32[]{:S(2)}) %collective-permute-start.8) | collective-permute-done | bytes 1179680 | tf_op jit(solution)/shard_map/ppermute | solution.py:732
  134.5 8.8 %collective-permute-done.7.refs_12_.refs_7_.refs_11_.refs_16_.refs_15_ = bf16[2,96,4608]{2,1,0:T(8,128)(2,1)} collective-permute-done((bf16[2,96,4608]{2,1,0:T(8,128)(2,1)}, bf16[2,96,4608]{2,1,0:T(8,128)(2,1)}, u32[]{:S(2)}, u32[]{:S(2)}) %collective-permute-start.7) | collective-permute-done | bytes 1769504 | tf_op jit(solution)/shard_map/ppermute | solution.py:732
  154.6 6.0 k_time_out.2
  169.8 14.9 %k_feed.2 = (bf16[512,768]{1,0:T(8,128)(2,1)S(1)}, bf16[512,768]{1,0:T(8,128)(2,1)S(1)}, bf16[512,3072]{1,0:T(8,128)(2,1)}, bf16[512,3072]{1,0:T(8,128)(2,1)}, b...) custom-call(s32[4,8]{1,0:T(4,128)S(1)} %copy-done.78, s32[3]{0:T(128)S(1)} %copy-done.87, ...), custom_call_target="tpu_custom_call" | custom-call | flops 271790912 | bytes 1179648 | tf_op jit(solution)/shard_map/k_feed/pallas_call | solution.py:568
  201.4 10.5 %k_time_in.3 = (bf16[512,768]{1,0:T(8,128)(2,1)S(1)}, bf16[512,768]{1,0:T(8,128)(2,1)S(1)}, bf16[512,768]{1,0:T(8,128)(2,1)S(1)}, f32[512,768]{1,0:T(8,128)}, f3...) custom-call(s32[4,8]{1,0:T(4,128)S(1)} %copy-done.78, ...), custom_call_target="tpu_custom_call" | custom-call | flops 90596968 | bytes 786432 | tf_op jit(solution)/shard_map/k_time_in/pallas_call | solution.py:568
  216.0 14.6 %all-gather.1 = bf16[32,2,768]{2,1,0:T(2,128)(2,1)S(1)} all-gather(bf16[4,2,768]{2,1,0:T(2,128)(2,1)S(1)} %convert_element_type.763), channel_id=3, replica_groups=mesh['dp'=4,'z'=4,'c'=2] {'z','c'}, dimensions={0}, use_global_device_ids=true | all-gather | bytes 110592 | tf_op jit(solution)/shard_map/all_gather | solution.py:829
  230.8 10.5 %collective-permute-done.24.refs_17_.refs_21_ = bf16[2,384,768]{2,1,0:T(8,128)(2,1)} collective-permute-done((bf16[2,384,768]{2,1,0:T(8,128)(2,1)S(1)}, bf16[2,384,768]{2,1,0:T(8,128)(2,1)}, u32[]{:S(2)}, u32[]{:S(2)}) %collective-permute-start.24) | collective-permute-done | bytes 1179680 | tf_op jit(solution)/shard_map/ppermute | solution.py:732
  248.7 6.2 k_time_out.3
  262.1 15.3 %k_feed.3 = (bf16[512,768]{1,0:T(8,128)(2,1)S(1)}, bf16[512,768]{1,0:T(8,128)(2,1)S(1)}, bf16[512,3072]{1,0:T(8,128)(2,1)}, bf16[512,3072]{1,0:T(8,128)(2,1)}, b...) custom-call(s32[4,8]{1,0:T(4,128)S(1)} %copy-done.78, s32[3]{0:T(128)S(1)} %copy-done.90, ...), custom_call_target="tpu_custom_call" | custom-call | flops 271790912 | bytes 1179648 | tf_op jit(solution)/shard_map/k_feed/pallas_call | solution.py:568
  277.4 15.6 %k_feed_back.2 = (bf16[512,768]{1,0:T(8,128)(2,1)S(1)}, bf16[512,768]{1,0:T(8,128)(2,1)S(1)}, bf16[512,3072]{1,0:T(8,128)(2,1)}, f32[512,768]{1,0:T(8,128)}, f32[4,768]{1,0:T(4,128)S(1)}, /*index=5*/f32[8,768]{1,0:T(8,128)S(1)}) custom-call(s32[4,8]{1,0:T(4,128)S(1)} %copy-done.78, s32[3]{0:T(128)S(1)} %copy-done.90, bf16[512,768]{1,0:T(8,128)(2,1)} %bitcast.362, ...), custom_call_target="tpu_custom_call" | custom-call | flops 271790912 | bytes 1179648 | tf_op jit(solution)/shard_map/k_feed_back/pallas_call | solution.py:568
  324.6 13.1 %k_mid_back.2 = (f32[512,768]{1,0:T(8,128)}, bf16[512,768]{1,0:T(8,128)(2,1)S(1)}, bf16[512,768]{1,0:T(8,128)(2,1)S(1)}, f32[512,768]{1,0:T(8,128)}, f32[512,768...) custom-call(s32[4,8]{1,0:T(4,128)S(1)} %copy-done.78, ...), custom_call_target="tpu_custom_call" | custom-call | flops 30198988 | bytes 983040 | tf_op jit(solution)/shard_map/k_mid_back/pallas_call | solution.py:568
  338.5 15.1 %all-gather.2 = bf16[32,2,768]{2,1,0:T(2,128)(2,1)S(1)} all-gather(bf16[4,2,768]{2,1,0:T(2,128)(2,1)S(1)} %convert_element_type.772), channel_id=4, replica_groups=mesh['dp'=4,'z'=4,'c'=2] {'z','c'}, dimensions={0}, use_global_device_ids=true | all-gather | bytes 110592 | tf_op jit(solution)/shard_map/all_gather | solution.py:829
  353.8 11.9 %k_time_back.2 = (bf16[512,768]{1,0:T(8,128)(2,1)S(1)}, bf16[512,768]{1,0:T(8,128)(2,1)S(1)}, f32[512,768]{1,0:T(8,128)}, f32[2,2,768]{2,1,0:T(2,128)S(1)}, f32[8,768]{1,0:T(8,128)S(1)}) custom-call(s32[4,8]{1,0:T(4,128)S(1)} %copy-done.78, s32[3]{0:T(128)S(1)} %copy-done.91, f32[512,768]{1,0:T(8,128)} %get-tuple-element.161.refs_2_.refs_0_, ...), custom_call_target="tpu_custom_call" | custom-call | flops 90596968 | bytes 983040 | tf_op jit(solution)/shard_map/k_time_back/pallas_call | solution.py:568
  365.8 6.1 k_weight_grad.2
  400.7 15.6 %k_feed_back.3 = (bf16[512,768]{1,0:T(8,128)(2,1)S(1)}, bf16[512,768]{1,0:T(8,128)(2,1)S(1)}, bf16[512,3072]{1,0:T(8,128)(2,1)}, f32[512,768]{1,0:T(8,128)}, f32[4,768]{1,0:T(4,128)S(1)}, /*index=5*/f32[8,768]{1,0:T(8,128)S(1)}) custom-call(s32[4,8]{1,0:T(4,128)S(1)} %copy-done.78, s32[3]{0:T(128)S(1)} %copy-done.91, f32[512,768]{1,0:T(8,128)} %copy-done.13, ...), custom_call_target="tpu_custom_call" | custom-call | flops 271790912 | bytes 1179648 | tf_op jit(solution)/shard_map/k_feed_back/pallas_call | solution.py:568
  445.7 24.4 %collective-permute-done.42 = bf16[5,2,4,24,768]{4,3,2,0,1:T(8,128)(2,1)S(1)} collective-permute-done((bf16[5,2,4,24,768]{4,3,2,0,1:T(8,128)(2,1)}, bf16[5,2,4,24,768]{4,3,2,0,1:T(8,128)(2,1)S(1)}, u32[]{:S(2)}, u32[]{:S(2)}) %collective-permute-start.42) | collective-permute-done | bytes 1474592 | tf_op jit(solution)/shard_map/ppermute | solution.py:732
  485.9 13.7 %k_mid_back.3 = (f32[512,768]{1,0:T(8,128)}, bf16[512,768]{1,0:T(8,128)(2,1)S(1)}, bf16[512,768]{1,0:T(8,128)(2,1)S(1)}, f32[512,768]{1,0:T(8,128)}, f32[512,768...) custom-call(s32[4,8]{1,0:T(4,128)S(1)} %copy-done.78, ...), custom_call_target="tpu_custom_call" | custom-call | flops 30198988 | bytes 983040 | tf_op jit(solution)/shard_map/k_mid_back/pallas_call | solution.py:568
  500.6 13.9 %all-gather.3 = bf16[32,2,768]{2,1,0:T(2,128)(2,1)S(1)} all-gather(bf16[4,2,768]{2,1,0:T(2,128)(2,1)S(1)} %convert_element_type.809), channel_id=5, replica_groups=mesh['dp'=4,'z'=4,'c'=2] {'z','c'}, dimensions={0}, use_global_device_ids=true | all-gather | bytes 110592 | tf_op jit(solution)/shard_map/all_gather | solution.py:829
  514.8 11.4 %k_time_back.3 = (bf16[512,768]{1,0:T(8,128)(2,1)S(1)}, bf16[512,768]{1,0:T(8,128)(2,1)S(1)}, f32[512,768]{1,0:T(8,128)}, f32[2,2,768]{2,1,0:T(2,128)S(1)}, f32[8,768]{1,0:T(8,128)S(1)}) custom-call(s32[4,8]{1,0:T(4,128)S(1)} %copy-done.78, s32[3]{0:T(128)S(1)} %copy-done.92, bf16[512,768]{1,0:T(8,128)(2,1)S(1)} %bitcast.356, ...), custom_call_target="tpu_custom_call" | custom-call | flops 90596968 | bytes 983040 | tf_op jit(solution)/shard_map/k_time_back/pallas_call | solution.py:568
  526.3 6.1 k_weight_grad.3
  557.9 6.0 collective-permute-done.50
  569.4 4.3 collective-permute-done.51
  577.8 24.9 %collective-permute-done.53 = bf16[5,2,4,24,768]{4,3,2,1,0:T(8,128)(2,1)} collective-permute-done((bf16[5,2,4,24,768]{4,3,2,1,0:T(8,128)(2,1)}, bf16[5,2,4,24,768]{4,3,2,1,0:T(8,128)(2,1)}, u32[]{:S(2)}, u32[]{:S(2)}) %collective-permute-start.53) | collective-permute-done | bytes 1474592 | tf_op jit(solution)/shard_map/ppermute | solution.py:732
  612.1 12.5 %collective-permute-done.54 = bf16[5,4,24,768]{3,2,1,0:T(8,128)(2,1)} collective-permute-done((bf16[5,4,24,768]{3,2,1,0:T(8,128)(2,1)}, bf16[5,4,24,768]{3,2,1,0:T(8,128)(2,1)}, u32[]{:S(2)}, u32[]{:S(2)}) %collective-permute-start.54) | collective-permute-done | bytes 737312 | tf_op jit(solution)/shard_map/ppermute | solution.py:732
  631.5 7.8 %reduce-scatter.18.cloned.1.call-done = bf16[24,3072]{1,0:T(8,128)(2,1)} async-done(((bf16[96,3072]{1,0:T(8,128)(2,1)}), bf16[24,3072]{1,0:T(8,128)(2,1)}) %reduce-scatter.18.cloned.1.call-update) | async-done | bytes 147472 | tf_op jit(solution)/shard_map/reduce_scatter | solution.py:816
  641.9 21.0 %reduce-scatter.14.cloned.1.call-done = bf16[120,768]{1,0:T(8,128)(2,1)} async-done(((bf16[480,768]{1,0:T(8,128)(2,1)}), bf16[120,768]{1,0:T(8,128)(2,1)}) %reduce-scatter.14.cloned.1.call-update) | async-done | bytes 184336 | tf_op jit(solution)/shard_map/reduce_scatter | solution.py:816
  (642 shorter events, 254.0 us)
Async XLA Ops:
  7.2 67.3 %all-gather.12.cloned.1.call-start = ((), (), s32[]{:S(2)}) async-start(), calls=%async_computation.8 | async-start | bytes 1327104 | tf_op jit(solution)/shard_map/all_gather | solution.py:740
  9.2 70.0 %all-gather.10.cloned.1.call-start = ((), (), s32[]{:S(2)}) async-start(), calls=%async_computation.7 | async-start | bytes 1990656 | tf_op jit(solution)/shard_map/all_gather | solution.py:740
  12.7 130.6 %all-gather.14.cloned.1.call-start = ((), (), s32[]{:S(2)}) async-start(), calls=%async_computation.9 | async-start | bytes 1658880 | tf_op jit(solution)/shard_map/all_gather | solution.py:740
  49.5 22.5 %collective-permute-start.2 = (bf16[2,96,2432]{2,1,0:T(8,128)(2,1)}, bf16[2,96,2432]{2,1,0:T(8,128)(2,1)}, u32[]{:S(2)}, u32[]{:S(2)}) collective-permute-start(bf16[2,96,2432]{2,1,0:T(8,128)(2,1)} %pad_maximum_fusion.4), channel_id=1, source_target_pairs={{0,16},{8,24},{16,0},{24,8},{1,17},{9,25},{17,1},{25,9},{2,18},{10... | collective-permute-start | bytes 2801672 | tf_op jit(solution)/shard_map/ppermute | solution.py:732
  51.0 21.5 %collective-permute-start = (bf16[4,768]{1,0:T(4,128)(2,1)S(1)}, bf16[4,768]{1,0:T(4,128)(2,1)S(1)}, u32[]{:S(2)}, u32[]{:S(2)}) collective-permute-start(bf16[4,768]{1,0:T(4,128)(2,1)S(1)} %bitcast.414), channel_id=1, source_target_pairs={{0,1},{1,2},{2,3},{3,4},{4,5},{5,6},{6,7},{8,9},{9,10},{10,11},{11... | collective-permute-start | bytes 18440 | tf_op jit(solution)/shard_map/ppermute | solution.py:824
  72.6 115.9 %all-gather.18.cloned.1.call-start = ((), (), s32[]{:S(2)}) async-start(), calls=%async_computation.11 | async-start | bytes 1327104 | tf_op jit(solution)/shard_map/all_gather | solution.py:740
  80.4 21.5 %collective-permute-start.5 = (bf16[96,4608]{1,0:T(8,128)(2,1)S(1)}, bf16[96,4608]{1,0:T(8,128)(2,1)S(1)}, u32[]{:S(2)}, u32[]{:S(2)}) collective-permute-start(bf16[96,4608]{1,0:T(8,128)(2,1)S(1)} %constant_dynamic-slice_fusion.10), channel_id=1, source_target_pairs={{0,8},{8,0},{16,24},{24,16},{1,9},{9,1},{17,25},{25,17},{2,10},{10... | collective-permute-start | bytes 2654216 | tf_op jit(solution)/shard_map/ppermute | solution.py:732
  103.5 39.9 %collective-permute-start.7 = (bf16[2,96,4608]{2,1,0:T(8,128)(2,1)}, bf16[2,96,4608]{2,1,0:T(8,128)(2,1)}, u32[]{:S(2)}, u32[]{:S(2)}) collective-permute-start(bf16[2,96,4608]{2,1,0:T(8,128)(2,1)} %pad_maximum_fusion), channel_id=1, source_target_pairs={{0,16},{8,24},{16,0},{24,8},{1,17},{9,25},{17,1},{25,9},{2,18},{10... | collective-permute-start | bytes 5308424 | tf_op jit(solution)/shard_map/ppermute | solution.py:732
  107.7 26.8 %collective-permute-start.8 = (bf16[2,384,768]{2,1,0:T(8,128)(2,1)}, bf16[2,384,768]{2,1,0:T(8,128)(2,1)S(1)}, u32[]{:S(2)}, u32[]{:S(2)}) collective-permute-start(bf16[2,384,768]{2,1,0:T(8,128)(2,1)} %pad_maximum_fusion.1), channel_id=1, source_target_pairs={{0,8},{8,0},{16,24},{24,16},{1,9},{9,1},{17,25},{25,17},{2,10},{10... | collective-permute-start | bytes 3538952 | tf_op jit(solution)/shard_map/ppermute | solution.py:732
  109.4 79.1 %all-gather.16.cloned.1.call-start = ((), (), s32[]{:S(2)}) async-start(), calls=%async_computation.10 | async-start | bytes 1327104 | tf_op jit(solution)/shard_map/all_gather | solution.py:740
  149.8 332.9 %reduce-scatter.10.cloned.1.call-start = ((), (), s32[]{:S(2)}) async-start(), calls=%async_computation.12 | async-start | bytes 737280 | tf_op jit(solution)/shard_map/reduce_scatter | solution.py:816
  164.7 23.7 %collective-permute-start.16 = (bf16[2,96,2304]{2,1,0:T(8,128)(2,1)S(1)}, bf16[2,96,2304]{2,1,0:T(8,128)(2,1)}, u32[]{:S(2)}, u32[]{:S(2)}) collective-permute-start(bf16[2,96,2304]{2,1,0:T(8,128)(2,1)S(1)} %pad_maximum_fusion.5), channel_id=1, source_target_pairs={{0,16},{8,24},{16,0},{24,8},{1,17},{9,25},{17,1},{25,9},{2,18},{10... | collective-permute-start | bytes 2654216 | tf_op jit(solution)/shard_map/ppermute | solution.py:732
  166.6 21.9 %collective-permute-start.17 = (bf16[2,96,1536]{2,1,0:T(8,128)(2,1)S(1)}, bf16[2,96,1536]{2,1,0:T(8,128)(2,1)}, u32[]{:S(2)}, u32[]{:S(2)}) collective-permute-start(bf16[2,96,1536]{2,1,0:T(8,128)(2,1)S(1)} %pad_maximum_fusion.6), channel_id=1, source_target_pairs={{0,8},{8,0},{16,24},{24,16},{1,9},{9,1},{17,25},{25,17},{2,10},{10... | collective-permute-start | bytes 1769480 | tf_op jit(solution)/shard_map/ppermute | solution.py:732
  192.6 20.3 %collective-permute-start.22 = (bf16[384,768]{1,0:T(8,128)(2,1)}, bf16[384,768]{1,0:T(8,128)(2,1)S(1)}, u32[]{:S(2)}, u32[]{:S(2)}) collective-permute-start(bf16[384,768]{1,0:T(8,128)(2,1)} %constant_dynamic-slice_fusion.6), channel_id=1, source_target_pairs={{0,16},{8,24},{16,0},{24,8},{1,17},{9,25},{17,1},{25,9},{2,18},{10... | collective-permute-start | bytes 1769480 | tf_op jit(solution)/shard_map/ppermute | solution.py:732
  193.0 20.0 %collective-permute-start.21 = (bf16[96,3072]{1,0:T(8,128)(2,1)}, bf16[96,3072]{1,0:T(8,128)(2,1)S(1)}, u32[]{:S(2)}, u32[]{:S(2)}) collective-permute-start(bf16[96,3072]{1,0:T(8,128)(2,1)} %constant_dynamic-slice_fusion.7), channel_id=1, source_target_pairs={{0,8},{8,0},{16,24},{24,16},{1,9},{9,1},{17,25},{25,17},{2,10},{10... | collective-permute-start | bytes 1769480 | tf_op jit(solution)/shard_map/ppermute | solution.py:732
  213.1 28.2 %collective-permute-start.24 = (bf16[2,384,768]{2,1,0:T(8,128)(2,1)S(1)}, bf16[2,384,768]{2,1,0:T(8,128)(2,1)}, u32[]{:S(2)}, u32[]{:S(2)}) collective-permute-start(bf16[2,384,768]{2,1,0:T(8,128)(2,1)S(1)} %pad_maximum_fusion.3), channel_id=1, source_target_pairs={{0,8},{8,0},{16,24},{24,16},{1,9},{9,1},{17,25},{25,17},{2,10},{10... | collective-permute-start | bytes 3538952 | tf_op jit(solution)/shard_map/ppermute | solution.py:732
  214.5 28.2 %collective-permute-start.23 = (bf16[2,96,3072]{2,1,0:T(8,128)(2,1)S(1)}, bf16[2,96,3072]{2,1,0:T(8,128)(2,1)}, u32[]{:S(2)}, u32[]{:S(2)}) collective-permute-start(bf16[2,96,3072]{2,1,0:T(8,128)(2,1)S(1)} %pad_maximum_fusion.2), channel_id=1, source_target_pairs={{0,16},{8,24},{16,0},{24,8},{1,17},{9,25},{17,1},{25,9},{2,18},{10... | collective-permute-start | bytes 3538952 | tf_op jit(solution)/shard_map/ppermute | solution.py:732
  311.1 42.7 %collective-permute-start.35 = (bf16[1,2,4,96,768]{4,3,2,1,0:T(8,128)(2,1)}, bf16[1,2,4,96,768]{4,3,2,1,0:T(8,128)(2,1)}, u32[]{:S(2)}, u32[]{:S(2)}) collective-permute-start(bf16[1,2,4,96,768]{4,3,2,1,0:T(8,128)(2,1)} %fusion.11), channel_id=1, source_target_pairs={{0,8},{8,0},{16,24},{24,16},{1,9},{9,1},{17,25},{25,17},{2,10},{10... | collective-permute-start | bytes 3538952 | tf_op jit(solution)/shard_map/ppermute | solution.py:732
  315.7 38.0 %collective-permute-start.36 = (bf16[1,2,4,24,3072]{4,3,2,1,0:T(8,128)(2,1)}, bf16[1,2,4,24,3072]{4,3,2,1,0:T(8,128)(2,1)}, u32[]{:S(2)}, u32[]{:S(2)}) collective-permute-start(bf16[1,2,4,24,3072]{4,3,2,1,0:T(8,128)(2,1)} %fusion.10), channel_id=1, source_target_pairs={{0,16},{8,24},{16,0},{24,8},{1,17},{9,25},{17,1},{25,9},{2,18},{10... | collective-permute-start | bytes 3538952 | tf_op jit(solution)/shard_map/ppermute | solution.py:732
  431.6 51.0 %reduce-scatter.12.cloned.1.call-start = ((), (), s32[]{:S(2)}) async-start(), calls=%async_computation.13 | async-start | bytes 737280 | tf_op jit(solution)/shard_map/reduce_scatter | solution.py:816
  434.7 35.4 %collective-permute-start.42 = (bf16[5,2,4,24,768]{4,3,2,0,1:T(8,128)(2,1)}, bf16[5,2,4,24,768]{4,3,2,0,1:T(8,128)(2,1)S(1)}, u32[]{:S(2)}, u32[]{:S(2)}) collective-permute-start(bf16[5,2,4,24,768]{4,3,2,0,1:T(8,128)(2,1)} %fusion.3), channel_id=1, source_target_pairs={{0,16},{8,24},{16,0},{24,8},{1,17},{9,25},{17,1},{25,9},{2,18},{10... | collective-permute-start | bytes 4423688 | tf_op jit(solution)/shard_map/ppermute | solution.py:732
  436.8 172.6 %reduce-scatter.16.cloned.1.call-start = ((), (), s32[]{:S(2)}) async-start(), calls=%async_computation.15 | async-start | bytes 921600 | tf_op jit(solution)/shard_map/reduce_scatter | solution.py:816
  439.8 74.9 %collective-permute-start.46 = (bf16[1,2,4,96,768]{4,3,2,1,0:T(8,128)(2,1)}, bf16[1,2,4,96,768]{4,3,2,1,0:T(8,128)(2,1)}, u32[]{:S(2)}, u32[]{:S(2)}) collective-permute-start(bf16[1,2,4,96,768]{4,3,2,1,0:T(8,128)(2,1)} %fusion.7), channel_id=1, source_target_pairs={{0,8},{8,0},{16,24},{24,16},{1,9},{9,1},{17,25},{25,17},{2,10},{10... | collective-permute-start | bytes 3538952 | tf_op jit(solution)/shard_map/ppermute | solution.py:732
  445.5 69.3 %collective-permute-start.47 = (bf16[1,2,4,24,3072]{4,3,2,1,0:T(8,128)(2,1)}, bf16[1,2,4,24,3072]{4,3,2,1,0:T(8,128)(2,1)}, u32[]{:S(2)}, u32[]{:S(2)}) collective-permute-start(bf16[1,2,4,24,3072]{4,3,2,1,0:T(8,128)(2,1)} %fusion.6), channel_id=1, source_target_pairs={{0,16},{8,24},{16,0},{24,8},{1,17},{9,25},{17,1},{25,9},{2,18},{10... | collective-permute-start | bytes 3538952 | tf_op jit(solution)/shard_map/ppermute | solution.py:732
  473.1 41.6 %collective-permute-start.45 = (bf16[5,4,24,768]{3,2,1,0:T(8,128)(2,1)}, bf16[5,4,24,768]{3,2,1,0:T(8,128)(2,1)}, u32[]{:S(2)}, u32[]{:S(2)}) collective-permute-start(bf16[5,4,24,768]{3,2,1,0:T(8,128)(2,1)} %fusion.18), channel_id=1, source_target_pairs={{0,8},{8,0},{16,24},{24,16},{1,9},{9,1},{17,25},{25,17},{2,10},{10... | collective-permute-start | bytes 2211848 | tf_op jit(solution)/shard_map/ppermute | solution.py:732
  536.2 28.4 %collective-permute-start.52 = (bf16[5,2,2,4,24,768]{5,4,3,2,0,1:T(8,128)(2,1)}, bf16[5,2,2,4,24,768]{5,4,3,2,0,1:T(8,128)(2,1)}, u32[]{:S(2)}, u32[]{:S(2)}) collective-permute-start(bf16[5,2,2,4,24,768]{5,4,3,2,0,1:T(8,128)(2,1)} %copy_bitcast_fusion), channel_id=1, source_target_pairs={{0,1},{1,0},{2,3},{3,2},{4,5},{5,4},{6,7},{7,6},{8,9},{9,8},{10,11... | collective-permute-start | bytes 8847368 | tf_op jit(solution)/shard_map/ppermute | solution.py:787
  541.7 69.6 %reduce-scatter.22.cloned.1.call-start = ((), (), s32[]{:S(2)}) async-start(), calls=%async_computation.18 | async-start | bytes 30720
  546.6 27.7 %collective-permute-start.56 = (bf16[1,4,96,768]{3,2,1,0:T(8,128)(2,1)}, bf16[1,4,96,768]{3,2,1,0:T(8,128)(2,1)S(1)}, u32[]{:S(2)}, u32[]{:S(2)}) collective-permute-start(bf16[1,4,96,768]{3,2,1,0:T(8,128)(2,1)} %fusion.28), channel_id=1, source_target_pairs={{0,16},{8,24},{16,0},{24,8},{1,17},{9,25},{17,1},{25,9},{2,18},{10... | collective-permute-start | bytes 1769480 | tf_op jit(solution)/shard_map/ppermute | solution.py:732
  568.0 34.7 %collective-permute-start.53 = (bf16[5,2,4,24,768]{4,3,2,1,0:T(8,128)(2,1)}, bf16[5,2,4,24,768]{4,3,2,1,0:T(8,128)(2,1)}, u32[]{:S(2)}, u32[]{:S(2)}) collective-permute-start(bf16[5,2,4,24,768]{4,3,2,1,0:T(8,128)(2,1)} %fusion), channel_id=1, source_target_pairs={{0,16},{8,24},{16,0},{24,8},{1,17},{9,25},{17,1},{25,9},{2,18},{10... | collective-permute-start | bytes 4423688 | tf_op jit(solution)/shard_map/ppermute | solution.py:732
  574.3 54.2 %reduce-scatter.20.cloned.1.call-start = ((), (), s32[]{:S(2)}) async-start(), calls=%async_computation.17 | async-start | bytes 737280 | tf_op jit(solution)/shard_map/reduce_scatter | solution.py:816
  575.3 63.9 %reduce-scatter.18.cloned.1.call-start = ((), (), s32[]{:S(2)}) async-start(), calls=%async_computation.16 | async-start | bytes 737280 | tf_op jit(solution)/shard_map/reduce_scatter | solution.py:816
  577.8 85.1 %reduce-scatter.14.cloned.1.call-start = ((), (), s32[]{:S(2)}) async-start(), calls=%async_computation.14 | async-start | bytes 921600 | tf_op jit(solution)/shard_map/reduce_scatter | solution.py:816
  (198 other events, 2154.9 us)
Sparse Core Ops, SparseCore 0:
  10.3 29.6 all-gather.11
  42.2 25.7 all-gather.9
  72.7 24.4 all-gather.13
  109.5 22.1 all-gather.17
  149.9 21.6 all-gather.15
  431.8 23.7 reduce-scatter.9
  458.5 20.2 reduce-scatter.11
  541.8 23.1 reduce-scatter.15
  574.4 18.5 reduce-scatter.21
  595.8 20.1 reduce-scatter.19
  619.0 20.1 reduce-scatter.17
  641.5 21.3 reduce-scatter.13

commit v3 on v2

v3 whole, which is shorter than its diff:
```python
import jax
import jax.numpy as jnp
from jax import lax
from jax.experimental import pallas as pl
from jax.experimental.pallas import tpu as pltpu
from jax.sharding import Mesh, PartitionSpec as P

norm_epsilon = 1e-05
beta_one = 0.9
beta_two = 0.99
adam_epsilon = 1e-08
step_count = 10
rate_main = 0.0006
rate_time = 0.0012
weight_decay = 0.1

RB = 2
COST = 20
VMEM = 63 * 1024 * 1024
F32, BF16 = jnp.float32, jnp.bfloat16


def dot_nn(a, b):
    return lax.dot_general(a, b, (((1,), (0,)), ((), ())), preferred_element_type=F32)


def dot_nt(a, b):
    return lax.dot_general(a, b, (((1,), (1,)), ((), ())), preferred_element_type=F32)


def dot_tn(a, b):
    return lax.dot_general(a, b, (((0,), (0,)), ((), ())), preferred_element_type=F32)


def colsum(a):
    return jnp.sum(a, axis=0, keepdims=True)


LANES = 128


def columns(D):
    return [slice(j, j + LANES) for j in range(0, D, LANES)]


def place_of(starts_ref, base_ref, row, T):
    local = lax.broadcasted_iota(jnp.int32, (T, LANES), 0)
    base = base_ref[0]
    begin = jnp.zeros((T, LANES), jnp.int32)
    last_begin = jnp.int32(0)
    for j in range(starts_ref.shape[1]):
        s = starts_ref[row, j]
        begin = jnp.where(local + base >= s, jnp.maximum(begin, s), begin)
        last_begin = jnp.where(base + T - 1 >= s, jnp.maximum(last_begin, s), last_begin)
    dist = local + base - begin
    tail = (local + base >= last_begin).astype(F32)
    return local, dist, tail


def levels(T):
    k = 1
    while k < T:
        yield k
        k *= 2


def keeps_of(local, dist, T):
    return [((dist >= k) & (local >= k)).astype(F32) for k in levels(T)]


def lane_mean(total, D):
    return jnp.broadcast_to(jnp.sum(total, axis=-1, keepdims=True) * (1.0 / D), total.shape)


def norm_stats(x, rows, D):
    mean = lane_mean(sum(x[rows, c].astype(F32) for c in columns(D)), D)
    spread = [x[rows, c].astype(F32) - mean for c in columns(D)]
    rstd = lax.rsqrt(lane_mean(sum(s * s for s in spread), D) + norm_epsilon)
    return mean, rstd


def norm_rows(x, gain, bias):
    centred = x - jnp.mean(x, axis=-1, keepdims=True)
    rstd = lax.rsqrt(jnp.mean(centred * centred, axis=-1, keepdims=True) + norm_epsilon)
    return centred * rstd * gain + bias


def previous_of(normalized, edge, local, joined):
    return jnp.where(local == 0, edge, pltpu.roll(normalized, 1, 0)) * joined


def mixed(x, rows, c, stats, vec, gain_row, edge, local, joined):
    mean, rstd = stats
    normalized = (x[rows, c].astype(F32) - mean) * rstd * vec[gain_row : gain_row + 1, c]
    normalized = normalized + vec[gain_row + 1 : gain_row + 2, c]
    previous = previous_of(normalized, edge, local, joined)
    return previous, normalized - previous


def shift_up(masked, local, T):
    return jnp.where(local == T - 1, 0.0, pltpu.roll(masked, T - 1, 0))


def scan_down(pair, rate, keeps, T):
    for k, keep in zip(levels(T), keeps):
        weight = keep * jnp.exp(-float(k) * rate)
        pair = tuple(a + weight * pltpu.roll(a, k, 0) for a in pair)
    return pair


def scan_up(pair, rate, keeps, T):
    for k, keep in zip(levels(T), keeps):
        weight = keep * jnp.exp(-float(k) * rate)
        pair = tuple(a + pltpu.roll(weight * a, T - k, 0) for a in pair)
    return pair


def piece_copies(base, pieces, item, target, sems, at):
    count, first_in_block, first, width, rows, bits = item
    columns = pl.ds(first, width)
    if count == 1:
        return [(0, pltpu.make_async_copy(pieces[0].at[:, pl.ds(first_in_block, width)], target, sems.at[at]))]
    block, one, two, other_one, other_two = pieces
    d, c = base[1], base[2]
    copies = []
    for half, first_ref, second_ref in ((c, one, two), (1 - c, other_one, other_two)):
        start = pl.multiple_of(half * rows, rows)
        for source, m in (
            (block.at[pl.ds(start, rows), pl.ds(first_in_block, width)], 0),
            (first_ref.at[:, columns], bits[0]),
            (second_ref.at[0, :, columns], bits[1]),
            (second_ref.at[1, :, columns], bits[0] | bits[1]),
        ):
            row = pl.multiple_of(((d ^ m) * 2 + half) * rows, rows)
            copies.append(
                (m, pltpu.make_async_copy(
                    source, target.at[pl.ds(row, rows)], sems.at[at + len(copies)]
                ))
            )
    return copies


def split_refs(items, refs):
    groups, at = [], 0
    for count in items:
        groups.append(refs[at : at + count])
        at += count
    return groups, refs[at:]


def k_time_in(items, T, starts, base, x, edge, vec, *refs):
    (pieces,), (mk, mv, mr, ko, vo, ro, no, do, last, w, sems) = split_refs([items[0][0]], refs)
    D = x.shape[1]
    i = pl.program_id(0)
    copies = [
        copy
        for s, item in enumerate(items)
        for copy in piece_copies(base, pieces, item, w.at[s], sems, 8 * s)
    ]

    @pl.when(i == 0)
    def _():
        for _, copy in copies:
            copy.start()

    edge_norm = norm_rows(edge[0], vec[0:1], vec[1:2])
    places = [place_of(starts, base, i * RB + q, T) for q in range(RB)]
    for q, (local, dist, _) in enumerate(places):
        rows = slice(q * T, q * T + T)
        joined = (dist >= 1).astype(F32)
        stats = norm_stats(x, rows, D)
        for c in columns(D):
            previous, change = mixed(
                x, rows, c, stats, vec, 0, edge_norm[q : q + 1, c], local, joined
            )
            for j, out in ((2, mk), (3, mv), (4, mr)):
                out[rows, c] = (previous + change * vec[j : j + 1, c]).astype(BF16)

    @pl.when(i == 0)
    def _():
        for _, copy in copies:
            copy.wait()

    ko[...] = dot_nn(mk[...], w[0])
    vo[...] = dot_nn(mv[...], w[1]).astype(vo.dtype)
    ro[...] = dot_nn(mr[...], w[2]).astype(ro.dtype)
    for q, (local, dist, _) in enumerate(places):
        rows = slice(q * T, q * T + T)
        keeps = keeps_of(local, dist, T)
        for c in columns(D):
            rate = jnp.exp(vec[5:6, c])
            weight = jnp.exp(ko[rows, c])
            sums = scan_down((weight * vo[rows, c].astype(F32), weight), rate, keeps, T)
            for side, (out, total) in enumerate(zip((no, do), sums)):
                out[rows, c] = (keeps[0] * pltpu.roll(total, 1, 0)).astype(out.dtype)
                last[q, side : side + 1, c] = total[T - 1 : T]


def decay_state(vec, c, key, value, num, den, state, local, dist):
    rate = jnp.exp(vec[5:6, c])
    fade = (dist >= local + 1).astype(F32) * jnp.exp(-local.astype(F32) * rate)
    full_n = num.astype(F32) + fade * state[0:1]
    full_d = den.astype(F32) + fade * state[1:2]
    extra = jnp.exp(vec[6:7, c] + key)
    inverse = 1.0 / (full_d + extra)
    mean = (full_n + extra * value) * inverse
    return full_n, full_d, extra, inverse, mean


def k_time_out(items, T, starts, base, x, key, value, recept, num, den, state, vec, *refs):
    (pieces,), (gated, middle, w, sems) = split_refs([items[0][0]], refs)
    D = x.shape[1]
    i = pl.program_id(0)
    copies = piece_copies(base, pieces, items[0], w, sems, 0)

    @pl.when(i == 0)
    def _():
        for _, copy in copies:
            copy.start()

    for q in range(RB):
        local, dist, _ = place_of(starts, base, i * RB + q, T)
        rows = slice(q * T, q * T + T)
        for c in columns(D):
            mean = decay_state(
                vec, c, key[rows, c], value[rows, c].astype(F32), num[rows, c], den[rows, c], state[q, :, c],
                local, dist,
            )[4]
            gated[rows, c] = (jax.nn.sigmoid(recept[rows, c].astype(F32)) * mean).astype(BF16)

    @pl.when(i == 0)
    def _():
        for _, copy in copies:
            copy.wait()

    middle[...] = x[...].astype(F32) + dot_nn(gated[...], w[...])


def feed_copies(items, base, pieces, wg, wk, wv, sems):
    items = items[1:]

    def copies(index, target, at):
        group, item = items[index]
        return piece_copies(base, pieces[group], item, target, sems, at)

    blocks = (len(items) - 1) // 2
    pairs = [
        copies(1 + b, wk.at[b], 8 + 16 * b) + copies(1 + blocks + b, wv.at[b], 16 + 16 * b)
        for b in range(blocks)
    ]
    return copies(0, wg, 0), pairs


def feed_start(copies):
    gate, pairs = copies
    for _, copy in [z for block in pairs for z in block] + gate:
        copy.start()


def feed_wait(copies, j):
    for b, block in enumerate(copies[1]):

        @pl.when(j == b)
        def _():
            for _, copy in block:
                copy.wait()


def k_feed(items, T, starts, base, middle, edge, vec, *refs):
    pieces, (fm, gm, sp, hid, vb, gl, xo, acc, wg, wk, wv, sems) = split_refs(items[0], refs)
    M, D = middle.shape
    j = pl.program_id(0)
    copies = feed_copies(items, base, pieces, wg, wk, wv, sems)

    @pl.when(j == 0)
    def _():
        feed_start(copies)
        edge_norm = norm_rows(edge[...], vec[7:8], vec[8:9])
        for q in range(M // T):
            local, dist, _ = place_of(starts, base, q, T)
            rows = slice(q * T, q * T + T)
            joined = (dist >= 1).astype(F32)
            stats = norm_stats(middle, rows, D)
            for c in columns(D):
                previous, change = mixed(
                    middle, rows, c, stats, vec, 7, edge_norm[q : q + 1, c], local, joined
                )
                fm[rows, c] = (previous + change * vec[9:10, c]).astype(BF16)
                gm[rows, c] = (previous + change * vec[10:11, c]).astype(BF16)
        acc[...] = jnp.zeros_like(acc)

    feed_wait(copies, j)
    pre = dot_nn(fm[...], wk[j])
    soft = jnp.maximum(pre, 0.0) + jnp.log(1.0 + jnp.exp(-jnp.abs(pre)))
    sp[...] = soft.astype(BF16)
    hidden = (soft * soft).astype(BF16)
    hid[...] = hidden
    acc[...] += dot_nn(hidden, wv[j])

    @pl.when(j == pl.num_programs(0) - 1)
    def _():
        for _, copy in copies[0]:
            copy.wait()
        gate = dot_nn(gm[...], wg[...])
        gl[...] = gate.astype(BF16)
        vb[...] = acc[...].astype(BF16)
        xo[...] = middle[...] + jax.nn.sigmoid(gate) * acc[...]


def k_feed_back(items, T, starts, base, grad, gl, vb, sp, middle, edge, vec, *refs):
    pieces, (gb, gg, gin, gn, first, sums, acc, gc, wg, wk, wv, sems) = split_refs(
        items[0], refs
    )
    M, D = middle.shape
    j = pl.program_id(0)
    copies = feed_copies(items, base, pieces, wg, wk, wv, sems)

    @pl.when(j == 0)
    def _():
        feed_start(copies)
        g = grad[...].astype(F32)
        s = jax.nn.sigmoid(gl[...].astype(F32))
        gb[...] = (g * s).astype(BF16)
        gg[...] = (g * vb[...].astype(F32) * s * (1.0 - s)).astype(BF16)
        acc[...] = jnp.zeros_like(acc)

    feed_wait(copies, j)
    soft = sp[...].astype(F32)
    gh = dot_nt(gb[...], wv[j])
    pre = (gh * (2.0 * soft * (1.0 - jnp.exp(-soft)))).astype(BF16)
    gin[...] = pre
    acc[...] += dot_nt(pre, wk[j])

    @pl.when(j == pl.num_programs(0) - 1)
    def _():
        for _, copy in copies[0]:
            copy.wait()
        gc[...] = dot_nt(gg[...], wg[...])
        edge_norm = norm_rows(edge[...], vec[7:8], vec[8:9])
        sums[...] = jnp.zeros_like(sums)
        for q in range(M // T):
            local, dist, _ = place_of(starts, base, q, T)
            rows = slice(q * T, q * T + T)
            joined = (dist >= 1).astype(F32)
            stats = norm_stats(middle, rows, D)
            for c in columns(D):
                _, change = mixed(
                    middle, rows, c, stats, vec, 7, edge_norm[q : q + 1, c], local, joined
                )
                ga, gb_ = acc[rows, c], gc[rows, c]
                sums[0:1, c] += colsum(ga * change)
                sums[1:2, c] += colsum(gb_ * change)
                direct = ga * vec[9:10, c] + gb_ * vec[10:11, c]
                masked = (ga + gb_ - direct) * joined
                gn[rows, c] = (direct + shift_up(masked, local, T)).astype(gn.dtype)
                first[q : q + 1, c] = masked[0:1]


def norm_back(x, rows, gain_row, vec, total, sums, D, put):
    mean, rstd = norm_stats(x, rows, D)
    one = two = None
    for c in columns(D):
        hat = (x[rows, c].astype(F32) - mean) * rstd
        g = total(c)
        scaled = g * vec[gain_row : gain_row + 1, c]
        sums[0:1, c] += colsum(g * hat)
        sums[1:2, c] += colsum(g)
        one = scaled if one is None else one + scaled
        two = scaled * hat if two is None else two + scaled * hat
    one, two = lane_mean(one, D), lane_mean(two, D)
    for c in columns(D):
        hat = (x[rows, c].astype(F32) - mean) * rstd
        put(c, rstd * (total(c) * vec[gain_row : gain_row + 1, c] - one - hat * two))


def with_edge(gn, rows, edge, local, T):
    return lambda c: gn[rows, c].astype(F32) + jnp.where(local == T - 1, edge[:, c], 0.0)


def k_mid_back(items, T, starts, base, gn, edge, middle, grad, vec,
               key, value, recept, num, den, state, *refs):
    (pieces,), rest = split_refs([items[0][0]], refs)
    gm, gblk, gr, gkp, gvp, gno, gdo, direct, sums, ggated, w, sems = rest
    D = middle.shape[1]
    i = pl.program_id(0)
    copies = piece_copies(base, pieces, items[0], w, sems, 0)

    @pl.when(i == 0)
    def _():
        for _, copy in copies:
            copy.start()
        sums[...] = jnp.zeros_like(sums)

    places = [place_of(starts, base, i * RB + q, T) for q in range(RB)]
    for q, (local, dist, _) in enumerate(places):
        rows = slice(q * T, q * T + T)

        def put(c, gx):
            gmid = grad[rows, c].astype(F32) + gx
            gm[rows, c] = gmid
            gblk[rows, c] = gmid.astype(BF16)

        total = with_edge(gn, rows, edge[0, q : q + 1], local, T)
        norm_back(middle, rows, 7, vec, total, sums, D, put)

    @pl.when(i == 0)
    def _():
        for _, copy in copies:
            copy.wait()

    ggated[...] = dot_nt(gblk[...], w[...])
    for q, (local, dist, _) in enumerate(places):
        rows = slice(q * T, q * T + T)
        joined = (dist >= 1).astype(F32)
        keeps = keeps_of(local, dist, T)
        for c in columns(D):
            v, g = value[rows, c].astype(F32), ggated[rows, c]
            _, _, extra, inverse, mean = decay_state(
                vec, c, key[rows, c], v, num[rows, c], den[rows, c], state[q, :, c], local, dist
            )
            s = jax.nn.sigmoid(recept[rows, c].astype(F32))
            gr[rows, c] = (g * mean * s * (1.0 - s)).astype(BF16)
            r = g * s * inverse
            ge = extra * r * (v - mean)
            gkp[rows, c] = ge.astype(gkp.dtype)
            gvp[rows, c] = (r * extra).astype(gvp.dtype)
            sums[2:3, c] += colsum(ge)
            rate = jnp.exp(vec[5:6, c])
            totals = scan_up((r, -r * mean), rate, keeps, T)
            for side, (out, a) in enumerate(zip((gno, gdo), totals)):
                out[rows, c] = pltpu.roll(keeps[0] * a, T - 1, 0).astype(out.dtype)
                direct[q, side : side + 1, c] = (joined * a)[0:1]


def k_time_back(items, T, starts, base, x, edge, vec, key, value, num, den, state,
                gkp, gvp, gno, gdo, after, gr, *refs):
    (pieces,), (gk, gv, gn, first, sums, mixes, w, sems) = split_refs([items[0][0]], refs)
    D = x.shape[1]
    i = pl.program_id(0)
    copies = [
        copy
        for s, item in enumerate(items)
        for copy in piece_copies(base, pieces, item, w.at[s], sems, 8 * s)
    ]

    @pl.when(i == 0)
    def _():
        for _, copy in copies:
            copy.start()
        sums[...] = jnp.zeros_like(sums)

    places = [place_of(starts, base, i * RB + q, T) for q in range(RB)]
    for q, (local, dist, tail) in enumerate(places):
        rows = slice(q * T, q * T + T)
        inside = (dist >= local + 1).astype(F32)
        for c in columns(D):
            rate = jnp.exp(vec[5:6, c])
            fade = inside * jnp.exp(-local.astype(F32) * rate)
            full_n = num[rows, c].astype(F32) + fade * state[q, 0:1, c]
            full_d = den[rows, c].astype(F32) + fade * state[q, 1:2, c]
            left = tail * jnp.exp(-(T - 1 - local).astype(F32) * rate)
            grad_n = gno[rows, c].astype(F32) + left * after[q, 0:1, c]
            grad_d = gdo[rows, c].astype(F32) + left * after[q, 1:2, c]
            weight = jnp.exp(key[rows, c])
            gk[rows, c] = (
                gkp[rows, c].astype(F32) + weight * (grad_n * value[rows, c].astype(F32) + grad_d)
            ).astype(BF16)
            gv[rows, c] = (gvp[rows, c].astype(F32) + weight * grad_n).astype(BF16)
            turn = colsum(grad_n * full_n + grad_d * full_d)
            sums[3:4, c] += -rate * jnp.exp(-rate) * turn

    @pl.when(i == 0)
    def _():
        for _, copy in copies:
            copy.wait()

    for s, g in enumerate((gk, gv, gr)):
        mixes[s] = dot_nt(g[...], w[s])
    edge_norm = norm_rows(edge[0], vec[0:1], vec[1:2])
    for q, (local, dist, _) in enumerate(places):
        rows = slice(q * T, q * T + T)
        joined = (dist >= 1).astype(F32)
        stats = norm_stats(x, rows, D)
        for c in columns(D):
            _, change = mixed(x, rows, c, stats, vec, 0, edge_norm[q : q + 1, c], local, joined)
            gs = [mixes[s, rows, c] for s in range(3)]
            for s in range(3):
                sums[s : s + 1, c] += colsum(gs[s] * change)
            direct = sum(g * vec[2 + s : 3 + s, c] for s, g in enumerate(gs))
            masked = (gs[0] + gs[1] + gs[2] - direct) * joined
            gn[rows, c] = (direct + shift_up(masked, local, T)).astype(gn.dtype)
            first[0, q : q + 1, c] = masked[0:1]


def k_norm_back(T, x, gn, edge, gmid, vec, go, sums):
    i = pl.program_id(0)
    D = x.shape[1]

    @pl.when(i == 0)
    def _():
        sums[...] = jnp.zeros_like(sums)

    local = lax.broadcasted_iota(jnp.int32, (T, LANES), 0)
    for q in range(RB):
        rows = slice(q * T, q * T + T)

        def put(c, gx):
            go[rows, c] = gmid[rows, c] + gx

        total = with_edge(gn, rows, edge[0, q : q + 1], local, T)
        norm_back(x, rows, 0, vec, total, sums, D, put)


def put_halves(base, product, n, mine, send):
    pairs = product.shape[0] // (2 * n)
    lead, Z = mine.shape[0], mine.shape[1]
    for p in range(pairs):
        for out, half in ((mine, base[2]), (send, 1 - base[2])):
            start = pl.multiple_of((2 * p + half) * n, 8)
            out[p // Z, p % Z, 0] = product[pl.ds(start, n), :].astype(BF16)


def k_halves_apart(n, count, T, starts, base, *refs):
    lefts, grads, rest = refs[:count], refs[count : 2 * count], refs[2 * count :]
    mine, send, left, grad, product, sems = rest
    i = pl.program_id(0)
    pairs = [
        [
            pltpu.make_async_copy(source, target.at[k], sems.at[2 * k + side])
            for side, (source, target) in enumerate(((lefts[k], left), (grads[k], grad)))
        ]
        for k in range(count)
    ]

    @pl.when(i == 0)
    def _():
        for pair in pairs:
            for copy in pair:
                copy.start()

    for k, pair in enumerate(pairs):

        @pl.when(i == k)
        def _():
            for copy in pair:
                copy.wait()

    product[...] = dot_tn(left[i], grad[i])
    put_halves(base, product, n, mine, send)


def k_halves_blocks(n, T, starts, base, left, grad, mine, send, product):
    product[...] = dot_tn(left[...], grad[...])
    put_halves(base, product, n, mine, send)


def k_flat(T, fm, gin, hid, gb, out):
    i = pl.program_id(0)
    half = pl.num_programs(0) // 2

    @pl.when(i < half)
    def _():
        out[...] = dot_tn(fm[...], gin[...]).astype(BF16)

    @pl.when(i >= half)
    def _():
        out[...] = dot_tn(hid[...], gb[...]).astype(BF16)


def smem():
    return pl.BlockSpec(memory_space=pltpu.SMEM)


def rows_spec(T, D):
    return pl.BlockSpec((RB * T, D), lambda i: (i, 0))


def col_spec(rows, width, at):
    return pl.BlockSpec((rows, width), lambda i: (0, at))


def whole_spec(shape):
    zeros = (0,) * len(shape)
    return pl.BlockSpec(shape, lambda i: zeros)


def edge_spec(D):
    return pl.BlockSpec((1, RB, D), lambda i: (i, 0, 0))


def state_spec(D):
    return pl.BlockSpec((RB, 2, D), lambda i: (i, 0, 0))


def shape(dims, kind):
    return jax.ShapeDtypeStruct(dims, kind)


def run(kernel, T, grid, in_specs, out_specs, outs, args, flops, moved, scratch=(), items=(),
        after=()):
    count = len(args)
    in_specs = in_specs + anywhere(len(after))
    args = args + tuple(after)

    def body(*refs):
        kernel(*(items if isinstance(items, tuple) else (items,) if items else ()), T, *refs[:count], *refs[count + len(after) :])

    return pl.pallas_call(
        body,
        grid=(grid,),
        in_specs=in_specs,
        out_specs=out_specs,
        out_shape=outs,
        scratch_shapes=scratch,
        compiler_params=pltpu.CompilerParams(
            dimension_semantics=("arbitrary",), vmem_limit_bytes=VMEM
        ),
        cost_estimate=pl.CostEstimate(
            flops=flops // COST, bytes_accessed=moved // COST, transcendentals=0
        ),
        name=kernel.__name__,
    )(*args)


def anywhere(count):
    return [pl.BlockSpec(memory_space=pl.ANY)] * count


def weight_room(shapes, copies):
    return [pltpu.VMEM(s, BF16) for s in shapes] + [pltpu.SemaphoreType.DMA((copies,))]


def time_in(T, place, x, edge, vec, weights, after=()):
    N, D = x.shape
    R = N // T
    rs = rows_spec(T, D)
    pieces = weights["key"][0]
    items = [weights[name][1] for name in ("key", "value", "recept")]
    return run(
        k_time_in, T, R // RB,
        [smem(), smem(), rs, edge_spec(D), whole_spec(vec.shape)] + anywhere(len(pieces)),
        [rs] * 8 + [state_spec(D)],
        [shape((N, D), BF16)] * 3 + [shape((N, D), F32)] + [shape((N, D), BF16)] * 4
        + [shape((R, 2, D), F32)],
        (*place, x, edge.reshape(R // RB, RB, D), vec, *pieces),
        6 * N * D * D, 40 * N * D,
        weight_room([(3, D, D)], 24), items, after,
    )


def time_out(T, place, x, kept, state, vec, weights, after=()):
    N, D = x.shape
    R = N // T
    rs = rows_spec(T, D)
    pieces, item = weights["output"]
    return run(
        k_time_out, T, R // RB,
        [smem(), smem()] + [rs] * 6 + [state_spec(D), whole_spec(vec.shape)] + anywhere(len(pieces)),
        [rs] * 2,
        [shape((N, D), BF16), shape((N, D), F32)],
        (*place, x, *kept, state, vec, *pieces),
        2 * N * D * D, 30 * N * D,
        weight_room([(D, D)], 8), [item], after,
    )


def feed_weights(weights):
    keys, values = (
        sorted(name for name in weights if name.startswith(kind)) for kind in ("feed_key", "feed_value")
    )
    groups, items = [], []
    for name in ["gate"] + keys + values:
        pieces, item = weights[name]
        found = [k for k, group in enumerate(groups) if group is pieces]
        if not found:
            found = [len(groups)]
            groups.append(pieces)
        items.append((found[0], item))
    pieces = tuple(piece for group in groups for piece in group)
    return [[len(group) for group in groups]] + items, pieces


def feed(T, place, middle, edge, vec, weights, after=()):
    N, D = middle.shape
    items, pieces = feed_weights(weights)
    B = (len(items) - 2) // 2
    F = B * D
    whole = whole_spec((N, D))
    wide_spec = pl.BlockSpec((N, D), lambda j: (0, j))
    return run(
        k_feed, T, B,
        [smem(), smem(), whole, whole_spec(edge.shape), whole_spec(vec.shape)] + anywhere(len(pieces)),
        [whole, whole, wide_spec, wide_spec, whole, whole, whole],
        [shape((N, D), BF16)] * 2 + [shape((N, F), BF16)] * 2 + [shape((N, D), BF16)] * 2
        + [shape((N, D), F32)],
        (*place, middle, edge, vec, *pieces),
        4 * N * D * F + 2 * N * D * D, 20 * N * D + 4 * N * F + 4 * D * F,
        [pltpu.VMEM((N, D), F32)]
        + weight_room([(D, D), (B, D, D), (B, D, D)], 8 * len(items)), items, after,
    )


def feed_back(T, place, grad, gl, vb, sp, middle, edge, vec, weights, after=()):
    N, D = middle.shape
    items, pieces = feed_weights(weights)
    B = (len(items) - 2) // 2
    F = B * D
    R = N // T
    whole = whole_spec((N, D))
    wide_spec = pl.BlockSpec((N, D), lambda j: (0, j))
    return run(
        k_feed_back, T, B,
        [smem(), smem(), whole, whole, whole, wide_spec, whole, whole_spec(edge.shape),
         whole_spec(vec.shape)] + anywhere(len(pieces)),
        [whole, whole, wide_spec, whole, whole_spec((R, D)), whole_spec((8, D))],
        [shape((N, D), BF16)] * 2 + [shape((N, F), BF16), shape((N, D), BF16)]
        + [shape((R, D), F32), shape((8, D), F32)],
        (*place, grad, gl, vb, sp, middle, edge, vec, *pieces),
        4 * N * D * F + 2 * N * D * D, 20 * N * D + 4 * N * F + 4 * D * F,
        [pltpu.VMEM((N, D), F32)] * 2
        + weight_room([(D, D), (B, D, D), (B, D, D)], 8 * len(items)), items, after,
    )


def mid_back(T, place, gn, edge, middle, grad, vec, weights, kept, state, after=()):
    N, D = middle.shape
    R = N // T
    rs = rows_spec(T, D)
    pieces, item = weights["output"]
    return run(
        k_mid_back, T, R // RB,
        [smem(), smem(), rs, edge_spec(D), rs, rs, whole_spec(vec.shape)]
        + [rs] * 5 + [state_spec(D)] + anywhere(len(pieces)),
        [rs] * 7 + [state_spec(D), whole_spec((8, D))],
        [shape((N, D), F32)] + [shape((N, D), BF16)] * 6
        + [shape((R, 2, D), F32), shape((8, D), F32)],
        (*place, gn, edge.reshape(R // RB, RB, D), middle, grad, vec, *kept, state, *pieces),
        2 * N * D * D, 50 * N * D,
        [pltpu.VMEM((RB * T, D), F32)] + weight_room([(D, D)], 8), [item], after,
    )


def time_back(T, place, x, edge, vec, weights, kept, state, part, later, gr, after=()):
    N, D = x.shape
    R = N // T
    rs = rows_spec(T, D)
    pieces = weights["key"][0]
    items = [weights[name][1] for name in ("key", "value", "recept")]
    return run(
        k_time_back, T, R // RB,
        [smem(), smem(), rs, edge_spec(D), whole_spec(vec.shape)]
        + [rs] * 4 + [state_spec(D)] + [rs] * 4 + [state_spec(D), rs] + anywhere(len(pieces)),
        [rs] * 3 + [edge_spec(D), whole_spec((8, D))],
        [shape((N, D), BF16)] * 3
        + [shape((R // RB, RB, D), F32), shape((8, D), F32)],
        (*place, x, edge.reshape(R // RB, RB, D), vec, *kept, state, *part, later, gr, *pieces),
        6 * N * D * D, 50 * N * D,
        [pltpu.VMEM((3, RB * T, D), F32)] + weight_room([(3, D, D)], 24), items, after,
    )


def norm_in_back(T, x, gn, edge, gmid, vec, after=()):
    N, D = x.shape
    R = N // T
    rs = rows_spec(T, D)
    return run(
        k_norm_back, T, R // RB,
        [rs, rs, edge_spec(D), rs, whole_spec(vec.shape)],
        [rs, whole_spec((8, D))],
        [shape((N, D), F32), shape((8, D), F32)],
        (x, gn, edge.reshape(R // RB, RB, D), gmid, vec),
        0, 16 * N * D, after=after,
    )


SEQ = ("z", "c")
AXES = ("dp", "z", "c")
SWAP = [(0, 1), (1, 0)]


def by_bit(block, bit):
    return lax.ppermute(block, "dp", [(i, i ^ bit) for i in range(lax.axis_size("dp"))])


def after(value, *others):
    return lax.optimization_barrier((value, *others))[0]


def gather_seq(part, *gate):
    return lax.all_gather(after(part, *gate), SEQ, axis=0, tiled=True)


class Gathered:
    def __init__(self, part, names, *gate):
        self.block = lax.all_gather(after(part, *gate), AXES, axis=0, tiled=True)
        self.names = names

    def weights(self):
        pieces, at, found = (self.block,), 0, {}
        for name, width in self.names:
            found[name] = (pieces, (1, at, 0, width, 0, (0, 0)))
            at += width
        return found


class Exchange:
    def __init__(self, block, names, start, bits):
        self.block, self.names, self.start, self.bits = block, names, start, bits
        self.width = sum(width for _, width in names)
        self.rows = block.shape[0] // 2

    def first(self, *gate):
        block = after(self.block, *gate)
        self.own = lax.dynamic_slice(
            block, (lax.axis_index("c") * self.rows, self.start), (self.rows, self.width)
        )
        self.one = by_bit(self.own, self.bits[0])
        return self.one

    def second(self, *gate):
        one = after(self.one, *gate)
        self.two = by_bit(jnp.stack([self.own, one]), self.bits[1])
        return self.two

    def cores(self, *gate):
        self.one, self.two = after((self.one, self.two), *gate)
        self.other_one = lax.ppermute(self.one, "c", SWAP)
        self.other_two = lax.ppermute(self.two, "c", SWAP)

    def weights(self):
        if not hasattr(self, "pieces"):
            self.pieces = (self.block, self.one, self.two, self.other_one, self.other_two)
        pieces, at, found = self.pieces, 0, {}
        for name, width in self.names:
            found[name] = (pieces, (5, self.start + at, at, width, self.rows, self.bits))
            at += width
        return found


class Scatter:
    def __init__(self, mine, send, bits):
        self.mine, self.send, self.bits = mine, send, bits

    def part(self, a, y, x):
        if y is not None:
            a = lax.dynamic_index_in_dim(a, y, 0, keepdims=True)
        if x is not None:
            a = lax.dynamic_index_in_dim(a, x, 1, keepdims=True)
        return a.astype(F32)

    def cores(self, *gate):
        self.received = lax.ppermute(after(self.send, *gate), "c", SWAP)
        return self.received

    def first(self, *gate):
        d = lax.axis_index("dp")
        y, x = d // 2, d % 2
        terms = after((self.mine, self.received), *gate)
        place = (1 - y, None) if self.bits[1] == 2 else (None, 1 - x)
        self.got = by_bit(sum(self.part(a, *place) for a in terms).astype(BF16), self.bits[1])
        return self.got

    def second(self, *gate):
        d = lax.axis_index("dp")
        y, x = d // 2, d % 2
        terms = after((self.mine, self.received, self.got), *gate)

        def total(y, x):
            got = self.part(terms[2], *((None, x) if self.bits[1] == 2 else (y, None)))
            return self.part(terms[0], y, x) + self.part(terms[1], y, x) + got

        there = (y, 1 - x) if self.bits[1] == 2 else (1 - y, x)
        self.two = by_bit(total(*there).astype(BF16), self.bits[0])
        self.keep = lambda two: (total(y, x) + two.astype(F32)).astype(BF16)
        return self.two


def finish(scatters, *gate):
    parts, shapes = [], []
    width = max(s.mine.shape[-1] for s in scatters)
    for scatter in scatters:
        total = scatter.keep(after(scatter.two, *gate))[0, 0]
        Z, I, n, C = total.shape
        if C < width:
            total = jnp.pad(total, ((0, 0), (0, 0), (0, 0), (0, width - C)))
        parts.append(total.reshape(Z, I * n, width))
        shapes.append((I, n, C))
    whole = jnp.concatenate(parts, axis=1)
    out = lax.psum_scatter(
        whole.reshape(-1, whole.shape[2]), "z", scatter_dimension=0, tiled=True
    )
    at = 0
    for scatter, (I, n, C) in zip(scatters, shapes):
        scatter.out = out[at : at + I * n, :C].reshape(I, n, C).astype(F32)
        at += I * n
    return out, whole


def from_behind(block, distance):
    devices = range(lax.axis_size(SEQ))
    route = [(i - distance, i) for i in devices if i - distance in devices]
    return lax.ppermute(block, SEQ, route)


def chain(mine, starts, rate, T, forward):
    S, i = lax.axis_size(SEQ), lax.axis_index(SEQ)
    all_states = lax.all_gather(mine.astype(BF16), SEQ).astype(F32)
    j = jnp.arange(S, dtype=jnp.int32)

    def document(at):
        return jnp.sum((starts[None] <= at[:, None, None]).astype(jnp.int32), axis=2)

    if forward:
        lag = i - 1 - j
        same = document((j + 1) * T - 1) == document((i * T - 1)[None])
    else:
        lag = j - 1 - i
        same = document(j * T - 1) == document(((i + 1) * T - 1)[None])
    keep = (same & (lag >= 0)[:, None]).astype(F32)
    fade = jnp.exp(-(T * jnp.maximum(lag, 0)).astype(F32)[:, None] * rate[None])
    weight = keep[:, :, None, None] * fade[:, None, None, :]
    return jnp.sum(weight * all_states, axis=0)


def layer_forward(T, place, starts, x, edge, vec, weights, hook):
    N, D = x.shape
    R = N // T
    rate = jnp.exp(vec[5])
    x = hook("start", x)
    mk, mv, mr, key, value, recept, num, den, last = time_in(T, place, x, edge, vec, weights())
    last = hook("time in", last)
    state = chain(last, starts, rate, T, True)
    state = hook("chain", state)
    gated, middle = time_out(T, place, x, (key, value, recept, num, den), state, vec, weights())
    middle = hook("time out", middle)
    edge_two = from_behind(middle.reshape(R, T, D)[:, -1], 1)
    edge_two = hook("edge", edge_two)
    fm, gm, sp, hid, vb, gl, out = feed(T, place, middle, edge_two, vec, weights())
    out = hook("feed", out)
    saved = (x, edge, mk, mv, mr, key, value, recept, num, den, state, gated, middle, edge_two,
             fm, gm, sp, hid, vb, gl)
    return out, saved


def weight_halves(place, lefts, grads, n, kind):
    N = lefts[0].shape[0]
    D = grads[0].shape[1] if kind == "lefts" else lefts[0].shape[1]
    Z = lax.axis_size("z")
    if kind == "apart":
        count = len(lefts)
    else:
        count = (lefts[0] if kind == "lefts" else grads[0]).shape[1] // D
    if n % 8:
        if kind == "lefts":
            lefts, grads = [lefts[0][:, k * D : (k + 1) * D] for k in range(count)], grads * count
        elif kind == "grads":
            lefts, grads = lefts * count, [grads[0][:, k * D : (k + 1) * D] for k in range(count)]
        products = [
            lax.dot_general(a, b, (((0,), (0,)), ((), ())), preferred_element_type=F32).astype(BF16)
            for a, b in zip(lefts, grads)
        ]
        whole = jnp.stack([p.reshape(2, 2, Z, 2, n, D) for p in products], axis=3)
        c = lax.axis_index("c")
        return tuple(
            lax.dynamic_index_in_dim(whole, which, 4, keepdims=False) for which in (c, 1 - c)
        )
    out = pl.BlockSpec((4, Z, 1, n, D), lambda i: (0, 0, i, 0, 0))
    outs = [shape((4, Z, count, n, D), BF16)] * 2
    cost = (2 * count * N * D * D, 2 * count * (2 * N * D + D * D))
    room = [pltpu.VMEM((D, D), F32)]
    if kind == "apart":
        halves = run(
            k_halves_apart, 0, count, [smem(), smem()] + anywhere(2 * count), [out] * 2, outs,
            (*place, *lefts, *grads), *cost,
            [pltpu.VMEM((count, N, D), BF16)] * 2 + room + [pltpu.SemaphoreType.DMA((2 * count,))],
            (n, count),
        )
    else:
        fixed = pl.BlockSpec((N, D), lambda i: (0, 0))
        moving = pl.BlockSpec((N, D), lambda i: (0, i))
        specs = [moving, fixed] if kind == "lefts" else [fixed, moving]
        halves = run(
            k_halves_blocks, 0, count, [smem(), smem()] + specs, [out] * 2, outs,
            (*place, *lefts, *grads), *cost, room, (n,),
        )
    return tuple(a.reshape(2, 2, *a.shape[1:]) for a in halves)


def flat_grads(fm, gin, hid, gb):
    N, D = fm.shape
    B = gin.shape[1] // D
    fixed = pl.BlockSpec((N, D), lambda i: (0, 0))
    return run(
        k_flat, 0, 2 * B,
        [fixed, pl.BlockSpec((N, D), lambda i: (0, jnp.minimum(i, B - 1))),
         pl.BlockSpec((N, D), lambda i: (0, jnp.maximum(i - B, 0))), fixed],
        [pl.BlockSpec((D, D), lambda i: (0, i))], [shape((D, 2 * B * D), BF16)],
        (fm, gin, hid, gb), 4 * B * N * D * D, 4 * B * (2 * N * D + D * D),
    )[0]


def layer_backward(T, place, starts, grad, saved, vec, weights, hook):
    (x, edge, mk, mv, mr, key, value, recept, num, den, state, gated, middle, edge_two,
     fm, gm, sp, hid, vb, gl) = saved
    rate = jnp.exp(vec[5])
    outs = feed_back(T, place, grad, gl, vb, sp, middle, edge_two, vec, weights)
    gb, gg, gin, gn, first, sums_feed = hook("feed", outs)
    hook("feed grads", (hid, gb, fm, gin))
    behind = from_behind(first, -1)
    behind = hook("edge", behind)
    outs = mid_back(
        T, place, gn, behind, middle, grad, vec, weights, (key, value, recept, num, den), state
    )
    gmid, gblk, gr, gkp, gvp, gno, gdo, direct, sums_mid = hook("mid", outs)
    hook("mid grads", ((gated, gm, mr), (gblk, gg, gr)))
    direct = hook("before chain", direct)
    later = chain(direct, starts, rate, T, False)
    later = hook("chain", later)
    outs = time_back(
        T, place, x, edge, vec, weights, (key, value, num, den), state, (gkp, gvp, gno, gdo),
        later, gr,
    )
    gk, gv, gn_one, first_one, sums_time = hook("time", outs)
    hook("time grads", ((mk, mv), (gk, gv)))
    behind_one = from_behind(first_one.reshape(edge.shape), -1)
    behind_one = hook("edge two", behind_one)
    grad_in, sums_norm = norm_in_back(T, x, gn_one, behind_one, gmid, vec)
    grad_in = hook("norm", grad_in)
    return grad_in, jnp.concatenate([sums_norm, sums_time, sums_mid, sums_feed], axis=0)


VECTOR_ROWS = (0, 1, 8, 9, 10, 11, 18, 16, 17, 24, 25)


class Scattered:
    def __init__(self, product):
        out = lax.psum_scatter(product, AXES, scatter_dimension=0, tiled=True)
        self.out = out.astype(F32)


def vector_rates(row_total):
    slot = jnp.arange(row_total)
    return jnp.where((slot == 5) | (slot == 6), rate_time, rate_main)[:, None]


def adam_step(parameter, gradient, first_moment, second_moment, learning_rates, decay_weight):
    new_first = beta_one * first_moment + (1.0 - beta_one) * gradient
    new_second = beta_two * second_moment + (1.0 - beta_two) * gradient * gradient
    step_ratio = (
        new_first
        / (1.0 - beta_one**step_count)
        / (jnp.sqrt(new_second / (1.0 - beta_two**step_count)) + adam_epsilon)
    )
    return (learning_rates * (step_ratio + decay_weight * parameter), new_first, new_second)


XY, YX = (1, 2), (2, 1)


def body(tokens, cotangent, document_starts, *rest):
    weights, means, powers = rest[:5], rest[5:10], rest[10:15]
    vectors, matrices, time_output, feed_key, feed_value = weights
    R, T, D = tokens.shape
    layers, kinds, n = vectors.shape
    blocks = feed_key.shape[2] // D
    base = jnp.stack(
        [lax.axis_index(SEQ) * T, lax.axis_index("dp"), lax.axis_index("c")]
    ).astype(jnp.int32)
    place = (document_starts, base)

    def by_block(a):
        return a.reshape(n, D // n, blocks, n).transpose(0, 2, 1, 3).reshape(n, blocks * D)

    def by_device(a):
        return a.reshape(n, blocks, D // n, n).transpose(0, 2, 1, 3).reshape(n, blocks * D)

    keys = [(f"feed_key{b}", D) for b in range(blocks)]
    values = [(f"feed_value{b}", D) for b in range(blocks)]
    time_names = [("key", D), ("value", D), ("recept", D)]
    rest_names = [("output", D), ("gate", D)] + keys + values
    layout = [[time_names + [("vectors", 128)], rest_names]]
    layout += [[time_names + rest_names[:1], rest_names[1:]]] * (layers - 1)

    vector_columns = jnp.pad(
        vectors.reshape(layers * kinds, n).T, ((0, 0), (0, 128 - layers * kinds))
    )

    def shard(l, names):
        found = {
            "key": matrices[l, 0], "value": matrices[l, 1], "recept": matrices[l, 2],
            "gate": matrices[l, 3], "output": time_output[l], "vectors": vector_columns,
        }
        if ("feed_key0", D) in names:
            key_blocks = by_block(feed_key[l].astype(BF16))
            for b in range(blocks):
                found[f"feed_key{b}"] = key_blocks[:, b * D : (b + 1) * D]
                found[f"feed_value{b}"] = feed_value[l, b * n : (b + 1) * n]
        return jnp.concatenate([found[name].astype(BF16) for name, _ in names], axis=1)

    def sets_of(l, k, gate, *split):
        part = shard(l, layout[l][k])
        block = gather_seq(part, *gate)
        shards.setdefault(l, []).append(part)
        sets, at = [], 0
        for count, bits in split:
            names = layout[l][k][at : at + count]
            sets.append(Exchange(block, names, sum(w for _, w in layout[l][k][:at]), bits))
            at += count
        return sets

    def weights_of(l):
        def found():
            have = {}
            for exchange in here[l]:
                if hasattr(exchange, "other_two") or isinstance(exchange, Gathered):
                    have.update(exchange.weights())
            return have

        return found

    shards = {}
    here = [[] for _ in range(layers)]
    A = sets_of(0, 0, (), (4, XY))[0]
    O, B, V = sets_of(0, 1, (), (1, YX), (1 + blocks, XY), (blocks, YX))
    here[0] = [A, O, B, V]
    A.first()
    for l in range(1, layers):
        here[l] = sets_of(l, 0, (B.block,), (4, XY))
        here[l] += sets_of(l, 1, (here[l][0].block,), (1 + blocks, XY), (blocks, YX))
    A.second()
    O.first(A.one)
    B.first(A.one)
    A.cores(O.one, B.one, *[p for l in range(1, layers) for p in shards[l]])
    O.second(A.two)
    V.first(A.two)
    B.second(A.two)
    pieces, item = A.weights()["vectors"]
    d, c = lax.axis_index("dp"), lax.axis_index("c")
    block, one, two, other_one, other_two = (a[..., item[2] : item[2] + 128] for a in pieces)
    bits, half = item[5], item[4]
    mine = lax.dynamic_slice_in_dim(block, c * half, half, axis=0)
    other = lax.dynamic_slice_in_dim(block, (1 - c) * half, half, axis=0)
    by_m = {
        0: (mine, other), bits[0]: (one, other_one), bits[1]: (two[0], other_two[0]),
        bits[0] | bits[1]: (two[1], other_two[1]),
    }
    rel = jnp.stack([jnp.stack(by_m[m]) for m in range(4)])
    rel = jnp.where(c == 0, rel, rel[:, ::-1])
    columns = jnp.stack([lax.dynamic_index_in_dim(rel, d ^ j, 0, keepdims=False) for j in range(4)])
    spread = columns.reshape(D, 128)[:, : layers * kinds].astype(F32).T.reshape(layers, kinds, D)
    vecs = [jnp.pad(spread[l], ((0, 16 - kinds), (0, 0))) for l in range(layers)]

    def hook_of(l):
        more = l + 1 < layers

        def hook(name, value):
            if name == "start" and l > 0:
                M, U, S = here[l]
                value = after(value, M.two)
                M.cores(value)
                U.second(value)
            elif name == "time in" and l == 0:
                value = after(value, O.two, V.one)
                O.cores(value)
                V.second(value)
            elif name == "time in":
                M, U, S = here[l]
                value = after(value, S.one)
                S.second(value)
            elif name == "time out" and l == 0:
                value = after(value, V.two)
                V.cores(value)
                if more:
                    here[l + 1][0].first(value)
            elif name == "time out":
                M, U, S = here[l]
                value = after(value, S.two, U.two)
                S.cores(value)
                U.cores(value)
            elif name == "edge" and l == 0:
                value = after(value, B.two)
                B.cores(value)
                if more:
                    value = after(value, here[l + 1][0].one)
                    here[l + 1][0].second(value)
                    here[l + 1][1].first(value)
            elif name == "feed" and more:
                M, U, S = here[l + 1]
                value = after(value, U.one)
                S.first(value)
            return value

        return hook

    x = tokens.reshape(R * T, D)
    saved = []
    for l in range(layers):
        edge = from_behind(x.reshape(R, T, D)[:, -1], 1).astype(F32)
        x, kept = layer_forward(
            T, place, document_starts, x, edge, vecs[l], weights_of(l), hook_of(l)
        )
        saved.append(kept)
    block_out = x.astype(BF16).reshape(R, T, D)

    grad = cotangent.reshape(R * T, D)
    vec_grads = [None] * layers
    sums = [dict() for _ in range(layers)]

    def back_hook_of(l):
        own, last = sums[l], sums[l + 1] if l + 1 < layers else None

        def hook(name, value):
            feed = own.get("feed") if l == 0 else None
            if name == "feed" and last:
                value = after(value, last["mid"].got, last["time"].got)
                last["mid"].second(value[3])
                last["time"].second(value[3])
            elif name == "feed grads":
                hid, gb, fm, gin = value
                if l > 0:
                    own["ready"] = flat_grads(fm, gin, hid, gb)
                    own["feed"] = Scattered(own["ready"])
                else:
                    one = Scatter(*weight_halves(place, [hid], [gb], n, "lefts"), YX)
                    one.cores()
                    halves = weight_halves(place, [fm], [after(gin, one.mine)], n, "grads")
                    if last:
                        halves = after(halves, last["mid"].two, last["time"].two)
                    two = Scatter(*halves, XY)
                    two.cores()
                    own["feed"] = [one, two]
            elif name == "edge" and l > 0:
                value = after(value, own["ready"])
            elif name == "edge":
                value = after(value, *[s.received for s in feed])
                for s in feed:
                    s.first()
            elif name == "mid grads":
                halves = weight_halves(place, *value, n, "apart")
                if l == 0:
                    halves = after(halves, *[s.got for s in feed])
                own["mid"] = Scatter(*halves, YX)
                own["mid"].cores()
                if last:
                    own["gate"] = finish(
                        [last["mid"], last["time"]], last["feed"].out, own["mid"].mine
                    )[0]
                if l == 0:
                    for s in feed:
                        s.second()
            elif name == "before chain" and l == 0:
                value = after(value, own["mid"].received)
                own["mid"].first()
            elif name == "chain" and l > 0:
                value = after(value, own["mid"].received)
                own["mid"].first(value)
            elif name == "time":
                if l == 0:
                    value = after(value, own["mid"].got, *[s.two for s in feed])
                    own["gate"], whole = finish(feed, *[own["gate"]] * (layers > 1))
                    value = after(value, whole)
                    own["mid"].second(value[0])
            elif name == "time grads":
                own["time"] = Scatter(*weight_halves(place, *value, n, "apart"), XY)
                own["time"].cores()
            elif name == "edge two" and l == 0:
                value = after(value, own["time"].received)
                own["time"].first()
            elif name == "norm" and l > 0:
                value = after(value, own["time"].received)
                own["time"].first()
            return value

        return hook

    for l in reversed(range(layers)):
        grad, vec_grads[l] = layer_backward(
            T, place, document_starts, grad, saved[l], vecs[l], weights_of(l)(), back_hook_of(l)
        )
    vec_columns = jnp.concatenate(vec_grads, axis=0).astype(BF16).T
    vec_columns = jnp.pad(vec_columns, ((0, 0), (0, 128 - vec_columns.shape[1])))
    vec_view = vec_columns.reshape(2, 2, lax.axis_size("z"), 1, 2, n, 128)
    vec_sum = Scatter(
        *[lax.dynamic_index_in_dim(vec_view, w, 4, keepdims=False) for w in (c, 1 - c)], XY
    )
    tail = sums[0]
    vec_sum.cores(tail["time"].got)
    vec_sum.first()
    tail["time"].second(tail["gate"])
    vec_sum.second()
    _, whole = finish([tail["mid"], tail["time"], vec_sum])
    for l in range(1, layers):
        for e in (sums[l]["feed"], sums[l]["mid"], sums[l]["time"]):
            e.out = after(e.out, whole)
    for e in tail["feed"]:
        e.out = after(e.out, whole)
    g_vec = vec_sum.out[0]
    grads = []
    for l in range(layers):
        if l > 0:
            feed = sums[l]["feed"].out
            g_fk, g_fv = feed[:, : blocks * D], feed[:, blocks * D :]
            g_fv = jnp.concatenate([g_fv[:, b * D : (b + 1) * D] for b in range(blocks)], axis=0)
        else:
            g_fv, g_fk = (s.out for s in sums[l]["feed"])
            g_fv, g_fk = g_fv.reshape(-1, D), jnp.concatenate(list(g_fk), axis=1)
        g_out, g_gate, g_recept = sums[l]["mid"].out
        g_key, g_value = sums[l]["time"].out
        grads.append(
            (
                g_vec[:, [32 * l + k for k in VECTOR_ROWS]].T,
                jnp.stack([g_key, g_value, g_recept, g_gate]),
                g_out,
                by_device(g_fk),
                g_fv,
            )
        )
    totals = tuple(jnp.stack([g[m] for g in grads]) for m in range(5))
    rates = (vector_rates(kinds),) + (rate_main,) * 4
    decays = (0.0,) + (weight_decay,) * 4
    new = [adam_step(*z) for z in zip(weights, totals, means, powers, rates, decays)]
    return (
        block_out,
        grad.reshape(R, T, D),
        *totals,
        *[z[0] for z in new],
        *[z[1] for z in new],
        *[z[2] for z in new],
    )


def solution(mesh):
    dp, seq = mesh.shape["dp"], mesh.shape["seq"]
    mesh = Mesh(mesh.devices.reshape(dp, seq // 2, 2), AXES)
    tokens = P("dp", SEQ, None)
    group = (
        P(None, None, AXES),
        P(None, None, AXES, None),
        P(None, AXES, None),
        P(None, AXES, None),
        P(None, AXES, None),
    )
    in_specs = (tokens, tokens, P("dp", None)) + group * 3
    out_specs = (tokens, tokens) + group * 4
    return jax.shard_map(body, mesh=mesh, in_specs=in_specs, out_specs=out_specs, check_vma=False)
```

time: 684 us -> 581 us (0.85)
  waiting for transfers between devices: 184 us -> 95.7 us
  Pallas kernels: 161 us -> 199 us
  local copies, waits for them, and re-layouts: 92.9 us -> 59.6 us
  matrix products: 11.8 us -> 0 us
    ppermute x28, waiting for transfers between devices: 142 us -> 74.5 us  [by_bit(): lax.ppermute(block, 'dp', [(i, i ^ bit) for i in range(lax.axis_size('dp'...]
    pallas_call x16 -> x21, Pallas kernels: 161 us -> 199 us  [run(): pl.pallas_call(body, grid=(grid,), in_specs=in_specs, out_specs=out_specs...]
    reduce_scatter x6 -> x4, waiting for transfers between devices: 28.8 us -> 9.1 us  [the longest x3 9.1 us: finish(): lax.psum_scatter(whole.reshape(-1, whole.shape[2]), 'z', scatter_dimensio...]
    unnamed x333 -> x190, local copies, waits for them, and re-layouts: 33.9 us -> 14.7 us
    add x7 -> x0, other arithmetic: 14.8 us -> none  [first(): self.kept = keep + got.astype(F32)]
    squeeze x7 -> x1, local copies, waits for them, and re-layouts: 14.2 us -> 0.03 us  [body(): lax.dynamic_index_in_dim(vec_view, w, 4, keepdims=False)]
    ppermute x4 -> x0, local copies, waits for them, and re-layouts: 12.2 us -> none  [the longest x3 11 us: cores(): self.received = lax.ppermute(self.pick(1 - c), 'c', SWAP)]
    dot_general x4 -> x0, matrix products: 11.8 us -> none  [weight_grad(): lax.dot_general(left, gradient, (((0,), (0,)), ((), ())), preferred_eleme...]
  transfers between devices with their start and end apart: 69 -> 64, of which waited for: 24 -> 26; matrix products, arithmetic and copies ran while one was open for 17% -> 15% of each run, Pallas kernels for 12% -> 26%
where the time goes in v3:
time: 581 us; the launch traced here: 573 us
  Pallas kernels  199 us (34%)
  waiting for transfers between devices  95.7 us (16%)
  blocking collectives  78.4 us (13%)
  other arithmetic  66.7 us (11%)
  local copies, waits for them, and re-layouts  59.6 us (10%)
  starting transfers between devices  58 us (10%)
  between operations  16.1 us (3%)
    pallas_call x21, Pallas kernels, run(): pl.pallas_call(body, grid=(grid,), in_specs=in_specs, out_specs=out_specs...  199 us
    ppermute x28, waiting for transfers between devices, by_bit(): lax.ppermute(block, 'dp', [(i, i ^ bit) for i in range(lax.axis_size('dp'...  74.5 us
    all_gather x4, blocking collectives, chain(): all_states = lax.all_gather(mine.astype(BF16), SEQ).astype(F32)  57 us
    ppermute x28, starting transfers between devices, by_bit(): lax.ppermute(block, 'dp', [(i, i ^ bit) for i in range(lax.axis_size('dp'...  34.9 us
    all_gather x1, blocking collectives, gather_seq(): return lax.all_gather(after(part, *gate), SEQ, axis=0, tiled=True)  21.4 us
    unnamed x190, local copies, waits for them, and re-layouts  14.7 us
    ppermute x8, starting transfers between devices, from_behind(): return lax.ppermute(block, SEQ, route)  13.3 us
    convert_element_type x7, other arithmetic, first(): sum((self.part(a, *place) for a in terms)).astype(BF16)  12 us
  transfers between devices with their start and end apart: 64, of which 26 were waited for; matrix products, arithmetic and copies ran while one was open for 15% of the time, Pallas kernels for 26%

profile of v3, /device:TPU:0, one launch (start us, length us, event | category | flops | bytes accessed | tf_op | source)
XLA Modules:
  0.0 573.2 jit_solution(6841388448192504550)
XLA Ops:
  19.9 21.4 %all_gather.36.refs_5_.refs_16_ = bf16[192,2432]{1,0:T(8,128)(2,1)S(1)} all-gather(bf16[24,2432]{1,0:T(8,128)(2,1)S(1)} %fusion.9), channel_id=1, replica_groups=mesh['dp'=4,'z'=4,'c'=2] {'z','c'}, dimensions={0}, use_global_device_ids=true | all-gather | bytes 1050624 | tf_op jit(solution)/shard_map/all_gather | solution.py:790
  44.2 10.2 %collective-permute-done.1.refs_6_.refs_17_ = bf16[96,2432]{1,0:T(8,128)(2,1)S(1)} collective-permute-done((bf16[96,2432]{1,0:T(8,128)(2,1)S(1)}, bf16[96,2432]{1,0:T(8,128)(2,1)S(1)}, u32[]{:S(2)}, u32[]{:S(2)}) %collective-permute-start.1) | collective-permute-done | bytes 466976 | tf_op jit(solution)/shard_map/ppermute | solution.py:782
  69.7 9.6 %collective-permute-done.2.refs_7_.refs_18_ = bf16[2,96,2432]{2,1,0:T(8,128)(2,1)S(1)} collective-permute-done((bf16[2,96,2432]{2,1,0:T(8,128)(2,1)}, bf16[2,96,2432]{2,1,0:T(8,128)(2,1)S(1)}, u32[]{:S(2)}, u32[]{:S(2)}) %collective-permute-start.2) | collective-permute-done | bytes 933920 | tf_op jit(solution)/shard_map/ppermute | solution.py:782
  92.6 10.5 %k_time_in.2 = (bf16[512,768]{1,0:T(8,128)(2,1)}, bf16[512,768]{1,0:T(8,128)(2,1)}, bf16[512,768]{1,0:T(8,128)(2,1)}, f32[512,768]{1,0:T(8,128)}, bf16[512,768]{...) custom-call(s32[4,8]{1,0:T(4,128)} %refs_0_.35, ...), custom_call_target="tpu_custom_call" | custom-call | flops 90596968 | bytes 786432 | tf_op jit(solution)/shard_map/k_time_in/pallas_call | solution.py:608
  109.3 14.2 %all-gather = bf16[32,2,768]{2,1,0:T(2,128)(2,1)S(1)} all-gather(bf16[4,2,768]{2,1,0:T(2,128)(2,1)S(1)} %convert_element_type.489), channel_id=2, replica_groups=mesh['dp'=4,'z'=4,'c'=2] {'z','c'}, dimensions={0}, use_global_device_ids=true | all-gather | bytes 110592 | tf_op jit(solution)/shard_map/all_gather | solution.py:907
  125.0 6.3 %k_time_out.2 = (bf16[512,768]{1,0:T(8,128)(2,1)}, f32[512,768]{1,0:T(8,128)}) custom-call(s32[4,8]{1,0:T(4,128)} %refs_0_.35, s32[3]{0:T(128)} %pad_add_fusion.refs_1_, bf16[512,768]{1,0:T(8,128)(2,1)} %bitcast.203, f32[512,768]{1,0:T(8,128)} %get-tuple-element.224.refs_3_.refs_7_.refs_5_, bf16[512,768]{1,0:T(8,128)(2,1)} %get-tuple-element.225.refs_4_.refs_8_.refs_6_, ...), custom_call_target="tpu_custom_call" | custom-call | flops 30198988 | bytes 589824 | tf_op jit(solution)/shard_map/k_time_out/pallas_call | solution.py:608
  142.2 6.0 %collective-permute-done.14.refs_6_.refs_11_.refs_14_.refs_17_ = bf16[96,3072]{1,0:T(8,128)(2,1)S(1)} collective-permute-done((bf16[96,3072]{1,0:T(8,128)(2,1)S(1)}, bf16[96,3072]{1,0:T(8,128)(2,1)S(1)}, u32[]{:S(2)}, u32[]{:S(2)}) %collective-permute-start.14) | collective-permute-done | bytes 589856 | tf_op jit(solution)/shard_map/ppermute | solution.py:782
  156.1 15.4 %k_feed.2 = (bf16[512,768]{1,0:T(8,128)(2,1)}, bf16[512,768]{1,0:T(8,128)(2,1)}, bf16[512,3072]{1,0:T(8,128)(2,1)}, bf16[512,3072]{1,0:T(8,128)(2,1)}, bf16[512,...) custom-call(s32[4,8]{1,0:T(4,128)} %refs_0_.35, s32[3]{0:T(128)} %pad_add_fusion.refs_1_, ...), custom_call_target="tpu_custom_call" | custom-call | flops 271790912 | bytes 1179648 | tf_op jit(solution)/shard_map/k_feed/pallas_call | solution.py:608
  190.0 10.6 %k_time_in.3 = (bf16[512,768]{1,0:T(8,128)(2,1)}, bf16[512,768]{1,0:T(8,128)(2,1)}, bf16[512,768]{1,0:T(8,128)(2,1)}, f32[512,768]{1,0:T(8,128)}, bf16[512,768]{...) custom-call(s32[4,8]{1,0:T(4,128)} %refs_0_.35, ...), custom_call_target="tpu_custom_call" | custom-call | flops 90596968 | bytes 786432 | tf_op jit(solution)/shard_map/k_time_in/pallas_call | solution.py:608
  204.5 14.3 %all-gather.1 = bf16[32,2,768]{2,1,0:T(2,128)(2,1)S(1)} all-gather(bf16[4,2,768]{2,1,0:T(2,128)(2,1)S(1)} %convert_element_type.491), channel_id=3, replica_groups=mesh['dp'=4,'z'=4,'c'=2] {'z','c'}, dimensions={0}, use_global_device_ids=true | all-gather | bytes 110592 | tf_op jit(solution)/shard_map/all_gather | solution.py:907
  219.4 6.6 %k_time_out.3 = (bf16[512,768]{1,0:T(8,128)(2,1)}, f32[512,768]{1,0:T(8,128)}) custom-call(s32[4,8]{1,0:T(4,128)} %refs_0_.35, s32[3]{0:T(128)} %pad_add_fusion.refs_1_, f32[512,768]{1,0:T(8,128)} %get-tuple-element.252.refs_2_.refs_0_, f32[512,768]{1,0:T(8,128)} %get-tuple-element.255.refs_3_.refs_7_.refs_5_, ...), custom_call_target="tpu_custom_call" | custom-call | flops 30198988 | bytes 589824 | tf_op jit(solution)/shard_map/k_time_out/pallas_call | solution.py:608
  239.6 15.4 %k_feed.3 = (bf16[512,768]{1,0:T(8,128)(2,1)}, bf16[512,768]{1,0:T(8,128)(2,1)}, bf16[512,3072]{1,0:T(8,128)(2,1)}, bf16[512,3072]{1,0:T(8,128)(2,1)}, bf16[512,...) custom-call(s32[4,8]{1,0:T(4,128)} %refs_0_.35, s32[3]{0:T(128)} %pad_add_fusion.refs_1_, ...), custom_call_target="tpu_custom_call" | custom-call | flops 271790912 | bytes 1179648 | tf_op jit(solution)/shard_map/k_feed/pallas_call | solution.py:608
  255.0 15.3 %k_feed_back.2 = (bf16[512,768]{1,0:T(8,128)(2,1)}, bf16[512,768]{1,0:T(8,128)(2,1)}, bf16[512,3072]{1,0:T(8,128)(2,1)}, bf16[512,768]{1,0:T(8,128)(2,1)}, f32[4,768]{1,0:T(4,128)}, /*index=5*/f32[8,768]{1,0:T(8,128)}) custom-call(s32[4,8]{1,0:T(4,128)} %refs_0_.35, s32[3]{0:T(128)} %pad_add_fusion.refs_1_, bf16[512,768]{1,0:T(8,128)(2,1)} %bitcast.211, ...), custom_call_target="tpu_custom_call" | custom-call | flops 271790912 | bytes 1179648 | tf_op jit(solution)/shard_map/k_feed_back/pallas_call | solution.py:608
  270.3 11.9 %k_flat.1 = bf16[768,6144]{1,0:T(8,128)(2,1)} custom-call(bf16[512,768]{1,0:T(8,128)(2,1)} %get-tuple-element.277.refs_0_, bf16[512,3072]{1,0:T(8,128)(2,1)} %get-tuple-element.278.refs_1_, bf16[512,3072]{1,0:T(8,128)(2,1)} %get-tuple-element.279.refs_2_, bf16[512,768]{1,0:T(8,128)(2,1)} %get-tuple-element.280.refs_3_), custom_call_target="tpu_custom_call" | custom-call | flops 241591904 | bytes 1101004 | tf_op jit(solution)/shard_map/k_flat/pallas_call | solution.py:608
  286.6 12.8 %k_mid_back.2 = (f32[512,768]{1,0:T(8,128)}, bf16[512,768]{1,0:T(8,128)(2,1)}, bf16[512,768]{1,0:T(8,128)(2,1)}, bf16[512,768]{1,0:T(8,128)(2,1)}, bf16[512,768]...) custom-call(s32[4,8]{1,0:T(4,128)} %refs_0_.35, ...), custom_call_target="tpu_custom_call" | custom-call | flops 30198988 | bytes 983040 | tf_op jit(solution)/shard_map/k_mid_back/pallas_call | solution.py:608
  299.4 6.3 %k_halves_apart.4 = (bf16[4,4,3,24,768]{4,3,2,1,0:T(8,128)(2,1)}, bf16[4,4,3,24,768]{4,3,2,1,0:T(8,128)(2,1)}) custom-call(s32[4,8]{1,0:T(4,128)} %refs_0_.35, s32[3]{0:T(128)} %pad_add_fusion.refs_1_, bf16[512,768]{1,0:T(8,128)(2,1)} %get-tuple-element.287.refs_2_, bf16[512,768]{1,0:T(8,128)(2,1)} %get-tuple-element.288.refs_3_, ...), custom_call_target="tpu_custom_call" | custom-call | flops 90596968 | bytes 412876 | tf_op jit(solution)/shard_map/k_halves_apart/pallas_call | solution.py:608
  308.3 14.1 %all-gather.2 = bf16[32,2,768]{2,1,0:T(2,128)(2,1)S(1)} all-gather(bf16[4,2,768]{2,1,0:T(2,128)(2,1)S(1)} %convert_element_type.498), channel_id=4, replica_groups=mesh['dp'=4,'z'=4,'c'=2] {'z','c'}, dimensions={0}, use_global_device_ids=true | all-gather | bytes 110592 | tf_op jit(solution)/shard_map/all_gather | solution.py:907
  323.2 10.6 %k_time_back.2 = (bf16[512,768]{1,0:T(8,128)(2,1)}, bf16[512,768]{1,0:T(8,128)(2,1)}, bf16[512,768]{1,0:T(8,128)(2,1)}, f32[2,2,768]{2,1,0:T(2,128)}, f32[8,768]{1,0:T(8,128)}) custom-call(s32[4,8]{1,0:T(4,128)} %refs_0_.35, s32[3]{0:T(128)} %pad_add_fusion.refs_1_, f32[512,768]{1,0:T(8,128)} %get-tuple-element.252.refs_2_.refs_0_, ...), custom_call_target="tpu_custom_call" | custom-call | flops 90596968 | bytes 983040 | tf_op jit(solution)/shard_map/k_time_back/pallas_call | solution.py:608
  333.8 5.1 k_halves_apart.5
  349.5 4.0 k_norm_back.2
  353.5 15.7 %k_feed_back.3 = (bf16[512,768]{1,0:T(8,128)(2,1)}, bf16[512,768]{1,0:T(8,128)(2,1)}, bf16[512,3072]{1,0:T(8,128)(2,1)}, bf16[512,768]{1,0:T(8,128)(2,1)}, f32[4,768]{1,0:T(4,128)}, /*index=5*/f32[8,768]{1,0:T(8,128)}) custom-call(s32[4,8]{1,0:T(4,128)} %refs_0_.35, s32[3]{0:T(128)} %pad_add_fusion.refs_1_, f32[512,768]{1,0:T(8,128)} %get-tuple-element.304.refs_2_.refs_5_, ...), custom_call_target="tpu_custom_call" | custom-call | flops 271790912 | bytes 1179648 | tf_op jit(solution)/shard_map/k_feed_back/pallas_call | solution.py:608
  376.1 7.0 %k_halves_blocks.2 = (bf16[4,4,4,24,768]{4,3,2,1,0:T(8,128)(2,1)}, bf16[4,4,4,24,768]{4,3,2,1,0:T(8,128)(2,1)}) custom-call(s32[4,8]{1,0:T(4,128)} %refs_0_.35, s32[3]{0:T(128)} %pad_add_fusion.refs_1_, bf16[512,3072]{1,0:T(8,128)(2,1)} %get-tuple-element.322.refs_2_, bf16[512,768]{1,0:T(8,128)(2,1)} %get-tuple-element.323.refs_3_), custom_call_target="tpu_custom_call" | custom-call | flops 120795952 | bytes 550502 | tf_op jit(solution)/shard_map/k_halves_blocks/pallas_call | solution.py:608
  384.3 7.0 %k_halves_blocks.3 = (bf16[4,4,4,24,768]{4,3,2,1,0:T(8,128)(2,1)}, bf16[4,4,4,24,768]{4,3,2,1,0:T(8,128)(2,1)}) custom-call(s32[4,8]{1,0:T(4,128)} %refs_0_.35, s32[3]{0:T(128)} %pad_add_fusion.refs_1_, bf16[512,768]{1,0:T(8,128)(2,1)} %get-tuple-element.325.refs_2_, bf16[512,3072]{1,0:T(8,128)(2,1)} %get-tuple-element.328.refs_3_), custom_call_target="tpu_custom_call" | custom-call | flops 120795952 | bytes 550502 | tf_op jit(solution)/shard_map/k_halves_blocks/pallas_call | solution.py:608
  403.4 12.9 %k_mid_back.3 = (f32[512,768]{1,0:T(8,128)}, bf16[512,768]{1,0:T(8,128)(2,1)}, bf16[512,768]{1,0:T(8,128)(2,1)}, bf16[512,768]{1,0:T(8,128)(2,1)}, bf16[512,768]...) custom-call(s32[4,8]{1,0:T(4,128)} %refs_0_.35, ...), custom_call_target="tpu_custom_call" | custom-call | flops 30198988 | bytes 983040 | tf_op jit(solution)/shard_map/k_mid_back/pallas_call | solution.py:608
  416.3 6.2 %k_halves_apart.6 = (bf16[4,4,3,24,768]{4,3,2,1,0:T(8,128)(2,1)}, bf16[4,4,3,24,768]{4,3,2,1,0:T(8,128)(2,1)}) custom-call(s32[4,8]{1,0:T(4,128)} %refs_0_.35, s32[3]{0:T(128)} %pad_add_fusion.refs_1_, bf16[512,768]{1,0:T(8,128)(2,1)} %get-tuple-element.344.refs_2_, bf16[512,768]{1,0:T(8,128)(2,1)} %get-tuple-element.345.refs_3_, ...), custom_call_target="tpu_custom_call" | custom-call | flops 90596968 | bytes 412876 | tf_op jit(solution)/shard_map/k_halves_apart/pallas_call | solution.py:608
  445.3 14.4 %all-gather.3 = bf16[32,2,768]{2,1,0:T(2,128)(2,1)S(1)} all-gather(bf16[4,2,768]{2,1,0:T(2,128)(2,1)S(1)} %convert_element_type.520), channel_id=5, replica_groups=mesh['dp'=4,'z'=4,'c'=2] {'z','c'}, dimensions={0}, use_global_device_ids=true | all-gather | bytes 110592 | tf_op jit(solution)/shard_map/all_gather | solution.py:907
  460.4 10.0 %k_time_back.3 = (bf16[512,768]{1,0:T(8,128)(2,1)}, bf16[512,768]{1,0:T(8,128)(2,1)}, bf16[512,768]{1,0:T(8,128)(2,1)}, f32[2,2,768]{2,1,0:T(2,128)}, f32[8,768]{1,0:T(8,128)}) custom-call(s32[4,8]{1,0:T(4,128)} %refs_0_.35, s32[3]{0:T(128)} %pad_add_fusion.refs_1_, bf16[512,768]{1,0:T(8,128)(2,1)} %bitcast.204, f32[2,2,768]{2,1,0:T(2,128)} %reshape.497.refs_3_, ...), custom_call_target="tpu_custom_call" | custom-call | flops 90596968 | bytes 983040 | tf_op jit(solution)/shard_map/k_time_back/pallas_call | solution.py:608
  476.6 5.2 k_halves_apart.7
  487.7 4.2 k_norm_back.3
  495.9 15.5 %collective-permute-done.52 = bf16[1,2,4,2,24,768]{5,4,3,2,1,0:T(8,128)(2,1)S(1)} collective-permute-done((bf16[1,2,4,2,24,768]{5,4,3,2,1,0:T(8,128)(2,1)}, bf16[1,2,4,2,24,768]{5,4,3,2,1,0:T(8,128)(2,1)S(1)}, u32[]{:S(2)}, u32[]{:S(2)}) %collective-permute-start.52) | collective-permute-done | bytes 589856 | tf_op jit(solution)/shard_map/ppermute | solution.py:782
  523.2 5.8 %collective-permute-done.53 = bf16[1,1,4,2,24,768]{5,4,3,2,1,0:T(8,128)(2,1)S(1)} collective-permute-done((bf16[1,1,4,2,24,768]{5,4,3,2,1,0:T(8,128)(2,1)S(1)}, bf16[1,1,4,2,24,768]{5,4,3,2,1,0:T(8,128)(2,1)S(1)}, u32[]{:S(2)}, u32[]{:S(2)}) %collective-permute-start.53) | collective-permute-done | bytes 294944 | tf_op jit(solution)/shard_map/ppermute | solution.py:782
  548.2 9.1 %reduce-scatter.13.cloned.1.call-done = bf16[144,768]{1,0:T(8,128)(2,1)} async-done(((bf16[576,768]{1,0:T(8,128)(2,1)}), bf16[144,768]{1,0:T(8,128)(2,1)}) %reduce-scatter.13.cloned.1.call-update) | async-done | bytes 221200 | tf_op jit(solution)/shard_map/reduce_scatter | solution.py:889
  (493 shorter events, 223.7 us)
Async XLA Ops:
  7.2 53.0 %all-gather.8.cloned.1.call-start = ((), (), s32[]{:S(2)}) async-start(), calls=%async_computation.4 | async-start | bytes 3317760 | tf_op jit(solution)/shard_map/all_gather | solution.py:790
  16.4 73.6 %all-gather.10.cloned.1.call-start = ((), (), s32[]{:S(2)}) async-start(), calls=%async_computation.5 | async-start | bytes 1327104 | tf_op jit(solution)/shard_map/all_gather | solution.py:790
  17.3 46.2 %collective-permute-start = (bf16[4,768]{1,0:T(4,128)(2,1)S(1)}, bf16[4,768]{1,0:T(4,128)(2,1)S(1)}, u32[]{:S(2)}, u32[]{:S(2)}) collective-permute-start(bf16[4,768]{1,0:T(4,128)(2,1)S(1)} %bitcast.261), channel_id=1, source_target_pairs={{0,1},{1,2},{2,3},{3,4},{4,5},{5,6},{6,7},{8,9},{9,10},{10,11},{11... | collective-permute-start | bytes 18440 | tf_op jit(solution)/shard_map/ppermute | solution.py:902
  55.4 23.8 %collective-permute-start.2 = (bf16[2,96,2432]{2,1,0:T(8,128)(2,1)}, bf16[2,96,2432]{2,1,0:T(8,128)(2,1)S(1)}, u32[]{:S(2)}, u32[]{:S(2)}) collective-permute-start(bf16[2,96,2432]{2,1,0:T(8,128)(2,1)} %pad_maximum_fusion.6), channel_id=1, source_target_pairs={{0,16},{8,24},{16,0},{24,8},{1,17},{9,25},{17,1},{25,9},{2,18},{10... | collective-permute-start | bytes 2801672 | tf_op jit(solution)/shard_map/ppermute | solution.py:782
  61.3 19.8 %collective-permute-start.4 = (bf16[96,3840]{1,0:T(8,128)(2,1)S(1)}, bf16[96,3840]{1,0:T(8,128)(2,1)S(1)}, u32[]{:S(2)}, u32[]{:S(2)}) collective-permute-start(bf16[96,3840]{1,0:T(8,128)(2,1)S(1)} %constant_dynamic-slice_fusion.10), channel_id=1, source_target_pairs={{0,8},{8,0},{16,24},{24,16},{1,9},{9,1},{17,25},{25,17},{2,10},{10... | collective-permute-start | bytes 2211848 | tf_op jit(solution)/shard_map/ppermute | solution.py:782
  66.7 84.3 %all-gather.12.cloned.1.call-start = ((), (), s32[]{:S(2)}) async-start(), calls=%async_computation.6 | async-start | bytes 2985984 | tf_op jit(solution)/shard_map/all_gather | solution.py:790
  82.4 20.7 %collective-permute-start.7 = (bf16[2,96,768]{2,1,0:T(8,128)(2,1)}, bf16[2,96,768]{2,1,0:T(8,128)(2,1)}, u32[]{:S(2)}, u32[]{:S(2)}) collective-permute-start(bf16[2,96,768]{2,1,0:T(8,128)(2,1)} %pad_maximum_fusion.11), channel_id=1, source_target_pairs={{0,8},{8,0},{16,24},{24,16},{1,9},{9,1},{17,25},{25,17},{2,10},{10... | collective-permute-start | bytes 884744 | tf_op jit(solution)/shard_map/ppermute | solution.py:782
  85.8 17.3 %collective-permute-start.8 = (bf16[96,3072]{1,0:T(8,128)(2,1)}, bf16[96,3072]{1,0:T(8,128)(2,1)}, u32[]{:S(2)}, u32[]{:S(2)}) collective-permute-start(bf16[96,3072]{1,0:T(8,128)(2,1)} %constant_dynamic-slice_fusion.9), channel_id=1, source_target_pairs={{0,16},{8,24},{16,0},{24,8},{1,17},{9,25},{17,1},{25,9},{2,18},{10... | collective-permute-start | bytes 1769480 | tf_op jit(solution)/shard_map/ppermute | solution.py:782
  90.1 338.4 %reduce-scatter.7.cloned.1.call-start = ((), (), s32[]{:S(2)}) async-start(), calls=%async_computation.7 | async-start | bytes 9732096 | tf_op jit(solution)/shard_map/reduce_scatter | solution.py:1037
  105.5 27.7 %collective-permute-start.11 = (bf16[2,96,3072]{2,1,0:T(8,128)(2,1)}, bf16[2,96,3072]{2,1,0:T(8,128)(2,1)}, u32[]{:S(2)}, u32[]{:S(2)}) collective-permute-start(bf16[2,96,3072]{2,1,0:T(8,128)(2,1)} %pad_maximum_fusion.2), channel_id=1, source_target_pairs={{0,8},{8,0},{16,24},{24,16},{1,9},{9,1},{17,25},{25,17},{2,10},{10... | collective-permute-start | bytes 3538952 | tf_op jit(solution)/shard_map/ppermute | solution.py:782
  107.4 33.7 %collective-permute-start.13 = (bf16[2,96,3840]{2,1,0:T(8,128)(2,1)}, bf16[2,96,3840]{2,1,0:T(8,128)(2,1)}, u32[]{:S(2)}, u32[]{:S(2)}) collective-permute-start(bf16[2,96,3840]{2,1,0:T(8,128)(2,1)} %pad_maximum_fusion), channel_id=1, source_target_pairs={{0,16},{8,24},{16,0},{24,8},{1,17},{9,25},{17,1},{25,9},{2,18},{10... | collective-permute-start | bytes 4423688 | tf_op jit(solution)/shard_map/ppermute | solution.py:782
  107.9 16.3 %collective-permute-start.9 = (bf16[96,768]{1,0:T(8,128)(2,1)S(1)}, bf16[96,768]{1,0:T(8,128)(2,1)S(1)}, u32[]{:S(2)}, u32[]{:S(2)}) collective-permute-start(bf16[96,768]{1,0:T(8,128)(2,1)S(1)} %collective-permute-done.3.refs_11_.refs_14_), channel_id=1, source_target_pairs={{0,1},{1,0},{2,3},{3,2},{4,5},{5,4},{6,7},{7,6},{8,9},{9,8},{10,11... | collective-permute-start | bytes 442376 | tf_op jit(solution)/shard_map/ppermute | solution.py:827
  108.0 16.2 %collective-permute-start.10 = (bf16[2,96,768]{2,1,0:T(8,128)(2,1)}, bf16[2,96,768]{2,1,0:T(8,128)(2,1)S(1)}, u32[]{:S(2)}, u32[]{:S(2)}) collective-permute-start(bf16[2,96,768]{2,1,0:T(8,128)(2,1)} %collective-permute-done.7.refs_12_.refs_15_), channel_id=1, source_target_pairs={{0,1},{1,0},{2,3},{3,2},{4,5},{5,4},{6,7},{7,6},{8,9},{9,8},{10,11... | collective-permute-start | bytes 884744 | tf_op jit(solution)/shard_map/ppermute | solution.py:828
  149.5 26.7 %collective-permute-start.20 = (bf16[2,96,3072]{2,1,0:T(8,128)(2,1)}, bf16[2,96,3072]{2,1,0:T(8,128)(2,1)}, u32[]{:S(2)}, u32[]{:S(2)}) collective-permute-start(bf16[2,96,3072]{2,1,0:T(8,128)(2,1)} %pad_maximum_fusion.3), channel_id=1, source_target_pairs={{0,16},{8,24},{16,0},{24,8},{1,17},{9,25},{17,1},{25,9},{2,18},{10... | collective-permute-start | bytes 3538952 | tf_op jit(solution)/shard_map/ppermute | solution.py:782
  153.0 19.7 %collective-permute-start.19 = (bf16[96,3840]{1,0:T(8,128)(2,1)}, bf16[96,3840]{1,0:T(8,128)(2,1)}, u32[]{:S(2)}, u32[]{:S(2)}) collective-permute-start(bf16[96,3840]{1,0:T(8,128)(2,1)} %constant_dynamic-slice_fusion), channel_id=1, source_target_pairs={{0,8},{8,0},{16,24},{24,16},{1,9},{9,1},{17,25},{25,17},{2,10},{10... | collective-permute-start | bytes 2211848 | tf_op jit(solution)/shard_map/ppermute | solution.py:782
  182.1 18.4 %collective-permute-start.24 = (bf16[96,3072]{1,0:T(8,128)(2,1)}, bf16[96,3072]{1,0:T(8,128)(2,1)}, u32[]{:S(2)}, u32[]{:S(2)}) collective-permute-start(bf16[96,3072]{1,0:T(8,128)(2,1)} %constant_dynamic-slice_fusion.8), channel_id=1, source_target_pairs={{0,16},{8,24},{16,0},{24,8},{1,17},{9,25},{17,1},{25,9},{2,18},{10... | collective-permute-start | bytes 1769480 | tf_op jit(solution)/shard_map/ppermute | solution.py:782
  188.2 41.5 %collective-permute-start.26 = (bf16[2,96,3840]{2,1,0:T(8,128)(2,1)}, bf16[2,96,3840]{2,1,0:T(8,128)(2,1)}, u32[]{:S(2)}, u32[]{:S(2)}) collective-permute-start(bf16[2,96,3840]{2,1,0:T(8,128)(2,1)} %pad_maximum_fusion.1), channel_id=1, source_target_pairs={{0,16},{8,24},{16,0},{24,8},{1,17},{9,25},{17,1},{25,9},{2,18},{10... | collective-permute-start | bytes 4423688 | tf_op jit(solution)/shard_map/ppermute | solution.py:782
  202.8 28.1 %collective-permute-start.25 = (bf16[2,96,3072]{2,1,0:T(8,128)(2,1)}, bf16[2,96,3072]{2,1,0:T(8,128)(2,1)}, u32[]{:S(2)}, u32[]{:S(2)}) collective-permute-start(bf16[2,96,3072]{2,1,0:T(8,128)(2,1)} %pad_maximum_fusion.4), channel_id=1, source_target_pairs={{0,8},{8,0},{16,24},{24,16},{1,9},{9,1},{17,25},{25,17},{2,10},{10... | collective-permute-start | bytes 3538952 | tf_op jit(solution)/shard_map/ppermute | solution.py:782
  282.3 189.4 %reduce-scatter.9.cloned.1.call-start = ((), (), s32[]{:S(2)}) async-start(), calls=%async_computation.8 | async-start | bytes 921600 | tf_op jit(solution)/shard_map/reduce_scatter | solution.py:889
  305.8 17.4 %collective-permute-start.33 = (bf16[2,2,4,3,24,768]{5,4,3,2,1,0:T(8,128)(2,1)}, bf16[2,2,4,3,24,768]{5,4,3,2,1,0:T(8,128)(2,1)}, u32[]{:S(2)}, u32[]{:S(2)}) collective-permute-start(bf16[2,2,4,3,24,768]{5,4,3,2,1,0:T(8,128)(2,1)} %bitcast.265), channel_id=1, source_target_pairs={{0,1},{1,0},{2,3},{3,2},{4,5},{5,4},{6,7},{7,6},{8,9},{9,8},{10,11... | collective-permute-start | bytes 5308424 | tf_op jit(solution)/shard_map/ppermute | solution.py:852
  340.9 30.3 %collective-permute-start.36 = (bf16[2,1,4,3,24,768]{5,4,3,2,1,0:T(8,128)(2,1)S(1)}, bf16[2,1,4,3,24,768]{5,4,3,2,1,0:T(8,128)(2,1)}, u32[]{:S(2)}, u32[]{:S(2)}) collective-permute-start(bf16[2,1,4,3,24,768]{5,4,3,2,1,0:T(8,128)(2,1)S(1)} %add_convert_fusion.3), channel_id=1, source_target_pairs={{0,8},{8,0},{16,24},{24,16},{1,9},{9,1},{17,25},{25,17},{2,10},{10... | collective-permute-start | bytes 2654216 | tf_op jit(solution)/shard_map/ppermute | solution.py:782
  344.0 27.2 %collective-permute-start.37 = (bf16[1,2,4,2,24,768]{5,4,3,2,1,0:T(8,128)(2,1)}, bf16[1,2,4,2,24,768]{5,4,3,2,1,0:T(8,128)(2,1)}, u32[]{:S(2)}, u32[]{:S(2)}) collective-permute-start(bf16[1,2,4,2,24,768]{5,4,3,2,1,0:T(8,128)(2,1)} %add_convert_fusion.9), channel_id=1, source_target_pairs={{0,16},{8,24},{16,0},{24,8},{1,17},{9,25},{17,1},{25,9},{2,18},{10... | collective-permute-start | bytes 1769480 | tf_op jit(solution)/shard_map/ppermute | solution.py:782
  372.7 18.6 %collective-permute-start.40 = (bf16[1,1,4,3,24,768]{5,4,3,2,1,0:T(8,128)(2,1)S(1)}, bf16[1,1,4,3,24,768]{5,4,3,2,1,0:T(8,128)(2,1)S(1)}, u32[]{:S(2)}, u32[]{:S(2)}) collective-permute-start(bf16[1,1,4,3,24,768]{5,4,3,2,1,0:T(8,128)(2,1)S(1)} %add_convert_fusion.13), channel_id=1, source_target_pairs={{0,16},{8,24},{16,0},{24,8},{1,17},{9,25},{17,1},{25,9},{2,18},{10... | collective-permute-start | bytes 1327112 | tf_op jit(solution)/shard_map/ppermute | solution.py:782
  394.6 30.9 %collective-permute-start.43 = (bf16[2,1,4,4,24,768]{5,4,3,2,1,0:T(8,128)(2,1)}, bf16[2,1,4,4,24,768]{5,4,3,2,1,0:T(8,128)(2,1)}, u32[]{:S(2)}, u32[]{:S(2)}) collective-permute-start(bf16[2,1,4,4,24,768]{5,4,3,2,1,0:T(8,128)(2,1)} %add_convert_fusion.1), channel_id=1, source_target_pairs={{0,8},{8,0},{16,24},{24,16},{1,9},{9,1},{17,25},{25,17},{2,10},{10... | collective-permute-start | bytes 3538952 | tf_op jit(solution)/shard_map/ppermute | solution.py:782
  398.0 30.4 %collective-permute-start.44 = (bf16[1,2,4,4,24,768]{5,4,3,2,1,0:T(8,128)(2,1)}, bf16[1,2,4,4,24,768]{5,4,3,2,1,0:T(8,128)(2,1)}, u32[]{:S(2)}, u32[]{:S(2)}) collective-permute-start(bf16[1,2,4,4,24,768]{5,4,3,2,1,0:T(8,128)(2,1)} %add_convert_fusion), channel_id=1, source_target_pairs={{0,16},{8,24},{16,0},{24,8},{1,17},{9,25},{17,1},{25,9},{2,18},{10... | collective-permute-start | bytes 3538952 | tf_op jit(solution)/shard_map/ppermute | solution.py:782
  433.6 87.3 %reduce-scatter.11.cloned.1.call-start = ((), (), s32[]{:S(2)}) async-start(), calls=%async_computation.9 | async-start | bytes 1474560 | tf_op jit(solution)/shard_map/reduce_scatter | solution.py:889
  436.7 35.0 %collective-permute-start.46 = (bf16[2,1,4,3,24,768]{5,4,3,2,1,0:T(8,128)(2,1)}, bf16[2,1,4,3,24,768]{5,4,3,2,1,0:T(8,128)(2,1)}, u32[]{:S(2)}, u32[]{:S(2)}) collective-permute-start(bf16[2,1,4,3,24,768]{5,4,3,2,1,0:T(8,128)(2,1)} %add_convert_fusion.2), channel_id=1, source_target_pairs={{0,8},{8,0},{16,24},{24,16},{1,9},{9,1},{17,25},{25,17},{2,10},{10... | collective-permute-start | bytes 2654216 | tf_op jit(solution)/shard_map/ppermute | solution.py:782
  440.2 30.2 %collective-permute-start.47 = (bf16[1,1,4,4,24,768]{5,4,3,2,1,0:T(8,128)(2,1)}, bf16[1,1,4,4,24,768]{5,4,3,2,1,0:T(8,128)(2,1)}, u32[]{:S(2)}, u32[]{:S(2)}) collective-permute-start(bf16[1,1,4,4,24,768]{5,4,3,2,1,0:T(8,128)(2,1)} %add_convert_fusion.8), channel_id=1, source_target_pairs={{0,16},{8,24},{16,0},{24,8},{1,17},{9,25},{17,1},{25,9},{2,18},{10... | collective-permute-start | bytes 1769480 | tf_op jit(solution)/shard_map/ppermute | solution.py:782
  443.8 27.8 %collective-permute-start.48 = (bf16[1,1,4,4,24,768]{5,4,3,2,1,0:T(8,128)(2,1)}, bf16[1,1,4,4,24,768]{5,4,3,2,1,0:T(8,128)(2,1)}, u32[]{:S(2)}, u32[]{:S(2)}) collective-permute-start(bf16[1,1,4,4,24,768]{5,4,3,2,1,0:T(8,128)(2,1)} %add_convert_fusion.7), channel_id=1, source_target_pairs={{0,8},{8,0},{16,24},{24,16},{1,9},{9,1},{17,25},{25,17},{2,10},{10... | collective-permute-start | bytes 1769480 | tf_op jit(solution)/shard_map/ppermute | solution.py:782
  483.2 74.1 %reduce-scatter.13.cloned.1.call-start = ((), (), s32[]{:S(2)}) async-start(), calls=%async_computation.10 | async-start | bytes 1105920 | tf_op jit(solution)/shard_map/reduce_scatter | solution.py:889
  485.4 30.5 %collective-permute-start.51 = (bf16[1,1,4,3,24,768]{5,4,3,2,1,0:T(8,128)(2,1)}, bf16[1,1,4,3,24,768]{5,4,3,2,1,0:T(8,128)(2,1)}, u32[]{:S(2)}, u32[]{:S(2)}) collective-permute-start(bf16[1,1,4,3,24,768]{5,4,3,2,1,0:T(8,128)(2,1)} %add_convert_fusion.11), channel_id=1, source_target_pairs={{0,16},{8,24},{16,0},{24,8},{1,17},{9,25},{17,1},{25,9},{2,18},{10... | collective-permute-start | bytes 1327112 | tf_op jit(solution)/shard_map/ppermute | solution.py:782
  495.1 16.3 %collective-permute-start.52 = (bf16[1,2,4,2,24,768]{5,4,3,2,1,0:T(8,128)(2,1)}, bf16[1,2,4,2,24,768]{5,4,3,2,1,0:T(8,128)(2,1)S(1)}, u32[]{:S(2)}, u32[]{:S(2)}) collective-permute-start(bf16[1,2,4,2,24,768]{5,4,3,2,1,0:T(8,128)(2,1)} %add_convert_fusion.4), channel_id=1, source_target_pairs={{0,16},{8,24},{16,0},{24,8},{1,17},{9,25},{17,1},{25,9},{2,18},{10... | collective-permute-start | bytes 1769480 | tf_op jit(solution)/shard_map/ppermute | solution.py:782
  (121 other events, 924.2 us)
Sparse Core Ops, SparseCore 0:
  16.5 43.5 all-gather.7
  66.8 20.0 all-gather.9
  90.2 33.5 all-gather.11
  282.4 145.5 reduce-scatter.6
  433.7 24.0 reduce-scatter.8
  483.3 30.7 reduce-scatter.10
  531.9 25.3 reduce-scatter.12

commit v4 on v3

--- a/solution.py
+++ b/solution.py
@@ -149,7 +149,7 @@
 
 
 def k_time_in(items, T, starts, base, x, edge, vec, *refs):
-    (pieces,), (mk, mv, mr, ko, vo, ro, no, do, last, w, sems) = split_refs([items[0][0]], refs)
+    (pieces,), (mk, mv, mr, ko, vo, no, do, last, w, sems) = split_refs([items[0][0]], refs)
     D = x.shape[1]
     i = pl.program_id(0)
     copies = [
@@ -183,7 +183,6 @@
 
     ko[...] = dot_nn(mk[...], w[0])
     vo[...] = dot_nn(mv[...], w[1]).astype(vo.dtype)
-    ro[...] = dot_nn(mr[...], w[2]).astype(ro.dtype)
     for q, (local, dist, _) in enumerate(places):
         rows = slice(q * T, q * T + T)
         keeps = keeps_of(local, dist, T)
@@ -207,17 +206,27 @@
     return full_n, full_d, extra, inverse, mean
 
 
-def k_time_out(items, T, starts, base, x, key, value, recept, num, den, state, vec, *refs):
-    (pieces,), (gated, middle, w, sems) = split_refs([items[0][0]], refs)
+def k_time_out(items, T, starts, base, x, key, value, mr, num, den, state, vec, *refs):
+    (pieces,), (gated, middle, recept, w, sems) = split_refs([items[0][0]], refs)
     D = x.shape[1]
     i = pl.program_id(0)
-    copies = piece_copies(base, pieces, items[0], w, sems, 0)
+    copies = [
+        copy
+        for s, item in enumerate(items)
+        for copy in piece_copies(base, pieces, item, w.at[s], sems, 8 * s)
+    ]
 
     @pl.when(i == 0)
     def _():
         for _, copy in copies:
             copy.start()
 
+    @pl.when(i == 0)
+    def _():
+        for _, copy in copies:
+            copy.wait()
+
+    recept[...] = dot_nn(mr[...], w[0]).astype(BF16)
     for q in range(RB):
         local, dist, _ = place_of(starts, base, i * RB + q, T)
         rows = slice(q * T, q * T + T)
@@ -228,12 +237,7 @@
             )[4]
             gated[rows, c] = (jax.nn.sigmoid(recept[rows, c].astype(F32)) * mean).astype(BF16)
 
-    @pl.when(i == 0)
-    def _():
-        for _, copy in copies:
-            copy.wait()
-
-    middle[...] = x[...].astype(F32) + dot_nn(gated[...], w[...])
+    middle[...] = x[...].astype(F32) + dot_nn(gated[...], w[1])
 
 
 def feed_copies(items, base, pieces, wg, wk, wv, sems):
@@ -434,13 +438,13 @@
 
 def k_time_back(items, T, starts, base, x, edge, vec, key, value, num, den, state,
                 gkp, gvp, gno, gdo, after, gr, *refs):
-    (pieces,), (gk, gv, gn, first, sums, mixes, w, sems) = split_refs([items[0][0]], refs)
+    pieces, (gk, gv, gn, first, sums, mixes, w, sems) = split_refs(items[0], refs)
     D = x.shape[1]
     i = pl.program_id(0)
     copies = [
         copy
-        for s, item in enumerate(items)
-        for copy in piece_copies(base, pieces, item, w.at[s], sems, 8 * s)
+        for s, (group, item) in enumerate(items[1:])
+        for copy in piece_copies(base, pieces[group], item, w.at[s], sems, 8 * s)
     ]
 
     @pl.when(i == 0)
@@ -635,16 +639,16 @@
     R = N // T
     rs = rows_spec(T, D)
     pieces = weights["key"][0]
-    items = [weights[name][1] for name in ("key", "value", "recept")]
+    items = [weights[name][1] for name in ("key", "value")]
     return run(
         k_time_in, T, R // RB,
         [smem(), smem(), rs, edge_spec(D), whole_spec(vec.shape)] + anywhere(len(pieces)),
-        [rs] * 8 + [state_spec(D)],
-        [shape((N, D), BF16)] * 3 + [shape((N, D), F32)] + [shape((N, D), BF16)] * 4
+        [rs] * 7 + [state_spec(D)],
+        [shape((N, D), BF16)] * 3 + [shape((N, D), F32)] + [shape((N, D), BF16)] * 3
         + [shape((R, 2, D), F32)],
         (*place, x, edge.reshape(R // RB, RB, D), vec, *pieces),
-        6 * N * D * D, 40 * N * D,
-        weight_room([(3, D, D)], 24), items, after,
+        4 * N * D * D, 40 * N * D,
+        weight_room([(2, D, D)], 16), items, after,
     )
 
 
@@ -652,24 +656,22 @@
     N, D = x.shape
     R = N // T
     rs = rows_spec(T, D)
-    pieces, item = weights["output"]
+    pieces = weights["output"][0]
+    items = [weights[name][1] for name in ("recept", "output")]
     return run(
         k_time_out, T, R // RB,
         [smem(), smem()] + [rs] * 6 + [state_spec(D), whole_spec(vec.shape)] + anywhere(len(pieces)),
-        [rs] * 2,
-        [shape((N, D), BF16), shape((N, D), F32)],
+        [rs] * 3,
+        [shape((N, D), BF16), shape((N, D), F32), shape((N, D), BF16)],
         (*place, x, *kept, state, vec, *pieces),
-        2 * N * D * D, 30 * N * D,
-        weight_room([(D, D)], 8), [item], after,
-    )
-
-
-def feed_weights(weights):
-    keys, values = (
-        sorted(name for name in weights if name.startswith(kind)) for kind in ("feed_key", "feed_value")
-    )
+        4 * N * D * D, 30 * N * D,
+        weight_room([(2, D, D)], 16), items, after,
+    )
+
+
+def grouped(weights, names):
     groups, items = [], []
-    for name in ["gate"] + keys + values:
+    for name in names:
         pieces, item = weights[name]
         found = [k for k, group in enumerate(groups) if group is pieces]
         if not found:
@@ -678,6 +680,13 @@
         items.append((found[0], item))
     pieces = tuple(piece for group in groups for piece in group)
     return [[len(group) for group in groups]] + items, pieces
+
+
+def feed_weights(weights):
+    keys, values = (
+        sorted(name for name in weights if name.startswith(kind)) for kind in ("feed_key", "feed_value")
+    )
+    return grouped(weights, ["gate"] + keys + values)
 
 
 def feed(T, place, middle, edge, vec, weights, after=()):
@@ -744,8 +753,7 @@
     N, D = x.shape
     R = N // T
     rs = rows_spec(T, D)
-    pieces = weights["key"][0]
-    items = [weights[name][1] for name in ("key", "value", "recept")]
+    items, pieces = grouped(weights, ("key", "value", "recept"))
     return run(
         k_time_back, T, R // RB,
         [smem(), smem(), rs, edge_spec(D), whole_spec(vec.shape)]
@@ -809,12 +817,16 @@
         self.width = sum(width for _, width in names)
         self.rows = block.shape[0] // 2
 
-    def first(self, *gate):
+    def prepare(self, *gate):
         block = after(self.block, *gate)
         self.own = lax.dynamic_slice(
             block, (lax.axis_index("c") * self.rows, self.start), (self.rows, self.width)
         )
-        self.one = by_bit(self.own, self.bits[0])
+        return self.own
+
+    def first(self, *gate):
+        own = self.prepare(*gate) if gate else self.own
+        self.one = by_bit(own, self.bits[0])
         return self.one
 
     def second(self, *gate):
@@ -857,7 +869,8 @@
         y, x = d // 2, d % 2
         terms = after((self.mine, self.received), *gate)
         place = (1 - y, None) if self.bits[1] == 2 else (None, 1 - x)
-        self.got = by_bit(sum(self.part(a, *place) for a in terms).astype(BF16), self.bits[1])
+        self.sent = sum(self.part(a, *place) for a in terms).astype(BF16)
+        self.got = by_bit(self.sent, self.bits[1])
         return self.got
 
     def second(self, *gate):
@@ -927,11 +940,13 @@
     R = N // T
     rate = jnp.exp(vec[5])
     x = hook("start", x)
-    mk, mv, mr, key, value, recept, num, den, last = time_in(T, place, x, edge, vec, weights())
+    mk, mv, mr, key, value, num, den, last = time_in(T, place, x, edge, vec, weights())
     last = hook("time in", last)
     state = chain(last, starts, rate, T, True)
     state = hook("chain", state)
-    gated, middle = time_out(T, place, x, (key, value, recept, num, den), state, vec, weights())
+    gated, middle, recept = time_out(
+        T, place, x, (key, value, mr, num, den), state, vec, weights()
+    )
     middle = hook("time out", middle)
     edge_two = from_behind(middle.reshape(R, T, D)[:, -1], 1)
     edge_two = hook("edge", edge_two)
@@ -1076,25 +1091,30 @@
 
     keys = [(f"feed_key{b}", D) for b in range(blocks)]
     values = [(f"feed_value{b}", D) for b in range(blocks)]
-    time_names = [("key", D), ("value", D), ("recept", D)]
-    rest_names = [("output", D), ("gate", D)] + keys + values
-    layout = [[time_names + [("vectors", 128)], rest_names]]
-    layout += [[time_names + rest_names[:1], rest_names[1:]]] * (layers - 1)
+    time_names = [("key", D), ("value", D)]
+    out_names = [("recept", D), ("output", D)]
+    key_names = [("gate", D)] + keys
+    layout = [[time_names + [("vectors", 128)], out_names + key_names, values]]
+    layout += [[time_names + out_names, key_names + values]] * (layers - 1)
 
     vector_columns = jnp.pad(
         vectors.reshape(layers * kinds, n).T, ((0, 0), (0, 128 - layers * kinds))
     )
 
+    arguments = {0: (matrices, time_output, feed_key, feed_value)}
+
     def shard(l, names):
+        matrices, time_output, feed_key, feed_value = arguments[l]
         found = {
             "key": matrices[l, 0], "value": matrices[l, 1], "recept": matrices[l, 2],
             "gate": matrices[l, 3], "output": time_output[l], "vectors": vector_columns,
         }
+        for b in range(blocks):
+            found[f"feed_value{b}"] = feed_value[l, b * n : (b + 1) * n]
         if ("feed_key0", D) in names:
             key_blocks = by_block(feed_key[l].astype(BF16))
             for b in range(blocks):
                 found[f"feed_key{b}"] = key_blocks[:, b * D : (b + 1) * D]
-                found[f"feed_value{b}"] = feed_value[l, b * n : (b + 1) * n]
         return jnp.concatenate([found[name].astype(BF16) for name, _ in names], axis=1)
 
     def sets_of(l, k, gate, *split):
@@ -1120,17 +1140,21 @@
 
     shards = {}
     here = [[] for _ in range(layers)]
-    A = sets_of(0, 0, (), (4, XY))[0]
-    O, B, V = sets_of(0, 1, (), (1, YX), (1 + blocks, XY), (blocks, YX))
+    A = sets_of(0, 0, (), (3, XY))[0]
+    O, B = sets_of(0, 1, (), (2, YX), (1 + blocks, XY))
+    V = sets_of(0, 2, (A.block,), (blocks, YX))[0]
     here[0] = [A, O, B, V]
+    A.prepare()
     A.first()
     for l in range(1, layers):
-        here[l] = sets_of(l, 0, (B.block,), (4, XY))
-        here[l] += sets_of(l, 1, (here[l][0].block,), (1 + blocks, XY), (blocks, YX))
-    A.second()
-    O.first(A.one)
-    B.first(A.one)
-    A.cores(O.one, B.one, *[p for l in range(1, layers) for p in shards[l]])
+        arguments[l] = after(arguments[0], A.block)
+        here[l] = sets_of(l, 0, (A.one,), (4, XY))
+    for l in range(1, layers):
+        here[l] += sets_of(l, 1, (B.block,), (1 + blocks, XY), (blocks, YX))
+    A.second(O.prepare(A.block), B.prepare(A.block), *[p for l in range(1, layers) for p in shards[l]])
+    O.first()
+    B.first()
+    A.cores(O.one, B.one)
     O.second(A.two)
     V.first(A.two)
     B.second(A.two)
@@ -1259,13 +1283,13 @@
                     value = after(value, own["mid"].got, *[s.two for s in feed])
                     own["gate"], whole = finish(feed, *[own["gate"]] * (layers > 1))
                     value = after(value, whole)
-                    own["mid"].second(value[0])
             elif name == "time grads":
-                own["time"] = Scatter(*weight_halves(place, *value, n, "apart"), XY)
+                own["time"] = Scatter(*weight_halves(place, *value, n, "apart"), XY if l else YX)
                 own["time"].cores()
             elif name == "edge two" and l == 0:
-                value = after(value, own["time"].received)
                 own["time"].first()
+                own["mid"].second(own["time"].sent)
+                value = after(value, own["time"].sent)
             elif name == "norm" and l > 0:
                 value = after(value, own["time"].received)
                 own["time"].first()
@@ -1284,10 +1308,10 @@
         *[lax.dynamic_index_in_dim(vec_view, w, 4, keepdims=False) for w in (c, 1 - c)], XY
     )
     tail = sums[0]
-    vec_sum.cores(tail["time"].got)
-    vec_sum.first()
-    tail["time"].second(tail["gate"])
-    vec_sum.second()
+    vec_sum.cores()
+    vec_sum.first(tail["time"].got)
+    tail["time"].second()
+    vec_sum.second(tail["gate"])
     _, whole = finish([tail["mid"], tail["time"], vec_sum])
     for l in range(1, layers):
         for e in (sums[l]["feed"], sums[l]["mid"], sums[l]["time"]):

time: 581 us -> 571 us (0.983)
  waiting for transfers between devices: 95.7 us -> 80 us
    ppermute x28, waiting for transfers between devices: 74.5 us -> 63.5 us  [by_bit(): lax.ppermute(block, 'dp', [(i, i ^ bit) for i in range(lax.axis_size('dp'...]
    unnamed x190 -> x189, local copies, waits for them, and re-layouts: 14.7 us -> 12 us
  transfers between devices with their start and end apart: 64 -> 65, of which waited for: 26 -> 22; matrix products, arithmetic and copies ran while one was open for 15% -> 18% of each run, Pallas kernels for 26% -> 27%
where the time goes in v4:
time: 571 us; the launch traced here: 563 us
  Pallas kernels  201 us (35%)
  waiting for transfers between devices  80 us (14%)
  blocking collectives  75.4 us (13%)
  other arithmetic  70.1 us (12%)
  local copies, waits for them, and re-layouts  64.2 us (11%)
  starting transfers between devices  55.4 us (10%)
  between operations  16.3 us (3%)
    pallas_call x21, Pallas kernels, run(): pl.pallas_call(body, grid=(grid,), in_specs=in_specs, out_specs=out_specs...  201 us
    ppermute x28, waiting for transfers between devices, by_bit(): lax.ppermute(block, 'dp', [(i, i ^ bit) for i in range(lax.axis_size('dp'...  63.5 us
    all_gather x4, blocking collectives, chain(): all_states = lax.all_gather(mine.astype(BF16), SEQ).astype(F32)  57 us
    ppermute x28, starting transfers between devices, by_bit(): lax.ppermute(block, 'dp', [(i, i ^ bit) for i in range(lax.axis_size('dp'...  29.1 us
    all_gather x1, blocking collectives, gather_seq(): return lax.all_gather(after(part, *gate), SEQ, axis=0, tiled=True)  18.4 us
    ppermute x8, starting transfers between devices, from_behind(): return lax.ppermute(block, SEQ, route)  14.3 us
    another operation x7, other arithmetic, second(): self.two = by_bit(jnp.stack([self.own, one]), self.bits[1])  12.2 us
    unnamed x189, local copies, waits for them, and re-layouts  12 us
  transfers between devices with their start and end apart: 65, of which 22 were waited for; matrix products, arithmetic and copies ran while one was open for 18% of the time, Pallas kernels for 27%

profile of v4, /device:TPU:0, one launch (start us, length us, event | category | flops | bytes accessed | tf_op | source)
XLA Modules:
  0.0 562.7 jit_solution(6741441414625923980)
XLA Ops:
  17.8 18.4 %all_gather.39.refs_5_.refs_16_ = bf16[192,1664]{1,0:T(8,128)(2,1)S(1)} all-gather(bf16[24,1664]{1,0:T(8,128)(2,1)S(1)} %fusion.9), channel_id=1, replica_groups=mesh['dp'=4,'z'=4,'c'=2] {'z','c'}, dimensions={0}, use_global_device_ids=true | all-gather | bytes 718848 | tf_op jit(solution)/shard_map/all_gather | solution.py:798
  60.7 13.6 %collective-permute-done.2.refs_7_.refs_18_ = bf16[2,96,1664]{2,1,0:T(8,128)(2,1)} collective-permute-done((bf16[2,96,1664]{2,1,0:T(8,128)(2,1)}, bf16[2,96,1664]{2,1,0:T(8,128)(2,1)}, u32[]{:S(2)}, u32[]{:S(2)}) %collective-permute-start.2) | collective-permute-done | bytes 639008 | tf_op jit(solution)/shard_map/ppermute | solution.py:790
  84.9 9.6 %k_time_in.2 = (bf16[512,768]{1,0:T(8,128)(2,1)}, bf16[512,768]{1,0:T(8,128)(2,1)}, bf16[512,768]{1,0:T(8,128)(2,1)}, f32[512,768]{1,0:T(8,128)}, bf16[512,768]{...) custom-call(s32[4,8]{1,0:T(4,128)} %refs_0_.35, ...), custom_call_target="tpu_custom_call" | custom-call | flops 60397976 | bytes 786432 | tf_op jit(solution)/shard_map/k_time_in/pallas_call | solution.py:612
  101.8 14.3 %all-gather = bf16[32,2,768]{2,1,0:T(2,128)(2,1)S(1)} all-gather(bf16[4,2,768]{2,1,0:T(2,128)(2,1)S(1)} %convert_element_type.489), channel_id=2, replica_groups=mesh['dp'=4,'z'=4,'c'=2] {'z','c'}, dimensions={0}, use_global_device_ids=true | all-gather | bytes 110592 | tf_op jit(solution)/shard_map/all_gather | solution.py:920
  119.4 8.3 %k_time_out.2 = (bf16[512,768]{1,0:T(8,128)(2,1)}, f32[512,768]{1,0:T(8,128)}, bf16[512,768]{1,0:T(8,128)(2,1)}) custom-call(s32[4,8]{1,0:T(4,128)} %refs_0_.35, s32[3]{0:T(128)} %pad_add_fusion.refs_1_, bf16[512,768]{1,0:T(8,128)(2,1)} %bitcast.191, f32[512,768]{1,0:T(8,128)} %get-tuple-element.234.refs_3_.refs_7_.refs_5_, ...), custom_call_target="tpu_custom_call" | custom-call | flops 60397976 | bytes 589824 | tf_op jit(solution)/shard_map/k_time_out/pallas_call | solution.py:612
  135.8 8.6 %collective-permute-done.14.refs_6_.refs_11_.refs_14_.refs_17_ = bf16[96,3072]{1,0:T(8,128)(2,1)S(1)} collective-permute-done((bf16[96,3072]{1,0:T(8,128)(2,1)S(1)}, bf16[96,3072]{1,0:T(8,128)(2,1)S(1)}, u32[]{:S(2)}, u32[]{:S(2)}) %collective-permute-start.14) | collective-permute-done | bytes 589856 | tf_op jit(solution)/shard_map/ppermute | solution.py:790
  150.5 15.4 %k_feed.2 = (bf16[512,768]{1,0:T(8,128)(2,1)}, bf16[512,768]{1,0:T(8,128)(2,1)}, bf16[512,3072]{1,0:T(8,128)(2,1)}, bf16[512,3072]{1,0:T(8,128)(2,1)}, bf16[512,...) custom-call(s32[4,8]{1,0:T(4,128)} %refs_0_.35, s32[3]{0:T(128)} %pad_add_fusion.refs_1_, ...), custom_call_target="tpu_custom_call" | custom-call | flops 271790912 | bytes 1179648 | tf_op jit(solution)/shard_map/k_feed/pallas_call | solution.py:612
  167.1 6.1 %collective-permute-done.20.refs_7_.refs_12_.refs_15_.refs_18_ = bf16[2,96,3072]{2,1,0:T(8,128)(2,1)} collective-permute-done((bf16[2,96,3072]{2,1,0:T(8,128)(2,1)}, bf16[2,96,3072]{2,1,0:T(8,128)(2,1)}, u32[]{:S(2)}, u32[]{:S(2)}) %collective-permute-start.20) | collective-permute-done | bytes 1179680 | tf_op jit(solution)/shard_map/ppermute | solution.py:790
  186.8 9.6 %k_time_in.3 = (bf16[512,768]{1,0:T(8,128)(2,1)}, bf16[512,768]{1,0:T(8,128)(2,1)}, bf16[512,768]{1,0:T(8,128)(2,1)}, f32[512,768]{1,0:T(8,128)}, bf16[512,768]{...) custom-call(s32[4,8]{1,0:T(4,128)} %refs_0_.35, ...), custom_call_target="tpu_custom_call" | custom-call | flops 60397976 | bytes 786432 | tf_op jit(solution)/shard_map/k_time_in/pallas_call | solution.py:612
  200.1 14.1 %all-gather.1 = bf16[32,2,768]{2,1,0:T(2,128)(2,1)S(1)} all-gather(bf16[4,2,768]{2,1,0:T(2,128)(2,1)S(1)} %convert_element_type.491), channel_id=3, replica_groups=mesh['dp'=4,'z'=4,'c'=2] {'z','c'}, dimensions={0}, use_global_device_ids=true | all-gather | bytes 110592 | tf_op jit(solution)/shard_map/all_gather | solution.py:920
  214.9 8.5 %k_time_out.3 = (bf16[512,768]{1,0:T(8,128)(2,1)}, f32[512,768]{1,0:T(8,128)}, bf16[512,768]{1,0:T(8,128)(2,1)}) custom-call(s32[4,8]{1,0:T(4,128)} %refs_0_.35, s32[3]{0:T(128)} %pad_add_fusion.refs_1_, f32[512,768]{1,0:T(8,128)} %get-tuple-element.263.refs_2_.refs_0_, f32[512,768]{1,0:T(8,128)} %get-tuple-element.266.refs_3_.refs_7_.refs_5_, ...), custom_call_target="tpu_custom_call" | custom-call | flops 60397976 | bytes 589824 | tf_op jit(solution)/shard_map/k_time_out/pallas_call | solution.py:612
  235.5 15.5 %k_feed.3 = (bf16[512,768]{1,0:T(8,128)(2,1)}, bf16[512,768]{1,0:T(8,128)(2,1)}, bf16[512,3072]{1,0:T(8,128)(2,1)}, bf16[512,3072]{1,0:T(8,128)(2,1)}, bf16[512,...) custom-call(s32[4,8]{1,0:T(4,128)} %refs_0_.35, s32[3]{0:T(128)} %pad_add_fusion.refs_1_, ...), custom_call_target="tpu_custom_call" | custom-call | flops 271790912 | bytes 1179648 | tf_op jit(solution)/shard_map/k_feed/pallas_call | solution.py:612
  251.0 15.3 %k_feed_back.2 = (bf16[512,768]{1,0:T(8,128)(2,1)}, bf16[512,768]{1,0:T(8,128)(2,1)}, bf16[512,3072]{1,0:T(8,128)(2,1)}, bf16[512,768]{1,0:T(8,128)(2,1)}, f32[4,768]{1,0:T(4,128)}, /*index=5*/f32[8,768]{1,0:T(8,128)}) custom-call(s32[4,8]{1,0:T(4,128)} %refs_0_.35, s32[3]{0:T(128)} %pad_add_fusion.refs_1_, bf16[512,768]{1,0:T(8,128)(2,1)} %bitcast.199, ...), custom_call_target="tpu_custom_call" | custom-call | flops 271790912 | bytes 1179648 | tf_op jit(solution)/shard_map/k_feed_back/pallas_call | solution.py:612
  266.3 12.1 %k_flat.1 = bf16[768,6144]{1,0:T(8,128)(2,1)} custom-call(bf16[512,768]{1,0:T(8,128)(2,1)} %get-tuple-element.288.refs_0_, bf16[512,3072]{1,0:T(8,128)(2,1)} %get-tuple-element.289.refs_1_, bf16[512,3072]{1,0:T(8,128)(2,1)} %get-tuple-element.290.refs_2_, bf16[512,768]{1,0:T(8,128)(2,1)} %get-tuple-element.291.refs_3_), custom_call_target="tpu_custom_call" | custom-call | flops 241591904 | bytes 1101004 | tf_op jit(solution)/shard_map/k_flat/pallas_call | solution.py:612
  282.8 12.8 %k_mid_back.2 = (f32[512,768]{1,0:T(8,128)}, bf16[512,768]{1,0:T(8,128)(2,1)}, bf16[512,768]{1,0:T(8,128)(2,1)}, bf16[512,768]{1,0:T(8,128)(2,1)}, bf16[512,768]...) custom-call(s32[4,8]{1,0:T(4,128)} %refs_0_.35, ...), custom_call_target="tpu_custom_call" | custom-call | flops 30198988 | bytes 983040 | tf_op jit(solution)/shard_map/k_mid_back/pallas_call | solution.py:612
  295.6 6.3 %k_halves_apart.4 = (bf16[4,4,3,24,768]{4,3,2,1,0:T(8,128)(2,1)}, bf16[4,4,3,24,768]{4,3,2,1,0:T(8,128)(2,1)}) custom-call(s32[4,8]{1,0:T(4,128)} %refs_0_.35, s32[3]{0:T(128)} %pad_add_fusion.refs_1_, bf16[512,768]{1,0:T(8,128)(2,1)} %get-tuple-element.299.refs_2_, bf16[512,768]{1,0:T(8,128)(2,1)} %get-tuple-element.300.refs_3_, ...), custom_call_target="tpu_custom_call" | custom-call | flops 90596968 | bytes 412876 | tf_op jit(solution)/shard_map/k_halves_apart/pallas_call | solution.py:612
  304.5 14.1 %all-gather.2 = bf16[32,2,768]{2,1,0:T(2,128)(2,1)S(1)} all-gather(bf16[4,2,768]{2,1,0:T(2,128)(2,1)S(1)} %convert_element_type.498), channel_id=4, replica_groups=mesh['dp'=4,'z'=4,'c'=2] {'z','c'}, dimensions={0}, use_global_device_ids=true | all-gather | bytes 110592 | tf_op jit(solution)/shard_map/all_gather | solution.py:920
  319.3 10.4 %k_time_back.2 = (bf16[512,768]{1,0:T(8,128)(2,1)}, bf16[512,768]{1,0:T(8,128)(2,1)}, bf16[512,768]{1,0:T(8,128)(2,1)}, f32[2,2,768]{2,1,0:T(2,128)}, f32[8,768]{1,0:T(8,128)}) custom-call(s32[4,8]{1,0:T(4,128)} %refs_0_.35, s32[3]{0:T(128)} %pad_add_fusion.refs_1_, f32[512,768]{1,0:T(8,128)} %get-tuple-element.263.refs_2_.refs_0_, ...), custom_call_target="tpu_custom_call" | custom-call | flops 90596968 | bytes 983040 | tf_op jit(solution)/shard_map/k_time_back/pallas_call | solution.py:612
  329.7 5.4 k_halves_apart.5
  348.0 15.7 %k_feed_back.3 = (bf16[512,768]{1,0:T(8,128)(2,1)}, bf16[512,768]{1,0:T(8,128)(2,1)}, bf16[512,3072]{1,0:T(8,128)(2,1)}, bf16[512,768]{1,0:T(8,128)(2,1)}, f32[4,768]{1,0:T(4,128)}, /*index=5*/f32[8,768]{1,0:T(8,128)}) custom-call(s32[4,8]{1,0:T(4,128)} %refs_0_.35, s32[3]{0:T(128)} %pad_add_fusion.refs_1_, f32[512,768]{1,0:T(8,128)} %get-tuple-element.315.refs_2_.refs_5_, ...), custom_call_target="tpu_custom_call" | custom-call | flops 271790912 | bytes 1179648 | tf_op jit(solution)/shard_map/k_feed_back/pallas_call | solution.py:612
  370.6 7.0 %k_halves_blocks.2 = (bf16[4,4,4,24,768]{4,3,2,1,0:T(8,128)(2,1)}, bf16[4,4,4,24,768]{4,3,2,1,0:T(8,128)(2,1)}) custom-call(s32[4,8]{1,0:T(4,128)} %refs_0_.35, s32[3]{0:T(128)} %pad_add_fusion.refs_1_, bf16[512,3072]{1,0:T(8,128)(2,1)} %get-tuple-element.333.refs_2_, bf16[512,768]{1,0:T(8,128)(2,1)} %get-tuple-element.334.refs_3_), custom_call_target="tpu_custom_call" | custom-call | flops 120795952 | bytes 550502 | tf_op jit(solution)/shard_map/k_halves_blocks/pallas_call | solution.py:612
  380.0 7.0 %k_halves_blocks.3 = (bf16[4,4,4,24,768]{4,3,2,1,0:T(8,128)(2,1)}, bf16[4,4,4,24,768]{4,3,2,1,0:T(8,128)(2,1)}) custom-call(s32[4,8]{1,0:T(4,128)} %refs_0_.35, s32[3]{0:T(128)} %pad_add_fusion.refs_1_, bf16[512,768]{1,0:T(8,128)(2,1)} %get-tuple-element.336.refs_2_, bf16[512,3072]{1,0:T(8,128)(2,1)} %get-tuple-element.339.refs_3_), custom_call_target="tpu_custom_call" | custom-call | flops 120795952 | bytes 550502 | tf_op jit(solution)/shard_map/k_halves_blocks/pallas_call | solution.py:612
  397.8 12.9 %k_mid_back.3 = (f32[512,768]{1,0:T(8,128)}, bf16[512,768]{1,0:T(8,128)(2,1)}, bf16[512,768]{1,0:T(8,128)(2,1)}, bf16[512,768]{1,0:T(8,128)(2,1)}, bf16[512,768]...) custom-call(s32[4,8]{1,0:T(4,128)} %refs_0_.35, ...), custom_call_target="tpu_custom_call" | custom-call | flops 30198988 | bytes 983040 | tf_op jit(solution)/shard_map/k_mid_back/pallas_call | solution.py:612
  410.7 6.2 %k_halves_apart.6 = (bf16[4,4,3,24,768]{4,3,2,1,0:T(8,128)(2,1)}, bf16[4,4,3,24,768]{4,3,2,1,0:T(8,128)(2,1)}) custom-call(s32[4,8]{1,0:T(4,128)} %refs_0_.35, s32[3]{0:T(128)} %pad_add_fusion.refs_1_, bf16[512,768]{1,0:T(8,128)(2,1)} %get-tuple-element.356.refs_2_, bf16[512,768]{1,0:T(8,128)(2,1)} %get-tuple-element.357.refs_3_, ...), custom_call_target="tpu_custom_call" | custom-call | flops 90596968 | bytes 412876 | tf_op jit(solution)/shard_map/k_halves_apart/pallas_call | solution.py:612
  417.0 4.1 collective-permute-done.43
  439.7 14.5 %all-gather.3 = bf16[32,2,768]{2,1,0:T(2,128)(2,1)S(1)} all-gather(bf16[4,2,768]{2,1,0:T(2,128)(2,1)S(1)} %convert_element_type.520), channel_id=5, replica_groups=mesh['dp'=4,'z'=4,'c'=2] {'z','c'}, dimensions={0}, use_global_device_ids=true | all-gather | bytes 110592 | tf_op jit(solution)/shard_map/all_gather | solution.py:920
  454.9 10.0 %k_time_back.3 = (bf16[512,768]{1,0:T(8,128)(2,1)}, bf16[512,768]{1,0:T(8,128)(2,1)}, bf16[512,768]{1,0:T(8,128)(2,1)}, f32[2,2,768]{2,1,0:T(2,128)}, f32[8,768]{1,0:T(8,128)}) custom-call(s32[4,8]{1,0:T(4,128)} %refs_0_.35, s32[3]{0:T(128)} %pad_add_fusion.refs_1_, bf16[512,768]{1,0:T(8,128)(2,1)} %bitcast.192, f32[2,2,768]{2,1,0:T(2,128)} %reshape.497.refs_3_, ...), custom_call_target="tpu_custom_call" | custom-call | flops 90596968 | bytes 983040 | tf_op jit(solution)/shard_map/k_time_back/pallas_call | solution.py:612
  472.2 5.2 k_halves_apart.7
  485.3 4.3 k_norm_back.3
  493.8 11.2 %collective-permute-done.51 = bf16[1,1,4,3,24,768]{5,4,3,2,1,0:T(8,128)(2,1)} collective-permute-done((bf16[1,1,4,3,24,768]{5,4,3,2,1,0:T(8,128)(2,1)S(1)}, bf16[1,1,4,3,24,768]{5,4,3,2,1,0:T(8,128)(2,1)}, u32[]{:S(2)}, u32[]{:S(2)}) %collective-permute-start.51) | collective-permute-done | bytes 442400 | tf_op jit(solution)/shard_map/ppermute | solution.py:790
  510.0 5.7 %collective-permute-done.53 = bf16[1,1,4,2,24,768]{5,4,3,2,1,0:T(8,128)(2,1)S(1)} collective-permute-done((bf16[1,1,4,2,24,768]{5,4,3,2,1,0:T(8,128)(2,1)S(1)}, bf16[1,1,4,2,24,768]{5,4,3,2,1,0:T(8,128)(2,1)S(1)}, u32[]{:S(2)}, u32[]{:S(2)}) %collective-permute-start.53) | collective-permute-done | bytes 294944 | tf_op jit(solution)/shard_map/ppermute | solution.py:790
  539.3 7.3 %reduce-scatter.13.cloned.1.call-done = bf16[144,768]{1,0:T(8,128)(2,1)} async-done(((bf16[576,768]{1,0:T(8,128)(2,1)}), bf16[144,768]{1,0:T(8,128)(2,1)}) %reduce-scatter.13.cloned.1.call-update) | async-done | bytes 221200 | tf_op jit(solution)/shard_map/reduce_scatter | solution.py:902
  (500 shorter events, 217.1 us)
Async XLA Ops:
  7.2 42.7 %all-gather.9.cloned.1.call-start = ((), (), s32[]{:S(2)}) async-start(), calls=%async_computation.4 | async-start | bytes 2322432 | tf_op jit(solution)/shard_map/all_gather | solution.py:798
  13.7 64.9 %all-gather.11.cloned.1.call-start = ((), (), s32[]{:S(2)}) async-start(), calls=%async_computation.5 | async-start | bytes 1327104 | tf_op jit(solution)/shard_map/all_gather | solution.py:798
  14.6 34.0 %collective-permute-start = (bf16[4,768]{1,0:T(4,128)(2,1)S(1)}, bf16[4,768]{1,0:T(4,128)(2,1)}, u32[]{:S(2)}, u32[]{:S(2)}) collective-permute-start(bf16[4,768]{1,0:T(4,128)(2,1)S(1)} %bitcast.249), channel_id=1, source_target_pairs={{0,1},{1,2},{2,3},{3,4},{4,5},{5,6},{6,7},{8,9},{9,10},{10,11},{11... | collective-permute-start | bytes 18440 | tf_op jit(solution)/shard_map/ppermute | solution.py:915
  39.2 88.6 %all-gather.13.cloned.1.call-start = ((), (), s32[]{:S(2)}) async-start(), calls=%async_computation.6 | async-start | bytes 1327104 | tf_op jit(solution)/shard_map/all_gather | solution.py:798
  47.0 99.4 %all-gather.15.cloned.1.call-start = ((), (), s32[]{:S(2)}) async-start(), calls=%async_computation.7 | async-start | bytes 2985984 | tf_op jit(solution)/shard_map/all_gather | solution.py:798
  55.1 19.2 %collective-permute-start.4 = (bf16[96,3840]{1,0:T(8,128)(2,1)}, bf16[96,3840]{1,0:T(8,128)(2,1)S(1)}, u32[]{:S(2)}, u32[]{:S(2)}) collective-permute-start(bf16[96,3840]{1,0:T(8,128)(2,1)} %constant_dynamic-slice_fusion.10), channel_id=1, source_target_pairs={{0,8},{8,0},{16,24},{24,16},{1,9},{9,1},{17,25},{25,17},{2,10},{10... | collective-permute-start | bytes 2211848 | tf_op jit(solution)/shard_map/ppermute | solution.py:790
  58.5 15.8 %collective-permute-start.2 = (bf16[2,96,1664]{2,1,0:T(8,128)(2,1)}, bf16[2,96,1664]{2,1,0:T(8,128)(2,1)}, u32[]{:S(2)}, u32[]{:S(2)}) collective-permute-start(bf16[2,96,1664]{2,1,0:T(8,128)(2,1)} %pad_maximum_fusion.8), channel_id=1, source_target_pairs={{0,16},{8,24},{16,0},{24,8},{1,17},{9,25},{17,1},{25,9},{2,18},{10... | collective-permute-start | bytes 1916936 | tf_op jit(solution)/shard_map/ppermute | solution.py:790
  60.1 363.9 %reduce-scatter.7.cloned.1.call-start = ((), (), s32[]{:S(2)}) async-start(), calls=%async_computation.8 | async-start | bytes 9732096 | tf_op jit(solution)/shard_map/reduce_scatter | solution.py:1052
  77.2 17.4 %collective-permute-start.7 = (bf16[2,96,1536]{2,1,0:T(8,128)(2,1)}, bf16[2,96,1536]{2,1,0:T(8,128)(2,1)}, u32[]{:S(2)}, u32[]{:S(2)}) collective-permute-start(bf16[2,96,1536]{2,1,0:T(8,128)(2,1)} %pad_maximum_fusion.9), channel_id=1, source_target_pairs={{0,8},{8,0},{16,24},{24,16},{1,9},{9,1},{17,25},{25,17},{2,10},{10... | collective-permute-start | bytes 1769480 | tf_op jit(solution)/shard_map/ppermute | solution.py:790
  98.4 29.3 %collective-permute-start.11 = (bf16[2,96,3072]{2,1,0:T(8,128)(2,1)}, bf16[2,96,3072]{2,1,0:T(8,128)(2,1)}, u32[]{:S(2)}, u32[]{:S(2)}) collective-permute-start(bf16[2,96,3072]{2,1,0:T(8,128)(2,1)} %pad_maximum_fusion.2), channel_id=1, source_target_pairs={{0,8},{8,0},{16,24},{24,16},{1,9},{9,1},{17,25},{25,17},{2,10},{10... | collective-permute-start | bytes 3538952 | tf_op jit(solution)/shard_map/ppermute | solution.py:790
  100.2 33.1 %collective-permute-start.13 = (bf16[2,96,3840]{2,1,0:T(8,128)(2,1)}, bf16[2,96,3840]{2,1,0:T(8,128)(2,1)}, u32[]{:S(2)}, u32[]{:S(2)}) collective-permute-start(bf16[2,96,3840]{2,1,0:T(8,128)(2,1)} %pad_maximum_fusion), channel_id=1, source_target_pairs={{0,16},{8,24},{16,0},{24,8},{1,17},{9,25},{17,1},{25,9},{2,18},{10... | collective-permute-start | bytes 4423688 | tf_op jit(solution)/shard_map/ppermute | solution.py:790
  101.6 16.9 %collective-permute-start.10 = (bf16[2,96,1536]{2,1,0:T(8,128)(2,1)}, bf16[2,96,1536]{2,1,0:T(8,128)(2,1)S(1)}, u32[]{:S(2)}, u32[]{:S(2)}) collective-permute-start(bf16[2,96,1536]{2,1,0:T(8,128)(2,1)} %collective-permute-done.7.refs_12_.refs_15_.refs_23_), channel_id=1, source_target_pairs={{0,1},{1,0},{2,3},{3,2},{4,5},{5,4},{6,7},{7,6},{8,9},{9,8},{10,11... | collective-permute-start | bytes 1769480 | tf_op jit(solution)/shard_map/ppermute | solution.py:840
  134.0 16.5 %collective-permute-start.16 = (bf16[2,96,3840]{2,1,0:T(8,128)(2,1)}, bf16[2,96,3840]{2,1,0:T(8,128)(2,1)}, u32[]{:S(2)}, u32[]{:S(2)}) collective-permute-start(bf16[2,96,3840]{2,1,0:T(8,128)(2,1)} %collective-permute-done.13.refs_7_.refs_11_), channel_id=1, source_target_pairs={{0,1},{1,0},{2,3},{3,2},{4,5},{5,4},{6,7},{7,6},{8,9},{9,8},{10,11... | collective-permute-start | bytes 4423688 | tf_op jit(solution)/shard_map/ppermute | solution.py:840
  145.7 27.5 %collective-permute-start.20 = (bf16[2,96,3072]{2,1,0:T(8,128)(2,1)}, bf16[2,96,3072]{2,1,0:T(8,128)(2,1)}, u32[]{:S(2)}, u32[]{:S(2)}) collective-permute-start(bf16[2,96,3072]{2,1,0:T(8,128)(2,1)} %pad_maximum_fusion.3), channel_id=1, source_target_pairs={{0,16},{8,24},{16,0},{24,8},{1,17},{9,25},{17,1},{25,9},{2,18},{10... | collective-permute-start | bytes 3538952 | tf_op jit(solution)/shard_map/ppermute | solution.py:790
  148.4 18.7 %collective-permute-start.19 = (bf16[96,3840]{1,0:T(8,128)(2,1)}, bf16[96,3840]{1,0:T(8,128)(2,1)}, u32[]{:S(2)}, u32[]{:S(2)}) collective-permute-start(bf16[96,3840]{1,0:T(8,128)(2,1)} %constant_dynamic-slice_fusion), channel_id=1, source_target_pairs={{0,8},{8,0},{16,24},{24,16},{1,9},{9,1},{17,25},{25,17},{2,10},{10... | collective-permute-start | bytes 2211848 | tf_op jit(solution)/shard_map/ppermute | solution.py:790
  179.0 17.4 %collective-permute-start.24 = (bf16[96,3072]{1,0:T(8,128)(2,1)}, bf16[96,3072]{1,0:T(8,128)(2,1)}, u32[]{:S(2)}, u32[]{:S(2)}) collective-permute-start(bf16[96,3072]{1,0:T(8,128)(2,1)} %constant_dynamic-slice_fusion.9), channel_id=1, source_target_pairs={{0,16},{8,24},{16,0},{24,8},{1,17},{9,25},{17,1},{25,9},{2,18},{10... | collective-permute-start | bytes 1769480 | tf_op jit(solution)/shard_map/ppermute | solution.py:790
  184.1 42.5 %collective-permute-start.26 = (bf16[2,96,3840]{2,1,0:T(8,128)(2,1)}, bf16[2,96,3840]{2,1,0:T(8,128)(2,1)}, u32[]{:S(2)}, u32[]{:S(2)}) collective-permute-start(bf16[2,96,3840]{2,1,0:T(8,128)(2,1)} %pad_maximum_fusion.1), channel_id=1, source_target_pairs={{0,16},{8,24},{16,0},{24,8},{1,17},{9,25},{17,1},{25,9},{2,18},{10... | collective-permute-start | bytes 4423688 | tf_op jit(solution)/shard_map/ppermute | solution.py:790
  198.6 28.1 %collective-permute-start.25 = (bf16[2,96,3072]{2,1,0:T(8,128)(2,1)}, bf16[2,96,3072]{2,1,0:T(8,128)(2,1)}, u32[]{:S(2)}, u32[]{:S(2)}) collective-permute-start(bf16[2,96,3072]{2,1,0:T(8,128)(2,1)} %pad_maximum_fusion.4), channel_id=1, source_target_pairs={{0,8},{8,0},{16,24},{24,16},{1,9},{9,1},{17,25},{25,17},{2,10},{10... | collective-permute-start | bytes 3538952 | tf_op jit(solution)/shard_map/ppermute | solution.py:790
  278.4 188.8 %reduce-scatter.9.cloned.1.call-start = ((), (), s32[]{:S(2)}) async-start(), calls=%async_computation.9 | async-start | bytes 921600 | tf_op jit(solution)/shard_map/reduce_scatter | solution.py:902
  301.9 17.4 %collective-permute-start.33 = (bf16[2,2,4,3,24,768]{5,4,3,2,1,0:T(8,128)(2,1)}, bf16[2,2,4,3,24,768]{5,4,3,2,1,0:T(8,128)(2,1)}, u32[]{:S(2)}, u32[]{:S(2)}) collective-permute-start(bf16[2,2,4,3,24,768]{5,4,3,2,1,0:T(8,128)(2,1)} %bitcast.253), channel_id=1, source_target_pairs={{0,1},{1,0},{2,3},{3,2},{4,5},{5,4},{6,7},{7,6},{8,9},{9,8},{10,11... | collective-permute-start | bytes 5308424 | tf_op jit(solution)/shard_map/ppermute | solution.py:864
  337.2 28.5 %collective-permute-start.36 = (bf16[2,1,4,3,24,768]{5,4,3,2,1,0:T(8,128)(2,1)S(1)}, bf16[2,1,4,3,24,768]{5,4,3,2,1,0:T(8,128)(2,1)}, u32[]{:S(2)}, u32[]{:S(2)}) collective-permute-start(bf16[2,1,4,3,24,768]{5,4,3,2,1,0:T(8,128)(2,1)S(1)} %add_convert_fusion.3), channel_id=1, source_target_pairs={{0,8},{8,0},{16,24},{24,16},{1,9},{9,1},{17,25},{25,17},{2,10},{10... | collective-permute-start | bytes 2654216 | tf_op jit(solution)/shard_map/ppermute | solution.py:790
  340.0 25.7 %collective-permute-start.37 = (bf16[1,2,4,2,24,768]{5,4,3,2,1,0:T(8,128)(2,1)}, bf16[1,2,4,2,24,768]{5,4,3,2,1,0:T(8,128)(2,1)}, u32[]{:S(2)}, u32[]{:S(2)}) collective-permute-start(bf16[1,2,4,2,24,768]{5,4,3,2,1,0:T(8,128)(2,1)} %add_convert_fusion.9), channel_id=1, source_target_pairs={{0,16},{8,24},{16,0},{24,8},{1,17},{9,25},{17,1},{25,9},{2,18},{10... | collective-permute-start | bytes 1769480 | tf_op jit(solution)/shard_map/ppermute | solution.py:790
  367.1 19.8 %collective-permute-start.40 = (bf16[1,1,4,3,24,768]{5,4,3,2,1,0:T(8,128)(2,1)S(1)}, bf16[1,1,4,3,24,768]{5,4,3,2,1,0:T(8,128)(2,1)S(1)}, u32[]{:S(2)}, u32[]{:S(2)}) collective-permute-start(bf16[1,1,4,3,24,768]{5,4,3,2,1,0:T(8,128)(2,1)S(1)} %add_convert_fusion.13), channel_id=1, source_target_pairs={{0,16},{8,24},{16,0},{24,8},{1,17},{9,25},{17,1},{25,9},{2,18},{10... | collective-permute-start | bytes 1327112 | tf_op jit(solution)/shard_map/ppermute | solution.py:790
  370.6 16.3 %collective-permute-start.41 = (bf16[1,1,4,2,24,768]{5,4,3,2,1,0:T(8,128)(2,1)}, bf16[1,1,4,2,24,768]{5,4,3,2,1,0:T(8,128)(2,1)}, u32[]{:S(2)}, u32[]{:S(2)}) collective-permute-start(bf16[1,1,4,2,24,768]{5,4,3,2,1,0:T(8,128)(2,1)} %add_convert_fusion.17), channel_id=1, source_target_pairs={{0,8},{8,0},{16,24},{24,16},{1,9},{9,1},{17,25},{25,17},{2,10},{10... | collective-permute-start | bytes 884744 | tf_op jit(solution)/shard_map/ppermute | solution.py:790
  390.3 30.8 %collective-permute-start.43 = (bf16[2,1,4,4,24,768]{5,4,3,2,1,0:T(8,128)(2,1)}, bf16[2,1,4,4,24,768]{5,4,3,2,1,0:T(8,128)(2,1)}, u32[]{:S(2)}, u32[]{:S(2)}) collective-permute-start(bf16[2,1,4,4,24,768]{5,4,3,2,1,0:T(8,128)(2,1)} %add_convert_fusion.1), channel_id=1, source_target_pairs={{0,8},{8,0},{16,24},{24,16},{1,9},{9,1},{17,25},{25,17},{2,10},{10... | collective-permute-start | bytes 3538952 | tf_op jit(solution)/shard_map/ppermute | solution.py:790
  393.6 30.4 %collective-permute-start.44 = (bf16[1,2,4,4,24,768]{5,4,3,2,1,0:T(8,128)(2,1)}, bf16[1,2,4,4,24,768]{5,4,3,2,1,0:T(8,128)(2,1)}, u32[]{:S(2)}, u32[]{:S(2)}) collective-permute-start(bf16[1,2,4,4,24,768]{5,4,3,2,1,0:T(8,128)(2,1)} %add_convert_fusion), channel_id=1, source_target_pairs={{0,16},{8,24},{16,0},{24,8},{1,17},{9,25},{17,1},{25,9},{2,18},{10... | collective-permute-start | bytes 3538952 | tf_op jit(solution)/shard_map/ppermute | solution.py:790
  429.2 87.8 %reduce-scatter.11.cloned.1.call-start = ((), (), s32[]{:S(2)}) async-start(), calls=%async_computation.10 | async-start | bytes 1474560 | tf_op jit(solution)/shard_map/reduce_scatter | solution.py:902
  432.2 35.0 %collective-permute-start.46 = (bf16[2,1,4,3,24,768]{5,4,3,2,1,0:T(8,128)(2,1)}, bf16[2,1,4,3,24,768]{5,4,3,2,1,0:T(8,128)(2,1)}, u32[]{:S(2)}, u32[]{:S(2)}) collective-permute-start(bf16[2,1,4,3,24,768]{5,4,3,2,1,0:T(8,128)(2,1)} %add_convert_fusion.2), channel_id=1, source_target_pairs={{0,8},{8,0},{16,24},{24,16},{1,9},{9,1},{17,25},{25,17},{2,10},{10... | collective-permute-start | bytes 2654216 | tf_op jit(solution)/shard_map/ppermute | solution.py:790
  435.3 29.6 %collective-permute-start.47 = (bf16[1,1,4,4,24,768]{5,4,3,2,1,0:T(8,128)(2,1)}, bf16[1,1,4,4,24,768]{5,4,3,2,1,0:T(8,128)(2,1)}, u32[]{:S(2)}, u32[]{:S(2)}) collective-permute-start(bf16[1,1,4,4,24,768]{5,4,3,2,1,0:T(8,128)(2,1)} %add_convert_fusion.8), channel_id=1, source_target_pairs={{0,16},{8,24},{16,0},{24,8},{1,17},{9,25},{17,1},{25,9},{2,18},{10... | collective-permute-start | bytes 1769480 | tf_op jit(solution)/shard_map/ppermute | solution.py:790
  438.6 28.7 %collective-permute-start.48 = (bf16[1,1,4,4,24,768]{5,4,3,2,1,0:T(8,128)(2,1)}, bf16[1,1,4,4,24,768]{5,4,3,2,1,0:T(8,128)(2,1)}, u32[]{:S(2)}, u32[]{:S(2)}) collective-permute-start(bf16[1,1,4,4,24,768]{5,4,3,2,1,0:T(8,128)(2,1)} %add_convert_fusion.7), channel_id=1, source_target_pairs={{0,8},{8,0},{16,24},{24,16},{1,9},{9,1},{17,25},{25,17},{2,10},{10... | collective-permute-start | bytes 1769480 | tf_op jit(solution)/shard_map/ppermute | solution.py:790
  481.3 65.3 %reduce-scatter.13.cloned.1.call-start = ((), (), s32[]{:S(2)}) async-start(), calls=%async_computation.11 | async-start | bytes 1105920 | tf_op jit(solution)/shard_map/reduce_scatter | solution.py:902
  484.0 21.0 %collective-permute-start.52 = (bf16[2,1,4,2,24,768]{5,4,3,2,1,0:T(8,128)(2,1)}, bf16[2,1,4,2,24,768]{5,4,3,2,1,0:T(8,128)(2,1)}, u32[]{:S(2)}, u32[]{:S(2)}) collective-permute-start(bf16[2,1,4,2,24,768]{5,4,3,2,1,0:T(8,128)(2,1)} %add_convert_fusion.4), channel_id=1, source_target_pairs={{0,8},{8,0},{16,24},{24,16},{1,9},{9,1},{17,25},{25,17},{2,10},{10... | collective-permute-start | bytes 1769480 | tf_op jit(solution)/shard_map/ppermute | solution.py:790
  (122 other events, 897.8 us)
Sparse Core Ops, SparseCore 0:
  13.8 34.2 all-gather.8
  50.3 22.5 all-gather.10
  75.1 22.2 all-gather.12
  99.5 34.1 all-gather.14
  278.5 144.0 reduce-scatter.6
  429.3 23.1 reduce-scatter.8
  481.5 29.8 reduce-scatter.10
  522.7 23.8 reduce-scatter.12

commit v5 on v4

--- a/solution.py
+++ b/solution.py
@@ -16,7 +16,7 @@
 
 RB = 2
 COST = 20
-VMEM = 63 * 1024 * 1024
+VMEM = 54 * 1024 * 1024
 F32, BF16 = jnp.float32, jnp.bfloat16
 
 

time: 571 us -> 566 us (level)
  other arithmetic: 70.1 us -> 61 us
    unnamed x189 -> x227, local copies, waits for them, and re-layouts: 12 us -> 14.1 us
  transfers between devices with their start and end apart: 65 -> 65, of which waited for: 22 -> 24; matrix products, arithmetic and copies ran while one was open for 18% -> 16% of each run, Pallas kernels for 27% -> 28%
where the time goes in v5:
time: 566 us; the launch traced here: 558 us
  Pallas kernels  202 us (36%)
  waiting for transfers between devices  81.7 us (14%)
  blocking collectives  75.5 us (13%)
  local copies, waits for them, and re-layouts  62 us (11%)
  other arithmetic  61 us (11%)
  starting transfers between devices  59.5 us (11%)
  between operations  16.5 us (3%)
    pallas_call x21, Pallas kernels, run(): pl.pallas_call(body, grid=(grid,), in_specs=in_specs, out_specs=out_specs...  202 us
    ppermute x28, waiting for transfers between devices, by_bit(): lax.ppermute(block, 'dp', [(i, i ^ bit) for i in range(lax.axis_size('dp'...  65.6 us
    all_gather x4, blocking collectives, chain(): all_states = lax.all_gather(mine.astype(BF16), SEQ).astype(F32)  56.5 us
    ppermute x28, starting transfers between devices, by_bit(): lax.ppermute(block, 'dp', [(i, i ^ bit) for i in range(lax.axis_size('dp'...  31.8 us
    all_gather x1, blocking collectives, gather_seq(): return lax.all_gather(after(part, *gate), SEQ, axis=0, tiled=True)  19 us
    unnamed x227, local copies, waits for them, and re-layouts  14.1 us
    ppermute x8, starting transfers between devices, from_behind(): return lax.ppermute(block, SEQ, route)  13.9 us
  transfers between devices with their start and end apart: 65, of which 24 were waited for; matrix products, arithmetic and copies ran while one was open for 16% of the time, Pallas kernels for 28%

profile of v5, /device:TPU:0, one launch (start us, length us, event | category | flops | bytes accessed | tf_op | source)
XLA Modules:
  0.0 558.4 jit_solution(12579290975390642210)
XLA Ops:
  17.2 19.0 %all_gather.39.refs_5_.refs_16_ = bf16[192,1664]{1,0:T(8,128)(2,1)S(1)} all-gather(bf16[24,1664]{1,0:T(8,128)(2,1)S(1)} %fusion.9), channel_id=1, replica_groups=mesh['dp'=4,'z'=4,'c'=2] {'z','c'}, dimensions={0}, use_global_device_ids=true | all-gather | bytes 718848 | tf_op jit(solution)/shard_map/all_gather | solution.py:798
  59.8 13.5 %collective-permute-done.2.refs_7_.refs_18_ = bf16[2,96,1664]{2,1,0:T(8,128)(2,1)} collective-permute-done((bf16[2,96,1664]{2,1,0:T(8,128)(2,1)}, bf16[2,96,1664]{2,1,0:T(8,128)(2,1)}, u32[]{:S(2)}, u32[]{:S(2)}) %collective-permute-start.2) | collective-permute-done | bytes 639008 | tf_op jit(solution)/shard_map/ppermute | solution.py:790
  84.0 9.7 %k_time_in.2 = (bf16[512,768]{1,0:T(8,128)(2,1)}, bf16[512,768]{1,0:T(8,128)(2,1)}, bf16[512,768]{1,0:T(8,128)(2,1)}, f32[512,768]{1,0:T(8,128)}, bf16[512,768]{...) custom-call(s32[4,8]{1,0:T(4,128)} %refs_0_.35, ...), custom_call_target="tpu_custom_call" | custom-call | flops 60397976 | bytes 786432 | tf_op jit(solution)/shard_map/k_time_in/pallas_call | solution.py:612
  99.1 14.0 %all-gather = bf16[32,2,768]{2,1,0:T(2,128)(2,1)S(1)} all-gather(bf16[4,2,768]{2,1,0:T(2,128)(2,1)S(1)} %convert_element_type.489), channel_id=2, replica_groups=mesh['dp'=4,'z'=4,'c'=2] {'z','c'}, dimensions={0}, use_global_device_ids=true | all-gather | bytes 110592 | tf_op jit(solution)/shard_map/all_gather | solution.py:920
  116.6 8.3 %k_time_out.2 = (bf16[512,768]{1,0:T(8,128)(2,1)}, f32[512,768]{1,0:T(8,128)}, bf16[512,768]{1,0:T(8,128)(2,1)}) custom-call(s32[4,8]{1,0:T(4,128)} %refs_0_.35, s32[3]{0:T(128)} %pad_add_fusion.refs_1_, bf16[512,768]{1,0:T(8,128)(2,1)} %bitcast.191, f32[512,768]{1,0:T(8,128)} %get-tuple-element.234.refs_3_.refs_7_.refs_5_, ...), custom_call_target="tpu_custom_call" | custom-call | flops 60397976 | bytes 589824 | tf_op jit(solution)/shard_map/k_time_out/pallas_call | solution.py:612
  133.4 8.2 %collective-permute-done.14.refs_6_.refs_11_.refs_14_.refs_17_ = bf16[96,3072]{1,0:T(8,128)(2,1)S(1)} collective-permute-done((bf16[96,3072]{1,0:T(8,128)(2,1)S(1)}, bf16[96,3072]{1,0:T(8,128)(2,1)S(1)}, u32[]{:S(2)}, u32[]{:S(2)}) %collective-permute-start.14) | collective-permute-done | bytes 589856 | tf_op jit(solution)/shard_map/ppermute | solution.py:790
  146.7 15.6 %k_feed.2 = (bf16[512,768]{1,0:T(8,128)(2,1)}, bf16[512,768]{1,0:T(8,128)(2,1)}, bf16[512,3072]{1,0:T(8,128)(2,1)}, bf16[512,3072]{1,0:T(8,128)(2,1)}, bf16[512,...) custom-call(s32[4,8]{1,0:T(4,128)} %refs_0_.35, s32[3]{0:T(128)} %pad_add_fusion.refs_1_, ...), custom_call_target="tpu_custom_call" | custom-call | flops 271790912 | bytes 1179648 | tf_op jit(solution)/shard_map/k_feed/pallas_call | solution.py:612
  162.4 7.8 %collective-permute-done.20.refs_7_.refs_12_.refs_15_.refs_18_ = bf16[2,96,3072]{2,1,0:T(8,128)(2,1)S(1)} collective-permute-done((bf16[2,96,3072]{2,1,0:T(8,128)(2,1)}, bf16[2,96,3072]{2,1,0:T(8,128)(2,1)S(1)}, u32[]{:S(2)}, u32[]{:S(2)}) %collective-permute-start.20) | collective-permute-done | bytes 1179680 | tf_op jit(solution)/shard_map/ppermute | solution.py:790
  182.1 9.5 %k_time_in.3 = (bf16[512,768]{1,0:T(8,128)(2,1)}, bf16[512,768]{1,0:T(8,128)(2,1)}, bf16[512,768]{1,0:T(8,128)(2,1)}, f32[512,768]{1,0:T(8,128)}, bf16[512,768]{...) custom-call(s32[4,8]{1,0:T(4,128)} %refs_0_.35, ...), custom_call_target="tpu_custom_call" | custom-call | flops 60397976 | bytes 786432 | tf_op jit(solution)/shard_map/k_time_in/pallas_call | solution.py:612
  194.7 14.1 %all-gather.1 = bf16[32,2,768]{2,1,0:T(2,128)(2,1)S(1)} all-gather(bf16[4,2,768]{2,1,0:T(2,128)(2,1)S(1)} %convert_element_type.491), channel_id=3, replica_groups=mesh['dp'=4,'z'=4,'c'=2] {'z','c'}, dimensions={0}, use_global_device_ids=true | all-gather | bytes 110592 | tf_op jit(solution)/shard_map/all_gather | solution.py:920
  209.5 8.5 %k_time_out.3 = (bf16[512,768]{1,0:T(8,128)(2,1)}, f32[512,768]{1,0:T(8,128)}, bf16[512,768]{1,0:T(8,128)(2,1)}) custom-call(s32[4,8]{1,0:T(4,128)} %refs_0_.35, s32[3]{0:T(128)} %pad_add_fusion.refs_1_, f32[512,768]{1,0:T(8,128)} %get-tuple-element.263.refs_2_.refs_0_, f32[512,768]{1,0:T(8,128)} %get-tuple-element.266.refs_3_.refs_7_.refs_5_, ...), custom_call_target="tpu_custom_call" | custom-call | flops 60397976 | bytes 589824 | tf_op jit(solution)/shard_map/k_time_out/pallas_call | solution.py:612
  218.0 5.1 collective-permute-done.26.refs_7_.refs_11_
  232.4 15.3 %k_feed.3 = (bf16[512,768]{1,0:T(8,128)(2,1)}, bf16[512,768]{1,0:T(8,128)(2,1)}, bf16[512,3072]{1,0:T(8,128)(2,1)}, bf16[512,3072]{1,0:T(8,128)(2,1)}, bf16[512,...) custom-call(s32[4,8]{1,0:T(4,128)} %refs_0_.35, s32[3]{0:T(128)} %pad_add_fusion.refs_1_, ...), custom_call_target="tpu_custom_call" | custom-call | flops 271790912 | bytes 1179648 | tf_op jit(solution)/shard_map/k_feed/pallas_call | solution.py:612
  247.7 15.3 %k_feed_back.2 = (bf16[512,768]{1,0:T(8,128)(2,1)}, bf16[512,768]{1,0:T(8,128)(2,1)}, bf16[512,3072]{1,0:T(8,128)(2,1)}, bf16[512,768]{1,0:T(8,128)(2,1)}, f32[4,768]{1,0:T(4,128)}, /*index=5*/f32[8,768]{1,0:T(8,128)}) custom-call(s32[4,8]{1,0:T(4,128)} %refs_0_.35, s32[3]{0:T(128)} %pad_add_fusion.refs_1_, bf16[512,768]{1,0:T(8,128)(2,1)} %bitcast.201, ...), custom_call_target="tpu_custom_call" | custom-call | flops 271790912 | bytes 1179648 | tf_op jit(solution)/shard_map/k_feed_back/pallas_call | solution.py:612
  263.0 12.0 %k_flat.1 = bf16[768,6144]{1,0:T(8,128)(2,1)} custom-call(bf16[512,768]{1,0:T(8,128)(2,1)} %get-tuple-element.288.refs_0_, bf16[512,3072]{1,0:T(8,128)(2,1)} %get-tuple-element.289.refs_1_, bf16[512,3072]{1,0:T(8,128)(2,1)} %get-tuple-element.290.refs_2_, bf16[512,768]{1,0:T(8,128)(2,1)} %get-tuple-element.291.refs_3_), custom_call_target="tpu_custom_call" | custom-call | flops 241591904 | bytes 1101004 | tf_op jit(solution)/shard_map/k_flat/pallas_call | solution.py:612
  279.5 12.8 %k_mid_back.2 = (f32[512,768]{1,0:T(8,128)}, bf16[512,768]{1,0:T(8,128)(2,1)}, bf16[512,768]{1,0:T(8,128)(2,1)}, bf16[512,768]{1,0:T(8,128)(2,1)}, bf16[512,768]...) custom-call(s32[4,8]{1,0:T(4,128)} %refs_0_.35, ...), custom_call_target="tpu_custom_call" | custom-call | flops 30198988 | bytes 983040 | tf_op jit(solution)/shard_map/k_mid_back/pallas_call | solution.py:612
  292.4 6.3 %k_halves_apart.4 = (bf16[4,4,3,24,768]{4,3,2,1,0:T(8,128)(2,1)}, bf16[4,4,3,24,768]{4,3,2,1,0:T(8,128)(2,1)}) custom-call(s32[4,8]{1,0:T(4,128)} %refs_0_.35, s32[3]{0:T(128)} %pad_add_fusion.refs_1_, bf16[512,768]{1,0:T(8,128)(2,1)} %get-tuple-element.299.refs_2_, bf16[512,768]{1,0:T(8,128)(2,1)} %get-tuple-element.300.refs_3_, ...), custom_call_target="tpu_custom_call" | custom-call | flops 90596968 | bytes 412876 | tf_op jit(solution)/shard_map/k_halves_apart/pallas_call | solution.py:612
  301.9 14.1 %all-gather.2 = bf16[32,2,768]{2,1,0:T(2,128)(2,1)S(1)} all-gather(bf16[4,2,768]{2,1,0:T(2,128)(2,1)S(1)} %convert_element_type.498), channel_id=4, replica_groups=mesh['dp'=4,'z'=4,'c'=2] {'z','c'}, dimensions={0}, use_global_device_ids=true | all-gather | bytes 110592 | tf_op jit(solution)/shard_map/all_gather | solution.py:920
  316.7 10.9 %k_time_back.2 = (bf16[512,768]{1,0:T(8,128)(2,1)}, bf16[512,768]{1,0:T(8,128)(2,1)}, bf16[512,768]{1,0:T(8,128)(2,1)}, f32[2,2,768]{2,1,0:T(2,128)}, f32[8,768]{1,0:T(8,128)}) custom-call(s32[4,8]{1,0:T(4,128)} %refs_0_.35, s32[3]{0:T(128)} %pad_add_fusion.refs_1_, f32[512,768]{1,0:T(8,128)} %get-tuple-element.263.refs_2_.refs_0_, ...), custom_call_target="tpu_custom_call" | custom-call | flops 90596968 | bytes 983040 | tf_op jit(solution)/shard_map/k_time_back/pallas_call | solution.py:612
  327.7 5.6 k_halves_apart.5
  347.6 15.7 %k_feed_back.3 = (bf16[512,768]{1,0:T(8,128)(2,1)}, bf16[512,768]{1,0:T(8,128)(2,1)}, bf16[512,3072]{1,0:T(8,128)(2,1)}, bf16[512,768]{1,0:T(8,128)(2,1)}, f32[4,768]{1,0:T(4,128)}, /*index=5*/f32[8,768]{1,0:T(8,128)}) custom-call(s32[4,8]{1,0:T(4,128)} %refs_0_.35, s32[3]{0:T(128)} %pad_add_fusion.refs_1_, f32[512,768]{1,0:T(8,128)} %get-tuple-element.315.refs_2_.refs_5_, ...), custom_call_target="tpu_custom_call" | custom-call | flops 271790912 | bytes 1179648 | tf_op jit(solution)/shard_map/k_feed_back/pallas_call | solution.py:612
  369.8 7.0 %k_halves_blocks.2 = (bf16[4,4,4,24,768]{4,3,2,1,0:T(8,128)(2,1)}, bf16[4,4,4,24,768]{4,3,2,1,0:T(8,128)(2,1)}) custom-call(s32[4,8]{1,0:T(4,128)} %refs_0_.35, s32[3]{0:T(128)} %pad_add_fusion.refs_1_, bf16[512,3072]{1,0:T(8,128)(2,1)} %get-tuple-element.333.refs_2_, bf16[512,768]{1,0:T(8,128)(2,1)} %get-tuple-element.334.refs_3_), custom_call_target="tpu_custom_call" | custom-call | flops 120795952 | bytes 550502 | tf_op jit(solution)/shard_map/k_halves_blocks/pallas_call | solution.py:612
  379.0 7.1 %k_halves_blocks.3 = (bf16[4,4,4,24,768]{4,3,2,1,0:T(8,128)(2,1)}, bf16[4,4,4,24,768]{4,3,2,1,0:T(8,128)(2,1)}) custom-call(s32[4,8]{1,0:T(4,128)} %refs_0_.35, s32[3]{0:T(128)} %pad_add_fusion.refs_1_, bf16[512,768]{1,0:T(8,128)(2,1)} %get-tuple-element.336.refs_2_, bf16[512,3072]{1,0:T(8,128)(2,1)} %get-tuple-element.339.refs_3_), custom_call_target="tpu_custom_call" | custom-call | flops 120795952 | bytes 550502 | tf_op jit(solution)/shard_map/k_halves_blocks/pallas_call | solution.py:612
  397.1 12.9 %k_mid_back.3 = (f32[512,768]{1,0:T(8,128)}, bf16[512,768]{1,0:T(8,128)(2,1)}, bf16[512,768]{1,0:T(8,128)(2,1)}, bf16[512,768]{1,0:T(8,128)(2,1)}, bf16[512,768]...) custom-call(s32[4,8]{1,0:T(4,128)} %refs_0_.35, ...), custom_call_target="tpu_custom_call" | custom-call | flops 30198988 | bytes 983040 | tf_op jit(solution)/shard_map/k_mid_back/pallas_call | solution.py:612
  410.0 6.2 %k_halves_apart.6 = (bf16[4,4,3,24,768]{4,3,2,1,0:T(8,128)(2,1)}, bf16[4,4,3,24,768]{4,3,2,1,0:T(8,128)(2,1)}) custom-call(s32[4,8]{1,0:T(4,128)} %refs_0_.35, s32[3]{0:T(128)} %pad_add_fusion.refs_1_, bf16[512,768]{1,0:T(8,128)(2,1)} %get-tuple-element.356.refs_2_, bf16[512,768]{1,0:T(8,128)(2,1)} %get-tuple-element.357.refs_3_, ...), custom_call_target="tpu_custom_call" | custom-call | flops 90596968 | bytes 412876 | tf_op jit(solution)/shard_map/k_halves_apart/pallas_call | solution.py:612
  435.9 14.3 %all-gather.3 = bf16[32,2,768]{2,1,0:T(2,128)(2,1)S(1)} all-gather(bf16[4,2,768]{2,1,0:T(2,128)(2,1)S(1)} %convert_element_type.520), channel_id=5, replica_groups=mesh['dp'=4,'z'=4,'c'=2] {'z','c'}, dimensions={0}, use_global_device_ids=true | all-gather | bytes 110592 | tf_op jit(solution)/shard_map/all_gather | solution.py:920
  451.0 10.0 %k_time_back.3 = (bf16[512,768]{1,0:T(8,128)(2,1)}, bf16[512,768]{1,0:T(8,128)(2,1)}, bf16[512,768]{1,0:T(8,128)(2,1)}, f32[2,2,768]{2,1,0:T(2,128)}, f32[8,768]{1,0:T(8,128)}) custom-call(s32[4,8]{1,0:T(4,128)} %refs_0_.35, s32[3]{0:T(128)} %pad_add_fusion.refs_1_, bf16[512,768]{1,0:T(8,128)(2,1)} %bitcast.192, f32[2,2,768]{2,1,0:T(2,128)} %reshape.497.refs_3_, ...), custom_call_target="tpu_custom_call" | custom-call | flops 90596968 | bytes 983040 | tf_op jit(solution)/shard_map/k_time_back/pallas_call | solution.py:612
  470.4 5.2 k_halves_apart.7
  481.1 4.4 k_norm_back.3
  491.3 9.7 %collective-permute-done.51 = bf16[1,1,4,3,24,768]{5,4,3,2,1,0:T(8,128)(2,1)} collective-permute-done((bf16[1,1,4,3,24,768]{5,4,3,2,1,0:T(8,128)(2,1)}, bf16[1,1,4,3,24,768]{5,4,3,2,1,0:T(8,128)(2,1)}, u32[]{:S(2)}, u32[]{:S(2)}) %collective-permute-start.51) | collective-permute-done | bytes 442400 | tf_op jit(solution)/shard_map/ppermute | solution.py:790
  505.8 6.2 %collective-permute-done.53 = bf16[1,1,4,2,24,768]{5,4,3,2,1,0:T(8,128)(2,1)S(1)} collective-permute-done((bf16[1,1,4,2,24,768]{5,4,3,2,1,0:T(8,128)(2,1)S(1)}, bf16[1,1,4,2,24,768]{5,4,3,2,1,0:T(8,128)(2,1)S(1)}, u32[]{:S(2)}, u32[]{:S(2)}) %collective-permute-start.53) | collective-permute-done | bytes 294944 | tf_op jit(solution)/shard_map/ppermute | solution.py:790
  536.2 6.1 %reduce-scatter.13.cloned.1.call-done = bf16[144,768]{1,0:T(8,128)(2,1)} async-done(((bf16[576,768]{1,0:T(8,128)(2,1)}), bf16[144,768]{1,0:T(8,128)(2,1)}) %reduce-scatter.13.cloned.1.call-update) | async-done | bytes 221200 | tf_op jit(solution)/shard_map/reduce_scatter | solution.py:902
  (538 shorter events, 211.5 us)
Async XLA Ops:
  7.2 41.9 %all-gather.9.cloned.1.call-start = ((), (), s32[]{:S(2)}) async-start(), calls=%async_computation.4 | async-start | bytes 2322432 | tf_op jit(solution)/shard_map/all_gather | solution.py:798
  13.7 64.5 %all-gather.11.cloned.1.call-start = ((), (), s32[]{:S(2)}) async-start(), calls=%async_computation.5 | async-start | bytes 1327104 | tf_op jit(solution)/shard_map/all_gather | solution.py:798
  14.6 33.9 %collective-permute-start = (bf16[4,768]{1,0:T(4,128)(2,1)S(1)}, bf16[4,768]{1,0:T(4,128)(2,1)S(1)}, u32[]{:S(2)}, u32[]{:S(2)}) collective-permute-start(bf16[4,768]{1,0:T(4,128)(2,1)S(1)} %bitcast.250), channel_id=1, source_target_pairs={{0,1},{1,2},{2,3},{3,4},{4,5},{5,6},{6,7},{8,9},{9,10},{10,11},{11... | collective-permute-start | bytes 18440 | tf_op jit(solution)/shard_map/ppermute | solution.py:915
  39.1 85.8 %all-gather.13.cloned.1.call-start = ((), (), s32[]{:S(2)}) async-start(), calls=%async_computation.6 | async-start | bytes 1327104 | tf_op jit(solution)/shard_map/all_gather | solution.py:798
  47.1 96.3 %all-gather.15.cloned.1.call-start = ((), (), s32[]{:S(2)}) async-start(), calls=%async_computation.7 | async-start | bytes 2985984 | tf_op jit(solution)/shard_map/all_gather | solution.py:798
  54.3 19.0 %collective-permute-start.4 = (bf16[96,3840]{1,0:T(8,128)(2,1)}, bf16[96,3840]{1,0:T(8,128)(2,1)S(1)}, u32[]{:S(2)}, u32[]{:S(2)}) collective-permute-start(bf16[96,3840]{1,0:T(8,128)(2,1)} %constant_dynamic-slice_fusion.10), channel_id=1, source_target_pairs={{0,8},{8,0},{16,24},{24,16},{1,9},{9,1},{17,25},{25,17},{2,10},{10... | collective-permute-start | bytes 2211848 | tf_op jit(solution)/shard_map/ppermute | solution.py:790
  57.6 15.6 %collective-permute-start.2 = (bf16[2,96,1664]{2,1,0:T(8,128)(2,1)}, bf16[2,96,1664]{2,1,0:T(8,128)(2,1)}, u32[]{:S(2)}, u32[]{:S(2)}) collective-permute-start(bf16[2,96,1664]{2,1,0:T(8,128)(2,1)} %pad_maximum_fusion.8), channel_id=1, source_target_pairs={{0,16},{8,24},{16,0},{24,8},{1,17},{9,25},{17,1},{25,9},{2,18},{10... | collective-permute-start | bytes 1916936 | tf_op jit(solution)/shard_map/ppermute | solution.py:790
  59.2 363.9 %reduce-scatter.7.cloned.1.call-start = ((), (), s32[]{:S(2)}) async-start(), calls=%async_computation.8 | async-start | bytes 9732096 | tf_op jit(solution)/shard_map/reduce_scatter | solution.py:1052
  76.8 16.9 %collective-permute-start.7 = (bf16[2,96,1536]{2,1,0:T(8,128)(2,1)}, bf16[2,96,1536]{2,1,0:T(8,128)(2,1)S(1)}, u32[]{:S(2)}, u32[]{:S(2)}) collective-permute-start(bf16[2,96,1536]{2,1,0:T(8,128)(2,1)} %pad_maximum_fusion.9), channel_id=1, source_target_pairs={{0,8},{8,0},{16,24},{24,16},{1,9},{9,1},{17,25},{25,17},{2,10},{10... | collective-permute-start | bytes 1769480 | tf_op jit(solution)/shard_map/ppermute | solution.py:790
  95.6 29.3 %collective-permute-start.11 = (bf16[2,96,3072]{2,1,0:T(8,128)(2,1)S(1)}, bf16[2,96,3072]{2,1,0:T(8,128)(2,1)}, u32[]{:S(2)}, u32[]{:S(2)}) collective-permute-start(bf16[2,96,3072]{2,1,0:T(8,128)(2,1)S(1)} %pad_maximum_fusion.2), channel_id=1, source_target_pairs={{0,8},{8,0},{16,24},{24,16},{1,9},{9,1},{17,25},{25,17},{2,10},{10... | collective-permute-start | bytes 3538952 | tf_op jit(solution)/shard_map/ppermute | solution.py:790
  97.5 33.3 %collective-permute-start.13 = (bf16[2,96,3840]{2,1,0:T(8,128)(2,1)}, bf16[2,96,3840]{2,1,0:T(8,128)(2,1)}, u32[]{:S(2)}, u32[]{:S(2)}) collective-permute-start(bf16[2,96,3840]{2,1,0:T(8,128)(2,1)} %pad_maximum_fusion), channel_id=1, source_target_pairs={{0,16},{8,24},{16,0},{24,8},{1,17},{9,25},{17,1},{25,9},{2,18},{10... | collective-permute-start | bytes 4423688 | tf_op jit(solution)/shard_map/ppermute | solution.py:790
  99.0 16.7 %collective-permute-start.10 = (bf16[2,96,1536]{2,1,0:T(8,128)(2,1)S(1)}, bf16[2,96,1536]{2,1,0:T(8,128)(2,1)S(1)}, u32[]{:S(2)}, u32[]{:S(2)}) collective-permute-start(bf16[2,96,1536]{2,1,0:T(8,128)(2,1)S(1)} %collective-permute-done.7.refs_12_.refs_15_.refs_23_), channel_id=1, source_target_pairs={{0,1},{1,0},{2,3},{3,2},{4,5},{5,4},{6,7},{7,6},{8,9},{9,8},{10,11... | collective-permute-start | bytes 1769480 | tf_op jit(solution)/shard_map/ppermute | solution.py:840
  126.1 15.5 %collective-permute-start.14 = (bf16[96,3072]{1,0:T(8,128)(2,1)S(1)}, bf16[96,3072]{1,0:T(8,128)(2,1)S(1)}, u32[]{:S(2)}, u32[]{:S(2)}) collective-permute-start(bf16[96,3072]{1,0:T(8,128)(2,1)S(1)} %constant_dynamic-slice_fusion.1), channel_id=1, source_target_pairs={{0,8},{8,0},{16,24},{24,16},{1,9},{9,1},{17,25},{25,17},{2,10},{10... | collective-permute-start | bytes 1769480 | tf_op jit(solution)/shard_map/ppermute | solution.py:790
  142.8 27.4 %collective-permute-start.20 = (bf16[2,96,3072]{2,1,0:T(8,128)(2,1)}, bf16[2,96,3072]{2,1,0:T(8,128)(2,1)S(1)}, u32[]{:S(2)}, u32[]{:S(2)}) collective-permute-start(bf16[2,96,3072]{2,1,0:T(8,128)(2,1)} %pad_maximum_fusion.3), channel_id=1, source_target_pairs={{0,16},{8,24},{16,0},{24,8},{1,17},{9,25},{17,1},{25,9},{2,18},{10... | collective-permute-start | bytes 3538952 | tf_op jit(solution)/shard_map/ppermute | solution.py:790
  144.6 17.8 %collective-permute-start.19 = (bf16[96,3840]{1,0:T(8,128)(2,1)S(1)}, bf16[96,3840]{1,0:T(8,128)(2,1)S(1)}, u32[]{:S(2)}, u32[]{:S(2)}) collective-permute-start(bf16[96,3840]{1,0:T(8,128)(2,1)S(1)} %constant_dynamic-slice_fusion), channel_id=1, source_target_pairs={{0,8},{8,0},{16,24},{24,16},{1,9},{9,1},{17,25},{25,17},{2,10},{10... | collective-permute-start | bytes 2211848 | tf_op jit(solution)/shard_map/ppermute | solution.py:790
  175.5 16.4 %collective-permute-start.24 = (bf16[96,3072]{1,0:T(8,128)(2,1)}, bf16[96,3072]{1,0:T(8,128)(2,1)}, u32[]{:S(2)}, u32[]{:S(2)}) collective-permute-start(bf16[96,3072]{1,0:T(8,128)(2,1)} %constant_dynamic-slice_fusion.9), channel_id=1, source_target_pairs={{0,16},{8,24},{16,0},{24,8},{1,17},{9,25},{17,1},{25,9},{2,18},{10... | collective-permute-start | bytes 1769480 | tf_op jit(solution)/shard_map/ppermute | solution.py:790
  177.9 45.2 %collective-permute-start.26 = (bf16[2,96,3840]{2,1,0:T(8,128)(2,1)}, bf16[2,96,3840]{2,1,0:T(8,128)(2,1)}, u32[]{:S(2)}, u32[]{:S(2)}) collective-permute-start(bf16[2,96,3840]{2,1,0:T(8,128)(2,1)} %pad_maximum_fusion.1), channel_id=1, source_target_pairs={{0,16},{8,24},{16,0},{24,8},{1,17},{9,25},{17,1},{25,9},{2,18},{10... | collective-permute-start | bytes 4423688 | tf_op jit(solution)/shard_map/ppermute | solution.py:790
  193.1 30.0 %collective-permute-start.25 = (bf16[2,96,3072]{2,1,0:T(8,128)(2,1)S(1)}, bf16[2,96,3072]{2,1,0:T(8,128)(2,1)S(1)}, u32[]{:S(2)}, u32[]{:S(2)}) collective-permute-start(bf16[2,96,3072]{2,1,0:T(8,128)(2,1)S(1)} %pad_maximum_fusion.4), channel_id=1, source_target_pairs={{0,8},{8,0},{16,24},{24,16},{1,9},{9,1},{17,25},{25,17},{2,10},{10... | collective-permute-start | bytes 3538952 | tf_op jit(solution)/shard_map/ppermute | solution.py:790
  275.1 190.8 %reduce-scatter.9.cloned.1.call-start = ((), (), s32[]{:S(2)}) async-start(), calls=%async_computation.9 | async-start | bytes 921600 | tf_op jit(solution)/shard_map/reduce_scatter | solution.py:902
  298.6 18.1 %collective-permute-start.33 = (bf16[2,2,4,3,24,768]{5,4,3,2,1,0:T(8,128)(2,1)}, bf16[2,2,4,3,24,768]{5,4,3,2,1,0:T(8,128)(2,1)S(1)}, u32[]{:S(2)}, u32[]{:S(2)}) collective-permute-start(bf16[2,2,4,3,24,768]{5,4,3,2,1,0:T(8,128)(2,1)} %bitcast.254), channel_id=1, source_target_pairs={{0,1},{1,0},{2,3},{3,2},{4,5},{5,4},{6,7},{7,6},{8,9},{9,8},{10,11... | collective-permute-start | bytes 5308424 | tf_op jit(solution)/shard_map/ppermute | solution.py:864
  334.8 28.5 %collective-permute-start.36 = (bf16[2,1,4,3,24,768]{5,4,3,2,1,0:T(8,128)(2,1)}, bf16[2,1,4,3,24,768]{5,4,3,2,1,0:T(8,128)(2,1)}, u32[]{:S(2)}, u32[]{:S(2)}) collective-permute-start(bf16[2,1,4,3,24,768]{5,4,3,2,1,0:T(8,128)(2,1)} %add_convert_fusion.3), channel_id=1, source_target_pairs={{0,8},{8,0},{16,24},{24,16},{1,9},{9,1},{17,25},{25,17},{2,10},{10... | collective-permute-start | bytes 2654216 | tf_op jit(solution)/shard_map/ppermute | solution.py:790
  338.7 24.6 %collective-permute-start.37 = (bf16[1,2,4,2,24,768]{5,4,3,2,1,0:T(8,128)(2,1)}, bf16[1,2,4,2,24,768]{5,4,3,2,1,0:T(8,128)(2,1)}, u32[]{:S(2)}, u32[]{:S(2)}) collective-permute-start(bf16[1,2,4,2,24,768]{5,4,3,2,1,0:T(8,128)(2,1)} %add_convert_fusion.9), channel_id=1, source_target_pairs={{0,16},{8,24},{16,0},{24,8},{1,17},{9,25},{17,1},{25,9},{2,18},{10... | collective-permute-start | bytes 1769480 | tf_op jit(solution)/shard_map/ppermute | solution.py:790
  365.2 20.9 %collective-permute-start.40 = (bf16[1,1,4,3,24,768]{5,4,3,2,1,0:T(8,128)(2,1)}, bf16[1,1,4,3,24,768]{5,4,3,2,1,0:T(8,128)(2,1)S(1)}, u32[]{:S(2)}, u32[]{:S(2)}) collective-permute-start(bf16[1,1,4,3,24,768]{5,4,3,2,1,0:T(8,128)(2,1)} %add_convert_fusion.13), channel_id=1, source_target_pairs={{0,16},{8,24},{16,0},{24,8},{1,17},{9,25},{17,1},{25,9},{2,18},{10... | collective-permute-start | bytes 1327112 | tf_op jit(solution)/shard_map/ppermute | solution.py:790
  368.0 18.1 %collective-permute-start.41 = (bf16[1,1,4,2,24,768]{5,4,3,2,1,0:T(8,128)(2,1)S(1)}, bf16[1,1,4,2,24,768]{5,4,3,2,1,0:T(8,128)(2,1)S(1)}, u32[]{:S(2)}, u32[]{:S(2)}) collective-permute-start(bf16[1,1,4,2,24,768]{5,4,3,2,1,0:T(8,128)(2,1)S(1)} %add_convert_fusion.17), channel_id=1, source_target_pairs={{0,8},{8,0},{16,24},{24,16},{1,9},{9,1},{17,25},{25,17},{2,10},{10... | collective-permute-start | bytes 884744 | tf_op jit(solution)/shard_map/ppermute | solution.py:790
  388.8 30.2 %collective-permute-start.43 = (bf16[2,1,4,4,24,768]{5,4,3,2,1,0:T(8,128)(2,1)}, bf16[2,1,4,4,24,768]{5,4,3,2,1,0:T(8,128)(2,1)S(1)}, u32[]{:S(2)}, u32[]{:S(2)}) collective-permute-start(bf16[2,1,4,4,24,768]{5,4,3,2,1,0:T(8,128)(2,1)} %add_convert_fusion.1), channel_id=1, source_target_pairs={{0,8},{8,0},{16,24},{24,16},{1,9},{9,1},{17,25},{25,17},{2,10},{10... | collective-permute-start | bytes 3538952 | tf_op jit(solution)/shard_map/ppermute | solution.py:790
  392.7 30.3 %collective-permute-start.44 = (bf16[1,2,4,4,24,768]{5,4,3,2,1,0:T(8,128)(2,1)}, bf16[1,2,4,4,24,768]{5,4,3,2,1,0:T(8,128)(2,1)S(1)}, u32[]{:S(2)}, u32[]{:S(2)}) collective-permute-start(bf16[1,2,4,4,24,768]{5,4,3,2,1,0:T(8,128)(2,1)} %add_convert_fusion), channel_id=1, source_target_pairs={{0,16},{8,24},{16,0},{24,8},{1,17},{9,25},{17,1},{25,9},{2,18},{10... | collective-permute-start | bytes 3538952 | tf_op jit(solution)/shard_map/ppermute | solution.py:790
  428.3 85.0 %reduce-scatter.11.cloned.1.call-start = ((), (), s32[]{:S(2)}) async-start(), calls=%async_computation.10 | async-start | bytes 1474560 | tf_op jit(solution)/shard_map/reduce_scatter | solution.py:902
  430.0 34.8 %collective-permute-start.46 = (bf16[2,1,4,3,24,768]{5,4,3,2,1,0:T(8,128)(2,1)S(1)}, bf16[2,1,4,3,24,768]{5,4,3,2,1,0:T(8,128)(2,1)S(1)}, u32[]{:S(2)}, u32[]{:S(2)}) collective-permute-start(bf16[2,1,4,3,24,768]{5,4,3,2,1,0:T(8,128)(2,1)S(1)} %add_convert_fusion.2), channel_id=1, source_target_pairs={{0,8},{8,0},{16,24},{24,16},{1,9},{9,1},{17,25},{25,17},{2,10},{10... | collective-permute-start | bytes 2654216 | tf_op jit(solution)/shard_map/ppermute | solution.py:790
  432.1 28.9 %collective-permute-start.47 = (bf16[1,1,4,4,24,768]{5,4,3,2,1,0:T(8,128)(2,1)S(1)}, bf16[1,1,4,4,24,768]{5,4,3,2,1,0:T(8,128)(2,1)S(1)}, u32[]{:S(2)}, u32[]{:S(2)}) collective-permute-start(bf16[1,1,4,4,24,768]{5,4,3,2,1,0:T(8,128)(2,1)S(1)} %add_convert_fusion.8), channel_id=1, source_target_pairs={{0,16},{8,24},{16,0},{24,8},{1,17},{9,25},{17,1},{25,9},{2,18},{10... | collective-permute-start | bytes 1769480 | tf_op jit(solution)/shard_map/ppermute | solution.py:790
  434.0 30.8 %collective-permute-start.48 = (bf16[1,1,4,4,24,768]{5,4,3,2,1,0:T(8,128)(2,1)S(1)}, bf16[1,1,4,4,24,768]{5,4,3,2,1,0:T(8,128)(2,1)S(1)}, u32[]{:S(2)}, u32[]{:S(2)}) collective-permute-start(bf16[1,1,4,4,24,768]{5,4,3,2,1,0:T(8,128)(2,1)S(1)} %add_convert_fusion.7), channel_id=1, source_target_pairs={{0,8},{8,0},{16,24},{24,16},{1,9},{9,1},{17,25},{25,17},{2,10},{10... | collective-permute-start | bytes 1769480 | tf_op jit(solution)/shard_map/ppermute | solution.py:790
  478.2 64.1 %reduce-scatter.13.cloned.1.call-start = ((), (), s32[]{:S(2)}) async-start(), calls=%async_computation.11 | async-start | bytes 1105920 | tf_op jit(solution)/shard_map/reduce_scatter | solution.py:902
  480.0 21.0 %collective-permute-start.52 = (bf16[2,1,4,2,24,768]{5,4,3,2,1,0:T(8,128)(2,1)}, bf16[2,1,4,2,24,768]{5,4,3,2,1,0:T(8,128)(2,1)}, u32[]{:S(2)}, u32[]{:S(2)}) collective-permute-start(bf16[2,1,4,2,24,768]{5,4,3,2,1,0:T(8,128)(2,1)} %add_convert_fusion.4), channel_id=1, source_target_pairs={{0,8},{8,0},{16,24},{24,16},{1,9},{9,1},{17,25},{25,17},{2,10},{10... | collective-permute-start | bytes 1769480 | tf_op jit(solution)/shard_map/ppermute | solution.py:790
  (141 other events, 1070.8 us)
Sparse Core Ops, SparseCore 0:
  13.8 34.1 all-gather.8
  50.3 22.4 all-gather.10
  75.0 22.2 all-gather.12
  99.4 34.0 all-gather.14
  275.2 144.0 reduce-scatter.6
  428.4 20.7 reduce-scatter.8
  478.3 27.8 reduce-scatter.10
  519.9 22.3 reduce-scatter.12
